TPU v7x, 32 devices: a whole 2x2x4 slice. The times are simulated.
32 devices in a mesh: gx: 4 (over y, core), gy: 2 (over x), gz: 4 (over z).
Axes of the slice: x: 2, y: 2, z: 4, core: 2. Of those that a mesh axis runs over, the one named last changes fastest.
Arguments:
- displacement: float32 [3, 8, 16, 512], P(None, 'gx', 'gy', 'gz'), may hold values from -6 to 6
- displacement_old: float32 [3, 8, 16, 512], P(None, 'gx', 'gy', 'gz'), may hold values from -6 to 6
- visco_state: float32 [6, 6, 8, 16, 512], P(None, None, 'gx', 'gy', 'gz'), may hold values from -3 to 3
- energy_max: float32 [8, 16, 512], P('gx', 'gy', 'gz'), may hold values from 0.1 to 4
- region: int32 [8, 16, 512], P('gx', 'gy', 'gz'), may hold values from 0 to 3
- dirichlet: int32 [8, 16, 512], P('gx', 'gy', 'gz'), may hold values 0 or 1
- prony_moduli: float32 [4, 6], replicated, may hold values from 0.02 to 0.12
- prony_times: float32 [4, 6], replicated, may hold values from 0.05 to 50
- shear_modulus: float32 [4], replicated, may hold values from 0.5 to 2
- mullins_ratio: float32 [4], replicated, may hold values from 1.5 to 4
- mullins_scale: float32 [4], replicated, may hold values from 0.3 to 3
Outputs:
- stress: float32 [6, 8, 16, 512], P(None, 'gx', 'gy', 'gz')
- visco_next: float32 [6, 6, 8, 16, 512], P(None, None, 'gx', 'gy', 'gz')
- energy_next: float32 [8, 16, 512], P('gx', 'gy', 'gz')
- damage_field: float32 [8, 16, 512], P('gx', 'gy', 'gz')
- residual: float32 [8, 16, 512], P('gx', 'gy', 'gz')
All inputs are finite; a program needn't handle non-finite values. No bound on the sum of `dirichlet` on one device may be relied on, other than what follows from the above.
Results may differ from a plain program's by a relative error of at most 0.0003.
Values sent between devices are 32-bit elements; how exact they have to be, the bound alone decides.
No kernel may reach another device: no remote copies, remote signals or barrier semaphores. Data moves between devices by JAX's collectives and lax.ppermute only.
A program may use at most 64 MiB of HBM per device.

v0:
```python
import jax
import jax.numpy as jnp
from jax import lax
from jax.sharding import PartitionSpec as P

ITERS = 4


LENGTH_SQUARED = 4.0


def extended_2(shard, sides, width):
    for axis, dim in sides:
        count, length = (lax.axis_size(axis), shard.shape[dim])
        up = [(i, (i + 1) % count) for i in range(count)]
        down = [(j, i) for i, j in up]
        last = lax.slice_in_dim(shard, length - width, length, axis=dim)
        leading = lax.slice_in_dim(shard, 0, width, axis=dim)
        before = lax.ppermute(last, axis, up)
        after = lax.ppermute(leading, axis, down)
        shard = jnp.concatenate([before, shard, after], axis=dim)
    return shard


def neighbours(field):
    extended = extended_2(field, (("gx", 1), ("gy", 2), ("gz", 3)), 1)
    index_y = lax.axis_index("gy")
    index_z = lax.axis_index("gz")
    rows_y = lax.broadcasted_iota(jnp.int32, (1, 1, extended.shape[2], 1), 2)
    rows_z = lax.broadcasted_iota(jnp.int32, (1, 1, 1, extended.shape[3]), 3)
    cut_y = (rows_y == 0) & (index_y == 0) | (rows_y == extended.shape[2] - 1) & (
        index_y == lax.axis_size("gy") - 1
    )
    cut_z = (rows_z == 0) & (index_z == 0) | (rows_z == extended.shape[3] - 1) & (
        index_z == lax.axis_size("gz") - 1
    )
    extended = jnp.where(cut_y | cut_z, 0.0, extended)
    next_x = extended[:, 2:, 1:-1, 1:-1]
    prev_x = extended[:, :-2, 1:-1, 1:-1]
    next_y = extended[:, 1:-1, 2:, 1:-1]
    prev_y = extended[:, 1:-1, :-2, 1:-1]
    next_z = extended[:, 1:-1, 1:-1, 2:]
    prev_z = extended[:, 1:-1, 1:-1, :-2]
    return (next_x, prev_x, next_y, prev_y, next_z, prev_z)


def deviator(grad_x, grad_y, grad_z):
    strain_xx = grad_x[0]
    strain_yy = grad_y[1]
    strain_zz = grad_z[2]
    strain_yz = 0.5 * (grad_z[1] + grad_y[2])
    strain_xz = 0.5 * (grad_z[0] + grad_x[2])
    strain_xy = 0.5 * (grad_y[0] + grad_x[1])
    trace_third = (strain_xx + strain_yy + strain_zz) / 3.0
    return jnp.stack(
        [
            strain_xx - trace_third,
            strain_yy - trace_third,
            strain_zz - trace_third,
            strain_yz,
            strain_xz,
            strain_xy,
        ]
    )


def contract(dev):
    return (
        dev[0] * dev[0]
        + dev[1] * dev[1]
        + dev[2] * dev[2]
        + 2.0 * (dev[3] * dev[3] + dev[4] * dev[4] + dev[5] * dev[5])
    )


def operate(field):
    next_x, prev_x, next_y, prev_y, next_z, prev_z = neighbours(field)
    beside_all = next_x + prev_x + next_y + prev_y + next_z + prev_z
    return (1.0 + 6.0 * LENGTH_SQUARED) * field - LENGTH_SQUARED * beside_all


def lookup_one(table_rows, onehot):
    return jnp.sum(table_rows[:, None, None, None] * onehot, axis=0)


def lookup_many(table_rows, onehot):
    return jnp.einsum("rk,rxyz->kxyz", table_rows, onehot, precision=lax.Precision.HIGHEST)


def merged_products(residual, image_res):
    return lax.psum(
        (jnp.sum(residual * residual), jnp.sum(residual * image_res)), ("gx", "gy", "gz")
    )


def on_device(
    displacement,
    displacement_old,
    visco_state,
    energy_max,
    region,
    dirichlet,
    prony_moduli,
    prony_times,
    shear_modulus,
    mullins_ratio,
    mullins_scale,
):
    free_share = (1 - dirichlet).astype(jnp.float32)
    stacked = jnp.concatenate([displacement, displacement_old], axis=0) * free_share[None]
    next_x, prev_x, next_y, prev_y, next_z, prev_z = neighbours(stacked)
    grad_x = 0.5 * (next_x - prev_x)
    grad_y = 0.5 * (next_y - prev_y)
    grad_z = 0.5 * (next_z - prev_z)
    dev_new = deviator(grad_x[0:3], grad_y[0:3], grad_z[0:3])
    dev_old = deviator(grad_x[3:6], grad_y[3:6], grad_z[3:6])
    region_count = prony_moduli.shape[0]
    labels = lax.broadcasted_iota(jnp.int32, (region_count, 1, 1, 1), 0)
    onehot = (region[None] == labels).astype(jnp.float32)
    shear_cells = lookup_one(shear_modulus, onehot)
    ratio_cells = lookup_one(mullins_ratio, onehot)
    scale_cells = lookup_one(mullins_scale, onehot)
    moduli_cells = lookup_many(prony_moduli, onehot)
    times_cells = lookup_many(prony_times, onehot)
    energy = shear_cells * contract(dev_new)
    energy_next = jnp.maximum(energy_max, energy)
    softening = 1.0 - jax.scipy.special.erf((energy_next - energy) / scale_cells) / ratio_cells
    stress_jump = 2.0 * shear_cells * (dev_new - dev_old)
    decays = jnp.exp(-1.0 / times_cells)
    weight = moduli_cells * (1.0 - decays) * times_cells
    visco_next = decays[:, None] * visco_state + weight[:, None] * stress_jump[None]
    long_term = 1.0 - lookup_one(jnp.sum(prony_moduli, axis=1), onehot)
    stress = softening * (long_term * 2.0 * shear_cells * dev_new + jnp.sum(visco_next, axis=0))
    local_drive = (softening * energy)[None]
    damage_field = jnp.zeros_like(local_drive)
    residual = local_drive
    image_res = operate(residual)
    norm_now, product = merged_products(residual, image_res)
    alpha_now = norm_now / product
    direction = residual
    image_dir = image_res
    for iteration in range(ITERS):
        damage_field = damage_field + alpha_now * direction
        residual = residual - alpha_now * image_dir
        if iteration + 1 < ITERS:
            image_res = operate(residual)
            norm_next, product = merged_products(residual, image_res)
            beta_now = norm_next / norm_now
            alpha_now = norm_next / (product - beta_now * norm_next / alpha_now)
            direction = residual + beta_now * direction
            image_dir = image_res + beta_now * image_dir
            norm_now = norm_next
    return (stress, visco_next, energy_next, damage_field[0], residual[0])


def solution(mesh):
    in_specs = (
        P(None, "gx", "gy", "gz"),
        P(None, "gx", "gy", "gz"),
        P(None, None, "gx", "gy", "gz"),
        P("gx", "gy", "gz"),
        P("gx", "gy", "gz"),
        P("gx", "gy", "gz"),
        P(),
        P(),
        P(),
        P(),
        P(),
    )
    out_specs = (
        P(None, "gx", "gy", "gz"),
        P(None, None, "gx", "gy", "gz"),
        P("gx", "gy", "gz"),
        P("gx", "gy", "gz"),
        P("gx", "gy", "gz"),
    )
    return jax.shard_map(
        on_device, mesh=mesh, in_specs=in_specs, out_specs=out_specs, check_vma=False
    )
```

profile of v0, /device:TPU:0, one launch (start us, length us, event | category | flops | bytes accessed | tf_op | source)
XLA Modules:
  0.0 261.4 jit_solution(4169171032535812650)
XLA Ops:
  2.6 2.0 collective-permute-start.1
  6.2 2.3 collective-permute-start.2
  10.1 2.0 collective-permute-done.3
  14.0 2.2 collective-permute-start.5
  16.4 5.6 %collective-permute-done.4 = f32[6,4,10,1]{3,2,1,0:T(8,128)S(1)} collective-permute-done((f32[6,4,10,1]{3,2,1,0:T(8,128)S(1)}, f32[6,4,10,1]{3,2,1,0:T(8,128)S(1)}, u32[]{:S(2)}, u32[]{:S(2)}) %collective-permute-start.4) | collective-permute-done | bytes 992 | tf_op jit(solution)/shard_map/ppermute | solution.py:19
  22.0 2.9 %collective-permute-done.5 = f32[6,4,10,1]{3,2,1,0:T(8,128)S(1)} collective-permute-done((f32[6,4,10,1]{3,2,1,0:T(8,128)S(1)}, f32[6,4,10,1]{3,2,1,0:T(8,128)S(1)}, u32[]{:S(2)}, u32[]{:S(2)}) %collective-permute-start.5) | collective-permute-done | bytes 992 | tf_op jit(solution)/shard_map/ppermute | solution.py:20
  35.8 2.7 %collective-permute-start.11 = (f32[1,4,10,1]{3,2,1,0:T(8,128)S(1)}, f32[1,4,10,1]{3,2,1,0:T(8,128)S(1)}, u32[]{:S(2)}, u32[]{:S(2)}) collective-permute-start(f32[1,4,10,1]{3,2,1,0:T(8,128)S(1)} %get-tuple-element.70), channel_id=1, source_target_pairs={{1,0},{2,1},{3,2},{0,3},{5,4},{6,5},{7,6},{4,7},{9,8},{10,9},{11,1... | collective-permute-start | bytes 488 | tf_op jit(solution)/shard_map/ppermute | solution.py:20
  38.5 1.9 collective-permute-done.10
  41.1 39.4 %all-reduce.3 = (f32[]{:T(128)}, f32[]{:T(128)}) all-reduce(f32[]{:T(128)} %get-tuple-element.30, f32[]{:T(128)} %get-tuple-element.28), channel_id=1, replica_groups=mesh['gx'=4,'gy'=2,'gz'=4] {'gx','gy','gz'}, use_global_device_ids=true, to_apply=%region_7.8 | all-reduce | flops 2 | bytes 16 | tf_op jit(solution)/shard_map/psum | solution.py:91
  85.2 2.1 collective-permute-start.14
  88.9 2.0 collective-permute-done.15
  91.0 2.1 collective-permute-start.16
  94.9 2.3 collective-permute-done.16
  98.1 39.3 %all-reduce.2 = (f32[]{:T(128)}, f32[]{:T(128)}) all-reduce(f32[]{:T(128)} %get-tuple-element.10, f32[]{:T(128)} %get-tuple-element.9), channel_id=1, replica_groups=mesh['gx'=4,'gy'=2,'gz'=4] {'gx','gy','gz'}, use_global_device_ids=true, to_apply=%region_11.12 | all-reduce | flops 2 | bytes 16 | tf_op jit(solution)/shard_map/psum | solution.py:91
  145.3 2.1 collective-permute-start.20
  149.1 2.0 collective-permute-done.21
  151.2 1.9 collective-permute-start.22
  153.0 2.0 collective-permute-start.23
  155.0 2.1 collective-permute-done.22
  158.1 39.2 %all-reduce.1 = (f32[]{:T(128)}, f32[]{:T(128)}) all-reduce(f32[]{:T(128)} %get-tuple-element.8, f32[]{:T(128)} %get-tuple-element.7), channel_id=1, replica_groups=mesh['gx'=4,'gy'=2,'gz'=4] {'gx','gy','gz'}, use_global_device_ids=true, to_apply=%region_15.16 | all-reduce | flops 2 | bytes 16 | tf_op jit(solution)/shard_map/psum | solution.py:91
  204.6 2.1 collective-permute-start.26
  208.3 2.0 collective-permute-done.27
  210.4 2.1 collective-permute-start.28
  217.4 39.4 %all-reduce = (f32[]{:T(128)}, f32[]{:T(128)}) all-reduce(f32[]{:T(128)} %get-tuple-element.6, f32[]{:T(128)} %get-tuple-element.5), channel_id=1, replica_groups=mesh['gx'=4,'gy'=2,'gz'=4] {'gx','gy','gz'}, use_global_device_ids=true, to_apply=%region_19.20 | all-reduce | flops 2 | bytes 16 | tf_op jit(solution)/shard_map/psum | solution.py:91
  (111 shorter events, 42.6 us)
Async XLA Ops:
  2.1 4.0 %collective-permute-start = (f32[6,1,8,128]{3,2,1,0:T(8,128)S(1)}, f32[6,1,8,128]{3,2,1,0:T(8,128)S(1)}, u32[]{:S(2)}, u32[]{:S(2)}) collective-permute-start(f32[6,1,8,128]{3,2,1,0:T(8,128)S(1)} %get-tuple-element.61), channel_id=1, source_target_pairs={{0,8},{8,16},{16,24},{24,0},{1,9},{9,17},{17,25},{25,1},{2,10},{10... | collective-permute-start | bytes 73736 | tf_op jit(solution)/shard_map/ppermute | solution.py:19
  2.6 3.5 %collective-permute-start.1 = (f32[6,1,8,128]{3,2,1,0:T(8,128)S(1)}, f32[6,1,8,128]{3,2,1,0:T(8,128)S(1)}, u32[]{:S(2)}, u32[]{:S(2)}) collective-permute-start(f32[6,1,8,128]{3,2,1,0:T(8,128)S(1)} %get-tuple-element.62), channel_id=1, source_target_pairs={{8,0},{16,8},{24,16},{0,24},{9,1},{17,9},{25,17},{1,25},{10,2},{18... | collective-permute-start | bytes 73736 | tf_op jit(solution)/shard_map/ppermute | solution.py:20
  6.2 3.9 %collective-permute-start.2 = (f32[6,4,1,128]{3,2,1,0:T(1,128)S(1)}, f32[6,4,1,128]{3,2,1,0:T(1,128)S(1)}, u32[]{:S(2)}, u32[]{:S(2)}) collective-permute-start(f32[6,4,1,128]{3,2,1,0:T(1,128)S(1)} %get-tuple-element.53), channel_id=1, source_target_pairs={{0,4},{4,0},{1,5},{5,1},{2,6},{6,2},{3,7},{7,3},{8,12},{12,8},{9,1... | collective-permute-start | bytes 36872 | tf_op jit(solution)/shard_map/ppermute | solution.py:19
  8.5 3.7 %collective-permute-start.3 = (f32[6,4,1,128]{3,2,1,0:T(1,128)S(1)}, f32[6,4,1,128]{3,2,1,0:T(1,128)S(1)}, u32[]{:S(2)}, u32[]{:S(2)}) collective-permute-start(f32[6,4,1,128]{3,2,1,0:T(1,128)S(1)} %get-tuple-element.54), channel_id=1, source_target_pairs={{4,0},{0,4},{5,1},{1,5},{6,2},{2,6},{7,3},{3,7},{12,8},{8,12},{13,... | collective-permute-start | bytes 36872 | tf_op jit(solution)/shard_map/ppermute | solution.py:20
  12.4 9.6 %collective-permute-start.4 = (f32[6,4,10,1]{3,2,1,0:T(8,128)S(1)}, f32[6,4,10,1]{3,2,1,0:T(8,128)S(1)}, u32[]{:S(2)}, u32[]{:S(2)}) collective-permute-start(f32[6,4,10,1]{3,2,1,0:T(8,128)S(1)} %get-tuple-element.43), channel_id=1, source_target_pairs={{0,1},{1,2},{2,3},{3,0},{4,5},{5,6},{6,7},{7,4},{8,9},{9,10},{10,1... | collective-permute-start | bytes 2888 | tf_op jit(solution)/shard_map/ppermute | solution.py:19
  14.0 10.9 %collective-permute-start.5 = (f32[6,4,10,1]{3,2,1,0:T(8,128)S(1)}, f32[6,4,10,1]{3,2,1,0:T(8,128)S(1)}, u32[]{:S(2)}, u32[]{:S(2)}) collective-permute-start(f32[6,4,10,1]{3,2,1,0:T(8,128)S(1)} %get-tuple-element.44), channel_id=1, source_target_pairs={{1,0},{2,1},{3,2},{0,3},{5,4},{6,5},{7,6},{4,7},{9,8},{10,9},{11,1... | collective-permute-start | bytes 2888 | tf_op jit(solution)/shard_map/ppermute | solution.py:20
  30.4 3.6 %collective-permute-start.8 = (f32[1,4,1,128]{3,2,1,0:T(1,128)S(1)}, f32[1,4,1,128]{3,2,1,0:T(1,128)S(1)}, u32[]{:S(2)}, u32[]{:S(2)}) collective-permute-start(f32[1,4,1,128]{3,2,1,0:T(1,128)S(1)} %get-tuple-element.77), channel_id=1, source_target_pairs={{0,4},{4,0},{1,5},{5,1},{2,6},{6,2},{3,7},{7,3},{8,12},{12,8},{9,1... | collective-permute-start | bytes 6152 | tf_op jit(solution)/shard_map/ppermute | solution.py:19
  31.0 3.6 %collective-permute-start.9 = (f32[1,4,1,128]{3,2,1,0:T(1,128)S(1)}, f32[1,4,1,128]{3,2,1,0:T(1,128)S(1)}, u32[]{:S(2)}, u32[]{:S(2)}) collective-permute-start(f32[1,4,1,128]{3,2,1,0:T(1,128)S(1)} %get-tuple-element.78), channel_id=1, source_target_pairs={{4,0},{0,4},{5,1},{1,5},{6,2},{2,6},{7,3},{3,7},{12,8},{8,12},{13,... | collective-permute-start | bytes 6152 | tf_op jit(solution)/shard_map/ppermute | solution.py:20
  34.6 5.7 %collective-permute-start.10 = (f32[1,4,10,1]{3,2,1,0:T(8,128)S(1)}, f32[1,4,10,1]{3,2,1,0:T(8,128)S(1)}, u32[]{:S(2)}, u32[]{:S(2)}) collective-permute-start(f32[1,4,10,1]{3,2,1,0:T(8,128)S(1)} %get-tuple-element.69), channel_id=1, source_target_pairs={{0,1},{1,2},{2,3},{3,0},{4,5},{5,6},{6,7},{7,4},{8,9},{9,10},{10,1... | collective-permute-start | bytes 488 | tf_op jit(solution)/shard_map/ppermute | solution.py:19
  35.8 4.6 %collective-permute-start.11 = (f32[1,4,10,1]{3,2,1,0:T(8,128)S(1)}, f32[1,4,10,1]{3,2,1,0:T(8,128)S(1)}, u32[]{:S(2)}, u32[]{:S(2)}) collective-permute-start(f32[1,4,10,1]{3,2,1,0:T(8,128)S(1)} %get-tuple-element.70), channel_id=1, source_target_pairs={{1,0},{2,1},{3,2},{0,3},{5,4},{6,5},{7,6},{4,7},{9,8},{10,9},{11,1... | collective-permute-start | bytes 488 | tf_op jit(solution)/shard_map/ppermute | solution.py:20
  82.0 3.2 %collective-permute-start.13 = (f32[1,1,8,128]{3,2,1,0:T(8,128)S(1)}, f32[1,1,8,128]{3,2,1,0:T(8,128)S(1)}, u32[]{:S(2)}, u32[]{:S(2)}) collective-permute-start(f32[1,1,8,128]{3,2,1,0:T(8,128)S(1)} %get-tuple-element.86), channel_id=1, source_target_pairs={{8,0},{16,8},{24,16},{0,24},{9,1},{17,9},{25,17},{1,25},{10,2},{18... | collective-permute-start | bytes 12296 | tf_op jit(solution)/shard_map/ppermute | solution.py:20
  85.2 3.7 %collective-permute-start.14 = (f32[1,4,1,128]{3,2,1,0:T(1,128)S(1)}, f32[1,4,1,128]{3,2,1,0:T(1,128)S(1)}, u32[]{:S(2)}, u32[]{:S(2)}) collective-permute-start(f32[1,4,1,128]{3,2,1,0:T(1,128)S(1)} %get-tuple-element.75), channel_id=1, source_target_pairs={{0,4},{4,0},{1,5},{5,1},{2,6},{6,2},{3,7},{7,3},{8,12},{12,8},{9,1... | collective-permute-start | bytes 6152 | tf_op jit(solution)/shard_map/ppermute | solution.py:19
  87.3 3.6 %collective-permute-start.15 = (f32[1,4,1,128]{3,2,1,0:T(1,128)S(1)}, f32[1,4,1,128]{3,2,1,0:T(1,128)S(1)}, u32[]{:S(2)}, u32[]{:S(2)}) collective-permute-start(f32[1,4,1,128]{3,2,1,0:T(1,128)S(1)} %get-tuple-element.76), channel_id=1, source_target_pairs={{4,0},{0,4},{5,1},{1,5},{6,2},{2,6},{7,3},{3,7},{12,8},{8,12},{13,... | collective-permute-start | bytes 6152 | tf_op jit(solution)/shard_map/ppermute | solution.py:20
  91.0 6.2 %collective-permute-start.16 = (f32[1,4,10,1]{3,2,1,0:T(8,128)S(1)}, f32[1,4,10,1]{3,2,1,0:T(8,128)S(1)}, u32[]{:S(2)}, u32[]{:S(2)}) collective-permute-start(f32[1,4,10,1]{3,2,1,0:T(8,128)S(1)} %get-tuple-element.67), channel_id=1, source_target_pairs={{0,1},{1,2},{2,3},{3,0},{4,5},{5,6},{6,7},{7,4},{8,9},{9,10},{10,1... | collective-permute-start | bytes 488 | tf_op jit(solution)/shard_map/ppermute | solution.py:19
  93.2 4.1 %collective-permute-start.17 = (f32[1,4,10,1]{3,2,1,0:T(8,128)S(1)}, f32[1,4,10,1]{3,2,1,0:T(8,128)S(1)}, u32[]{:S(2)}, u32[]{:S(2)}) collective-permute-start(f32[1,4,10,1]{3,2,1,0:T(8,128)S(1)} %get-tuple-element.68), channel_id=1, source_target_pairs={{1,0},{2,1},{3,2},{0,3},{5,4},{6,5},{7,6},{4,7},{9,8},{10,9},{11,1... | collective-permute-start | bytes 488 | tf_op jit(solution)/shard_map/ppermute | solution.py:20
  145.3 3.7 %collective-permute-start.20 = (f32[1,4,1,128]{3,2,1,0:T(1,128)S(1)}, f32[1,4,1,128]{3,2,1,0:T(1,128)S(1)}, u32[]{:S(2)}, u32[]{:S(2)}) collective-permute-start(f32[1,4,1,128]{3,2,1,0:T(1,128)S(1)} %get-tuple-element.73), channel_id=1, source_target_pairs={{0,4},{4,0},{1,5},{5,1},{2,6},{6,2},{3,7},{7,3},{8,12},{12,8},{9,1... | collective-permute-start | bytes 6152 | tf_op jit(solution)/shard_map/ppermute | solution.py:19
  147.5 3.6 %collective-permute-start.21 = (f32[1,4,1,128]{3,2,1,0:T(1,128)S(1)}, f32[1,4,1,128]{3,2,1,0:T(1,128)S(1)}, u32[]{:S(2)}, u32[]{:S(2)}) collective-permute-start(f32[1,4,1,128]{3,2,1,0:T(1,128)S(1)} %get-tuple-element.74), channel_id=1, source_target_pairs={{4,0},{0,4},{5,1},{1,5},{6,2},{2,6},{7,3},{3,7},{12,8},{8,12},{13,... | collective-permute-start | bytes 6152 | tf_op jit(solution)/shard_map/ppermute | solution.py:20
  151.2 5.9 %collective-permute-start.22 = (f32[1,4,10,1]{3,2,1,0:T(8,128)S(1)}, f32[1,4,10,1]{3,2,1,0:T(8,128)S(1)}, u32[]{:S(2)}, u32[]{:S(2)}) collective-permute-start(f32[1,4,10,1]{3,2,1,0:T(8,128)S(1)} %get-tuple-element.65), channel_id=1, source_target_pairs={{0,1},{1,2},{2,3},{3,0},{4,5},{5,6},{6,7},{7,4},{8,9},{9,10},{10,1... | collective-permute-start | bytes 488 | tf_op jit(solution)/shard_map/ppermute | solution.py:19
  153.0 4.2 %collective-permute-start.23 = (f32[1,4,10,1]{3,2,1,0:T(8,128)S(1)}, f32[1,4,10,1]{3,2,1,0:T(8,128)S(1)}, u32[]{:S(2)}, u32[]{:S(2)}) collective-permute-start(f32[1,4,10,1]{3,2,1,0:T(8,128)S(1)} %get-tuple-element.66), channel_id=1, source_target_pairs={{1,0},{2,1},{3,2},{0,3},{5,4},{6,5},{7,6},{4,7},{9,8},{10,9},{11,1... | collective-permute-start | bytes 488 | tf_op jit(solution)/shard_map/ppermute | solution.py:20
  201.4 3.2 %collective-permute-start.25 = (f32[1,1,8,128]{3,2,1,0:T(8,128)S(1)}, f32[1,1,8,128]{3,2,1,0:T(8,128)S(1)}, u32[]{:S(2)}, u32[]{:S(2)}) collective-permute-start(f32[1,1,8,128]{3,2,1,0:T(8,128)S(1)} %get-tuple-element.82), channel_id=1, source_target_pairs={{8,0},{16,8},{24,16},{0,24},{9,1},{17,9},{25,17},{1,25},{10,2},{18... | collective-permute-start | bytes 12296 | tf_op jit(solution)/shard_map/ppermute | solution.py:20
  204.6 3.7 %collective-permute-start.26 = (f32[1,4,1,128]{3,2,1,0:T(1,128)S(1)}, f32[1,4,1,128]{3,2,1,0:T(1,128)S(1)}, u32[]{:S(2)}, u32[]{:S(2)}) collective-permute-start(f32[1,4,1,128]{3,2,1,0:T(1,128)S(1)} %get-tuple-element.71), channel_id=1, source_target_pairs={{0,4},{4,0},{1,5},{5,1},{2,6},{6,2},{3,7},{7,3},{8,12},{12,8},{9,1... | collective-permute-start | bytes 6152 | tf_op jit(solution)/shard_map/ppermute | solution.py:19
  206.8 3.6 %collective-permute-start.27 = (f32[1,4,1,128]{3,2,1,0:T(1,128)S(1)}, f32[1,4,1,128]{3,2,1,0:T(1,128)S(1)}, u32[]{:S(2)}, u32[]{:S(2)}) collective-permute-start(f32[1,4,1,128]{3,2,1,0:T(1,128)S(1)} %get-tuple-element.72), channel_id=1, source_target_pairs={{4,0},{0,4},{5,1},{1,5},{6,2},{2,6},{7,3},{3,7},{12,8},{8,12},{13,... | collective-permute-start | bytes 6152 | tf_op jit(solution)/shard_map/ppermute | solution.py:20
  210.4 6.0 %collective-permute-start.28 = (f32[1,4,10,1]{3,2,1,0:T(8,128)S(1)}, f32[1,4,10,1]{3,2,1,0:T(8,128)S(1)}, u32[]{:S(2)}, u32[]{:S(2)}) collective-permute-start(f32[1,4,10,1]{3,2,1,0:T(8,128)S(1)} %get-tuple-element.63), channel_id=1, source_target_pairs={{0,1},{1,2},{2,3},{3,0},{4,5},{5,6},{6,7},{7,4},{8,9},{9,10},{10,1... | collective-permute-start | bytes 488 | tf_op jit(solution)/shard_map/ppermute | solution.py:19
  212.5 4.1 %collective-permute-start.29 = (f32[1,4,10,1]{3,2,1,0:T(8,128)S(1)}, f32[1,4,10,1]{3,2,1,0:T(8,128)S(1)}, u32[]{:S(2)}, u32[]{:S(2)}) collective-permute-start(f32[1,4,10,1]{3,2,1,0:T(8,128)S(1)} %get-tuple-element.64), channel_id=1, source_target_pairs={{1,0},{2,1},{3,2},{0,3},{5,4},{6,5},{7,6},{4,7},{9,8},{10,9},{11,1... | collective-permute-start | bytes 488 | tf_op jit(solution)/shard_map/ppermute | solution.py:20
  (14 other events, 123.2 us)
where the time goes:
time: 263 us; the launch traced here: 261 us
  blocking collectives  157 us (60%)
  starting transfers between devices  39.9 us (15%)
  waiting for transfers between devices  38.3 us (15%)
  between operations  14.8 us (6%)
  other arithmetic  8.93 us (3%)
    psum x4, blocking collectives, merged_products(): lax.psum((jnp.sum(residual * residual), jnp.sum(residual * image_res)), (...  157 us
    ppermute x15, waiting for transfers between devices, extended_2(): before = lax.ppermute(last, axis, up)  25.6 us
    ppermute x15, starting transfers between devices, extended_2(): after = lax.ppermute(leading, axis, down)  21.1 us
    ppermute x15, starting transfers between devices, extended_2(): before = lax.ppermute(last, axis, up)  18.8 us
    ppermute x15, waiting for transfers between devices, extended_2(): after = lax.ppermute(leading, axis, down)  12.7 us
  transfers between devices with their start and end apart: 30, of which 28 were waited for; matrix products, arithmetic and copies ran while one was open for 1% of the time, Pallas kernels for 0%

commit v1 on v0

v1 whole, which is shorter than its diff:
```python
import functools
import typing

import jax
import jax.numpy as jnp
import numpy as np
from jax import lax
from jax.experimental import pallas as pl
from jax.experimental.pallas import tpu as pltpu
from jax.sharding import PartitionSpec as P

ITERS = 4
LENGTH_SQUARED = 4.0

SHIFTS = (0.0, 6.0, 1.5, 9.0)
PAIRS = [(i, j) for i in range(ITERS + 1) for j in range(i, ITERS + 1) if i < ITERS]

WIDE, NARROW = 5, 3
REACHES = (ITERS + 1,) * WIDE + (1,) * NARROW
FIELDS = WIDE + NARROW
MB = 1 << 20


class Geometry(typing.NamedTuple):
    lx: int
    ly: int
    lz: int
    gx: int
    gy: int
    gz: int
    hops_x: int
    hops_y: int
    full: bool

    @property
    def bx(self):
        return self.gx if self.full else 2 * self.hops_x + 1

    @property
    def by(self):
        return self.gy if self.full else 2 * self.hops_y + 1


def geometry(block):
    lx, ly, lz = block
    gx, gy, gz = (lax.axis_size(name) for name in ("gx", "gy", "gz"))
    hops_x, hops_y = -(-(ITERS + 1) // lx), -(-(ITERS + 1) // ly)
    full = gx <= 2 * hops_x + 1 and gy <= hops_y + 1
    return Geometry(lx, ly, lz, gx, gy, gz, hops_x, hops_y, full)


def places(geo):
    result, tile, at = [], 0, 0
    for reach in REACHES:
        for _ in range(geo.lx):
            if at + 2 * reach > geo.lz:
                tile, at = tile + 1, 0
            result.append((tile, at + reach))
            at += 2 * reach
    return result, tile + 1


def left_lanes(geo):
    spots, tiles = places(geo)
    mask = np.zeros((tiles, 1, geo.lz), np.bool_)
    for index, (tile, centre) in enumerate(spots):
        mask[tile, 0, centre - REACHES[index // geo.lx] : centre] = True
    return mask


def iota(shape, dim):
    return lax.broadcasted_iota(jnp.int32, shape, dim)


def pack_kernel(geo, new, old, energy_max, region, dirichlet, main, slab):
    spots, tiles = places(geo)
    lane = iota((geo.ly, geo.lz), 1)
    edges = [jnp.zeros((geo.ly, geo.lz), jnp.float32)] * tiles
    for i in range(geo.lx):
        share = (1 - dirichlet[i]).astype(jnp.float32)
        values = [new[a, i] * share for a in range(3)]
        values += [energy_max[i], region[i].astype(jnp.float32)]
        values += [old[a, i] * share for a in range(3)]
        for f, value in enumerate(values):
            main[f * geo.lx + i] = value
            tile, centre = spots[f * geo.lx + i]
            inside = (lane >= centre - REACHES[f]) & (lane < centre + REACHES[f])
            edges[tile] = jnp.where(inside, pltpu.roll(value, centre, 1), edges[tile])
    for tile in range(tiles):
        slab[tile] = edges[tile]


def lookup(table, label):
    value = jnp.full(label.shape, table[table.shape[0] - 1], jnp.float32)
    for index in range(table.shape[0] - 1):
        value = jnp.where(label == index, table[index], value)
    return value


def deviator(grad):
    trace_third = (grad[0][0] + grad[1][1] + grad[2][2]) / 3.0
    return [
        grad[0][0] - trace_third,
        grad[1][1] - trace_third,
        grad[2][2] - trace_third,
        0.5 * (grad[1][2] + grad[2][1]),
        0.5 * (grad[0][2] + grad[2][0]),
        0.5 * (grad[1][0] + grad[0][1]),
    ]


def contract(dev):
    return (
        dev[0] * dev[0]
        + dev[1] * dev[1]
        + dev[2] * dev[2]
        + 2.0 * (dev[3] * dev[3] + dev[4] * dev[4] + dev[5] * dev[5])
    )


def soften(energy, energy_next, scale, ratio):
    return 1.0 - lax.erf((energy_next - energy) / scale) / ratio


def basis_kernel(geo, shear, ratio, scale, blocks, basis, dev_own, grams, held, field, dev_all):
    lx, ly, lz = geo.lx, geo.ly, geo.lz
    planes, rows, lanes = geo.bx * lx, geo.by * ly, 2 * lz
    spots, _ = places(geo)
    row, lane = iota((rows, lanes), 0), iota((rows, lanes), 1)
    index_y, index_z = lax.axis_index("gy"), lax.axis_index("gz")
    if geo.full:
        grid_row = row
        own_x, own_y = lax.axis_index("gx") * lx, pl.multiple_of(index_y * ly, ly)
    else:
        grid_row = index_y * ly + jnp.where(row < (1 + geo.hops_y) * ly, row, row - rows)
        own_x, own_y = 0, 0
    end_y, start_y = grid_row == geo.gy * ly - 1, grid_row == 0
    end_z = (lane == lz - 1) & (index_z == geo.gz - 1)
    start_z = (lane == 0) & (index_z == 0)

    def whole_plane(f, p):
        tile, centre = spots[f * lx + p % lx]
        parts = []
        for b in range(geo.by):
            at = (p // lx) * geo.by + b
            edge = pltpu.roll(blocks[at, FIELDS * lx + tile], lz - centre, 1)
            parts.append(jnp.concatenate([blocks[at, f * lx + p % lx], edge], axis=1))
        return jnp.concatenate(parts, axis=0)

    def beside(value):
        next_y = jnp.where(end_y, 0.0, pltpu.roll(value, rows - 1, 0))
        prev_y = jnp.where(start_y, 0.0, pltpu.roll(value, 1, 0))
        next_z = jnp.where(end_z, 0.0, pltpu.roll(value, lanes - 1, 1))
        prev_z = jnp.where(start_z, 0.0, pltpu.roll(value, 1, 1))
        return next_y, prev_y, next_z, prev_z

    for p in range(planes):
        for a in range(3):
            held[a, p] = whole_plane(a, p)
    for p in range(planes):
        grad = []
        for a in range(3):
            next_y, prev_y, next_z, prev_z = beside(held[a, p])
            next_x, prev_x = held[a, (p + 1) % planes], held[a, (p - 1) % planes]
            grad.append([0.5 * (next_x - prev_x), 0.5 * (next_y - prev_y), 0.5 * (next_z - prev_z)])
        dev = deviator(grad)
        for k in range(6):
            dev_all[k, p] = dev[k][:, :lz]
        label = whole_plane(4, p)
        energy = lookup(shear, label) * contract(dev)
        energy_next = jnp.maximum(whole_plane(3, p), energy)
        softening = soften(energy, energy_next, lookup(scale, label), lookup(ratio, label))
        field[0, p] = softening * energy
    for j, shift in enumerate(SHIFTS):
        for p in range(planes):
            value = field[j, p]
            next_y, prev_y, next_z, prev_z = beside(value)
            next_x, prev_x = field[j, (p + 1) % planes], field[j, (p - 1) % planes]
            image = (value - next_x) + (value - prev_x)
            image += (value - next_y) + (value - prev_y)
            image += (value - next_z) + (value - prev_z)
            field[j + 1, p] = image - shift * value if shift else image

    grams[...] = jnp.zeros(grams.shape, jnp.float32)
    sums = [jnp.zeros((ly, lz), jnp.float32)] * len(PAIRS)
    for p in range(planes if geo.full else lx):
        for b in range(geo.by if geo.full else 1):
            own = [field[j, p, b * ly : (b + 1) * ly, :lz] for j in range(ITERS + 1)]
            sums = [total + own[i] * own[j] for total, (i, j) in zip(sums, PAIRS)]
    for k, total in enumerate(sums):
        grams[k : k + 1, :] = jnp.sum(total, axis=0, keepdims=True)
    for i in range(lx):
        for j in range(ITERS + 1):
            basis[j, i] = field[j, own_x + i, pl.ds(own_y, ly), :lz]
        for k in range(6):
            dev_own[k, i] = dev_all[k, own_x + i, pl.ds(own_y, ly), :]


def visco_kernel(
    geo, moduli, times, shear, ratio, scale, blocks, dev_own, visco, energy_max, region, stress, visco_next, energy_next
):
    lx, ly, lz = geo.lx, geo.ly, geo.lz
    spots, _ = places(geo)
    row, lane = iota((ly, lz), 0), iota((ly, lz), 1)
    index_y = lax.axis_index("gy")
    own_x, own_y = (lax.axis_index("gx"), index_y) if geo.full else (0, 0)

    def block(step_x, step_y):
        return lax.rem(own_x + step_x + geo.bx, geo.bx) * geo.by + lax.rem(own_y + step_y + geo.by, geo.by)

    here, right, left, above, below = block(0, 0), block(1, 0), block(-1, 0), block(0, 1), block(0, -1)
    regions, terms = moduli.shape
    for i in range(lx):
        grad = []
        for a in range(3):
            at = (WIDE + a) * lx + i
            value = blocks[here, at]
            next_x = blocks[here, at + 1] if i + 1 < lx else blocks[right, at + 1 - lx]
            prev_x = blocks[here, at - 1] if i else blocks[left, at + lx - 1]
            first = jnp.where(index_y == geo.gy - 1, 0.0, blocks[above, at])
            last = jnp.where(index_y == 0, 0.0, blocks[below, at])
            next_y = pltpu.roll(jnp.where(row == 0, first, value), ly - 1, 0)
            prev_y = pltpu.roll(jnp.where(row == ly - 1, last, value), 1, 0)
            tile, centre = spots[at]
            edge = blocks[here, FIELDS * lx + tile]
            next_z = jnp.where(lane == lz - 1, pltpu.roll(edge, lz - 1 - centre, 1), pltpu.roll(value, lz - 1, 1))
            prev_z = jnp.where(lane == 0, pltpu.roll(edge, lz + 1 - centre, 1), pltpu.roll(value, 1, 1))
            grad.append([0.5 * (next_x - prev_x), 0.5 * (next_y - prev_y), 0.5 * (next_z - prev_z)])
        dev_old = deviator(grad)
        dev_new = [dev_own[k, i] for k in range(6)]
        label = region[i]
        masks = [label == index for index in range(regions - 1)]

        def choose(entries):
            value = jnp.full(label.shape, entries[-1], jnp.float32)
            for mask, entry in zip(masks, entries):
                value = jnp.where(mask, entry, value)
            return value

        shear_cells = choose([shear[r] for r in range(regions)])
        energy = shear_cells * contract(dev_new)
        energy_after = jnp.maximum(energy_max[i], energy)
        energy_next[i] = energy_after
        softening = soften(
            energy,
            energy_after,
            choose([scale[r] for r in range(regions)]),
            choose([ratio[r] for r in range(regions)]),
        )
        jump = [2.0 * shear_cells * (dev_new[k] - dev_old[k]) for k in range(6)]
        totals, long_term = [0.0] * 6, 1.0
        for term in range(terms):
            modulus = choose([moduli[r, term] for r in range(regions)])
            time = choose([times[r, term] for r in range(regions)])
            decay = jnp.exp(-1.0 / time)
            weight = modulus * (1.0 - decay) * time
            long_term = long_term - modulus
            for k in range(6):
                value = decay * visco[term, k, i] + weight * jump[k]
                visco_next[term, k, i] = value
                totals[k] = totals[k] + value
        for k in range(6):
            stress[k, i] = softening * (long_term * 2.0 * shear_cells * dev_new[k] + totals[k])


def solve_kernel(geo, grams, basis, damage, residual):
    total = grams[0]
    for n in range(1, grams.shape[0]):
        total = total + grams[n]
    column = jnp.sum(total, axis=1, keepdims=True)
    gram = {}
    for k, (i, j) in enumerate(PAIRS):
        gram[i, j] = gram[j, i] = column[k : k + 1]

    def image_of(p):
        out = [(1.0 + LENGTH_SQUARED * SHIFTS[j]) * p[j] for j in range(len(p))]
        out.append(LENGTH_SQUARED * p[-1])
        for j in range(1, len(p)):
            out[j] = out[j] + LENGTH_SQUARED * p[j - 1]
        return out

    def product(u, v):
        value = None
        for i in range(len(u)):
            inner = None
            for j in range(len(v)):
                inner = gram[i, j] * v[j] if inner is None else inner + gram[i, j] * v[j]
            value = u[i] * inner if value is None else value + u[i] * inner
        return value

    one = jnp.ones((1, 1), jnp.float32)
    field, rest, direction = [], [one], [one]
    norm_now = gram[0, 0]
    for iteration in range(ITERS):
        image = image_of(direction)
        alpha = norm_now / product(image, direction)
        field = [x + alpha * d for x, d in zip(field, direction)] + [alpha * direction[-1]]
        rest = [r - alpha * w for r, w in zip(rest, image)] + [-alpha * image[-1]]
        if iteration + 1 < ITERS:
            norm_next = product(rest, rest)
            beta = norm_next / norm_now
            direction = [r + beta * d for r, d in zip(rest, direction)] + [rest[-1]]
            norm_now = norm_next
    for i in range(geo.lx):
        vectors = [basis[j, i] for j in range(ITERS + 1)]
        damage[i] = functools.reduce(jnp.add, [c * t for c, t in zip(field, vectors)])
        residual[i] = functools.reduce(jnp.add, [c * t for c, t in zip(rest, vectors)])


def shaped(*shape):
    return jax.ShapeDtypeStruct(shape, jnp.float32)


def call(kernel, outs, tables, arrays, scratch=(), flops=0, vmem=32 * MB):
    smem, vmem_spec = pl.BlockSpec(memory_space=pltpu.SMEM), pl.BlockSpec(memory_space=pltpu.VMEM)
    moved = 4 * sum(int(np.prod(a.shape)) for a in list(arrays) + list(outs))
    return pl.pallas_call(
        kernel,
        out_shape=outs,
        in_specs=[smem] * len(tables) + [vmem_spec] * len(arrays),
        out_specs=[vmem_spec] * len(outs),
        scratch_shapes=list(scratch),
        compiler_params=pltpu.CompilerParams(vmem_limit_bytes=vmem),
        cost_estimate=pl.CostEstimate(flops=flops, bytes_accessed=moved, transcendentals=0),
    )(*tables, *arrays)


def ring(shard, axis, hops):
    count = lax.axis_size(axis)
    steps = list(range(hops + 1)) + list(range(-hops, 0))
    moved = [lax.ppermute(shard, axis, [((i + step) % count, i) for i in range(count)]) if step else shard for step in steps]
    return jnp.stack(moved)


def on_device(
    displacement,
    displacement_old,
    visco_state,
    energy_max,
    region,
    dirichlet,
    prony_moduli,
    prony_times,
    shear_modulus,
    mullins_ratio,
    mullins_scale,
):
    geo = geometry(energy_max.shape)
    lx, ly, lz = energy_max.shape
    _, tiles = places(geo)
    main, slab = call(
        functools.partial(pack_kernel, geo),
        [shaped(FIELDS * lx, ly, lz), shaped(tiles, ly, lz)],
        [],
        [displacement, displacement_old, energy_max, region, dirichlet],
    )
    up = [(i, i + 1) for i in range(geo.gz - 1)]
    down = [(j, i) for i, j in up]
    from_left, from_right = lax.ppermute(slab, "gz", up), lax.ppermute(slab, "gz", down)
    edges = jnp.where(left_lanes(geo), from_left, from_right)
    payload = jnp.concatenate([main, edges], axis=0)
    if geo.full:
        blocks = lax.all_gather(payload, ("gx", "gy"))
    else:
        blocks = ring(ring(payload, "gy", geo.hops_y), "gx", geo.hops_x)
        blocks = blocks.reshape((geo.bx * geo.by,) + payload.shape)
    planes, rows = geo.bx * lx, geo.by * ly
    basis, dev_own, grams = call(
        functools.partial(basis_kernel, geo),
        [shaped(ITERS + 1, lx, ly, lz), shaped(6, lx, ly, lz), shaped(-(-len(PAIRS) // 8) * 8, lz)],
        [shear_modulus, mullins_ratio, mullins_scale],
        [blocks],
        [
            pltpu.VMEM((3, planes, rows, 2 * lz), jnp.float32),
            pltpu.VMEM((ITERS + 1, planes, rows, 2 * lz), jnp.float32),
            pltpu.VMEM((6, planes, rows, lz), jnp.float32),
        ],
        flops=planes * rows * lz * 500,
    )
    if geo.full:
        sums = lax.all_gather(grams, "gz")
    else:
        sums = lax.psum(grams, ("gx", "gy", "gz"))[None]
    stress, visco_next, energy_next = call(
        functools.partial(visco_kernel, geo),
        [shaped(6, lx, ly, lz), shaped(*visco_state.shape), shaped(lx, ly, lz)],
        [prony_moduli, prony_times, shear_modulus, mullins_ratio, mullins_scale],
        [blocks, dev_own, visco_state, energy_max, region],
        flops=lx * ly * lz * 500,
    )
    damage_field, residual = call(
        functools.partial(solve_kernel, geo),
        [shaped(lx, ly, lz), shaped(lx, ly, lz)],
        [],
        [sums, basis],
    )
    return (stress, visco_next, energy_next, damage_field, residual)


def solution(mesh):
    in_specs = (
        P(None, "gx", "gy", "gz"),
        P(None, "gx", "gy", "gz"),
        P(None, None, "gx", "gy", "gz"),
        P("gx", "gy", "gz"),
        P("gx", "gy", "gz"),
        P("gx", "gy", "gz"),
        P(),
        P(),
        P(),
        P(),
        P(),
    )
    out_specs = (
        P(None, "gx", "gy", "gz"),
        P(None, None, "gx", "gy", "gz"),
        P("gx", "gy", "gz"),
        P("gx", "gy", "gz"),
        P("gx", "gy", "gz"),
    )
    return jax.shard_map(
        on_device, mesh=mesh, in_specs=in_specs, out_specs=out_specs, check_vma=False
    )
```

time: 263 us -> 50.6 us (0.19)
  blocking collectives: 157 us -> 30.9 us
  waiting for transfers between devices: 38.3 us -> 4.2 us
  starting transfers between devices: 39.9 us -> 6.22 us
  between operations: 14.8 us -> 0.73 us
  other arithmetic: 8.93 us -> 0.01 us
  Pallas kernels: 0 us -> 3.85 us
    psum x4 -> x0, blocking collectives: 157 us -> none  [merged_products(): lax.psum((jnp.sum(residual * residual), jnp.sum(residual * image_res)), (...]
    ppermute x30 -> x2, waiting for transfers between devices: 38.3 us -> 4.2 us  [the longest x1 4.19 us: on_device(): lax.ppermute(slab, 'gz', down)]
    ppermute x30 -> x2, starting transfers between devices: 39.9 us -> 6.22 us  [the longest x1 4.93 us: on_device(): lax.ppermute(slab, 'gz', up)]
    all_gather x0 -> x2, blocking collectives: none -> 30.9 us  [the longest x1 17.5 us: on_device(): blocks = lax.all_gather(payload, ('gx', 'gy'))]
    reduce_sum x8 -> x0, other arithmetic: 5 us -> none  [the longest x4 2.76 us: merged_products(): jnp.sum(residual * image_res)]
    pallas_call x0 -> x4, Pallas kernels: none -> 3.85 us  [call(): pl.pallas_call(kernel, out_shape=outs, in_specs=[smem] * len(tables) + [v...]
    unnamed x16 -> x28, local copies, waits for them, and re-layouts: 1.22 us -> 4.26 us
  transfers between devices with their start and end apart: 30 -> 2, of which waited for: 28 -> 1; matrix products, arithmetic and copies ran while one was open for 1% -> 0% of each run, Pallas kernels for 0% -> 0%
where the time goes in v1:
time: 50.6 us; the launch traced here: 50.2 us
  blocking collectives  30.9 us (61%)
  starting transfers between devices  6.22 us (12%)
  local copies, waits for them, and re-layouts  4.26 us (8%)
  waiting for transfers between devices  4.2 us (8%)
  Pallas kernels  3.85 us (8%)
  between operations  0.73 us (1%)
    all_gather x1, blocking collectives, on_device(): blocks = lax.all_gather(payload, ('gx', 'gy'))  17.5 us
    all_gather x1, blocking collectives, on_device(): sums = lax.all_gather(grams, 'gz')  13.4 us
    ppermute x1, starting transfers between devices, on_device(): lax.ppermute(slab, 'gz', up)  4.93 us
    unnamed x28, local copies, waits for them, and re-layouts  4.26 us
    ppermute x1, waiting for transfers between devices, on_device(): lax.ppermute(slab, 'gz', down)  4.19 us
    pallas_call x4, Pallas kernels, call(): pl.pallas_call(kernel, out_shape=outs, in_specs=[smem] * len(tables) + [v...  3.85 us
    ppermute x1, starting transfers between devices, on_device(): lax.ppermute(slab, 'gz', down)  1.29 us
  transfers between devices with their start and end apart: 2, of which 1 were waited for; matrix products, arithmetic and copies ran while one was open for 0% of the time, Pallas kernels for 0%

profile of v1, /device:TPU:0, one launch (start us, length us, event | category | flops | bytes accessed | tf_op | source)
XLA Modules:
  0.0 50.2 jit_solution(4753616646202160383)
XLA Ops:
  0.6 0.0 copy-start.1
  0.6 0.7 %copy-done.1 = f32[2,8,128]{2,1,0:T(8,128)S(1)} copy-done((f32[2,8,128]{2,1,0:T(8,128)S(1)}, f32[2,8,128]{2,1,0:T(8,128)}, u32[]{:S(2)}) %copy-start.1) | copy-done | bytes 8216
  1.3 0.7 %copy-done.3 = s32[2,8,128]{2,1,0:T(8,128)S(1)} copy-done((s32[2,8,128]{2,1,0:T(8,128)S(1)}, s32[2,8,128]{2,1,0:T(8,128)}, u32[]{:S(2)}) %copy-start.3) | copy-done | bytes 8216
  2.0 0.7 %copy-done.5 = f32[3,2,8,128]{3,2,1,0:T(8,128)S(1)} copy-done((f32[3,2,8,128]{3,2,1,0:T(8,128)S(1)}, f32[3,2,8,128]{3,2,1,0:T(8,128)}, u32[]{:S(2)}) %copy-start.5) | copy-done | bytes 24600
  2.8 0.7 %copy-done.6 = f32[3,2,8,128]{3,2,1,0:T(8,128)S(1)} copy-done((f32[3,2,8,128]{3,2,1,0:T(8,128)S(1)}, f32[3,2,8,128]{3,2,1,0:T(8,128)}, u32[]{:S(2)}) %copy-start.6) | copy-done | bytes 24600
  3.5 0.7 %copy-done.7 = s32[2,8,128]{2,1,0:T(8,128)S(1)} copy-done((s32[2,8,128]{2,1,0:T(8,128)S(1)}, s32[2,8,128]{2,1,0:T(8,128)}, u32[]{:S(2)}) %copy-start.7) | copy-done | bytes 8216
  4.2 0.1 shard_map.155
  4.3 0.0 copy-start.13
  4.3 4.9 %collective-permute-start = (f32[1,8,128]{2,1,0:T(8,128)S(1)}, f32[1,8,128]{2,1,0:T(8,128)S(1)}, u32[]{:S(2)}, u32[]{:S(2)}) collective-permute-start(f32[1,8,128]{2,1,0:T(8,128)S(1)} %get-tuple-element.16), channel_id=1, source_target_pairs={{0,1},{1,2},{2,3},{4,5},{5,6},{6,7},{8,9},{9,10},{10,11},{12,13},{... | collective-permute-start | bytes 12296 | tf_op jit(solution)/shard_map/ppermute | solution.py:359
  9.2 1.3 %collective-permute-start.1 = (f32[1,8,128]{2,1,0:T(8,128)S(1)}, f32[1,8,128]{2,1,0:T(8,128)S(1)}, u32[]{:S(2)}, u32[]{:S(2)}) collective-permute-start(f32[1,8,128]{2,1,0:T(8,128)S(1)} %get-tuple-element.16), channel_id=1, source_target_pairs={{1,0},{2,1},{3,2},{5,4},{6,5},{7,6},{9,8},{10,9},{11,10},{13,12},{... | collective-permute-start | bytes 12296 | tf_op jit(solution)/shard_map/ppermute | solution.py:359
  10.5 0.0 collective-permute-done
  10.6 4.2 %collective-permute-done.1 = f32[1,8,128]{2,1,0:T(8,128)S(1)} collective-permute-done((f32[1,8,128]{2,1,0:T(8,128)S(1)}, f32[1,8,128]{2,1,0:T(8,128)S(1)}, u32[]{:S(2)}, u32[]{:S(2)}) %collective-permute-start.1) | collective-permute-done | bytes 4128 | tf_op jit(solution)/shard_map/ppermute | solution.py:359
  14.7 0.0 copy-done.13
  14.8 17.5 %all-gather = f32[136,8,128]{2,1,0:T(8,128)S(1)} all-gather(f32[17,8,128]{2,1,0:T(8,128)S(1)} %pad_maximum_fusion), channel_id=2, replica_groups=mesh['gx'=4,'gy'=2,'gz'=4] {'gx','gy'}, dimensions={0}, use_global_device_ids=true | all-gather | bytes 626688 | tf_op jit(solution)/shard_map/all_gather | solution.py:363
  32.3 0.0 copy-start.12
  32.3 0.6 %copy-done.10 = f32[4]{0:T(128)S(1)} copy-done((f32[4]{0:T(128)S(1)}, f32[4]{0:T(128)}, u32[]{:S(2)}) %copy-start.10) | copy-done | bytes 40
  32.9 0.0 copy-done.11
  33.0 0.0 copy-done.12
  33.0 1.4 %shard_map.156 = (f32[5,2,8,128]{3,2,1,0:T(8,128)S(1)}, f32[6,2,8,128]{3,2,1,0:T(8,128)S(1)}, f32[16,128]{1,0:T(8,128)S(1)}) custom-call(f32[4]{0:T(128)S(1)} %copy-done.10, f32[4]{0:T(128)S(1)} %copy-done.11, f32[4]{0:T(128)S(1)} %copy-done.12, f32[8,17,8,128]{3,2,1,0:T(8,128)S(1)} %bitcast.2), custom_call_target="tpu_custom_call" | custom-call | flops 8192000 | bytes 655360 | tf_op jit(solution)/shard_map/pallas_call | solution.py:317
  34.4 13.4 %all-gather.1 = f32[64,128]{1,0:T(8,128)S(1)} all-gather(f32[16,128]{1,0:T(8,128)S(1)} %get-tuple-element.21), channel_id=3, replica_groups=mesh['gx'=4,'gy'=2,'gz'=4] {'gz'}, dimensions={0}, use_global_device_ids=true | all-gather | bytes 40960 | tf_op jit(solution)/shard_map/all_gather | solution.py:381
  47.8 0.8 %shard_map.158 = (f32[2,8,128]{2,1,0:T(8,128)}, f32[2,8,128]{2,1,0:T(8,128)}) custom-call(f32[4,16,128]{2,1,0:T(8,128)S(1)} %bitcast.4, f32[5,2,8,128]{3,2,1,0:T(8,128)S(1)} %get-tuple-element.22.basis), custom_call_target="tpu_custom_call" | custom-call | bytes 90112 | tf_op jit(solution)/shard_map/pallas_call | solution.py:317
  48.7 0.0 copy-done.8
  48.7 0.0 copy-done.9
  48.7 1.5 %shard_map.157 = (f32[6,2,8,128]{3,2,1,0:T(8,128)}, f32[6,6,2,8,128]{4,3,2,1,0:T(8,128)}, f32[2,8,128]{2,1,0:T(8,128)}) custom-call(f32[4,6]{1,0:T(4,128)S(1)} %copy-done.8, f32[4,6]{1,0:T(4,128)S(1)} %copy-done.9, f32[4]{0:T(128)S(1)} %copy-done.10, f32[4]{0:T(128)S(1)} %copy-done.11, f32[4]{0:T(128)S(1)} %copy-done.12, f32[8,17,8,128]{3,2,1,0:T(8,128)S(1)} %bitcast.3, ...), custom_call_target="tpu_custom_call" | custom-call | flops 1024000 | bytes 1269760 | tf_op jit(solution)/shard_map/pallas_call | solution.py:317
  (16 shorter events, 0.0 us)
Async XLA Ops:
  0.6 0.7 %copy-start.1 = (f32[2,8,128]{2,1,0:T(8,128)S(1)}, f32[2,8,128]{2,1,0:T(8,128)}, u32[]{:S(2)}) copy-start(f32[2,8,128]{2,1,0:T(8,128)} %energy_max.3) | copy-start | bytes 24580
  1.3 0.7 %copy-start.3 = (s32[2,8,128]{2,1,0:T(8,128)S(1)}, s32[2,8,128]{2,1,0:T(8,128)}, u32[]{:S(2)}) copy-start(s32[2,8,128]{2,1,0:T(8,128)} %region.3) | copy-start | bytes 24580
  2.0 0.7 %copy-start.5 = (f32[3,2,8,128]{3,2,1,0:T(8,128)S(1)}, f32[3,2,8,128]{3,2,1,0:T(8,128)}, u32[]{:S(2)}) copy-start(f32[3,2,8,128]{3,2,1,0:T(8,128)} %new.1) | copy-start | bytes 73732
  2.8 0.7 %copy-start.6 = (f32[3,2,8,128]{3,2,1,0:T(8,128)S(1)}, f32[3,2,8,128]{3,2,1,0:T(8,128)}, u32[]{:S(2)}) copy-start(f32[3,2,8,128]{3,2,1,0:T(8,128)} %old.1) | copy-start | bytes 73732
  3.5 0.7 %copy-start.7 = (s32[2,8,128]{2,1,0:T(8,128)S(1)}, s32[2,8,128]{2,1,0:T(8,128)}, u32[]{:S(2)}) copy-start(s32[2,8,128]{2,1,0:T(8,128)} %dirichlet.1) | copy-start | bytes 24580
  4.3 10.5 %copy-start.13 = (pred[128]{0:T(512)(128)(4,1)S(1)}, pred[128]{0:T(512)(128)(4,1)}, u32[]{:S(2)}) copy-start(pred[128]{0:T(512)(128)(4,1)} %constant.9) | copy-start | bytes 388
  4.3 6.2 %collective-permute-start = (f32[1,8,128]{2,1,0:T(8,128)S(1)}, f32[1,8,128]{2,1,0:T(8,128)S(1)}, u32[]{:S(2)}, u32[]{:S(2)}) collective-permute-start(f32[1,8,128]{2,1,0:T(8,128)S(1)} %get-tuple-element.16), channel_id=1, source_target_pairs={{0,1},{1,2},{2,3},{4,5},{5,6},{6,7},{8,9},{9,10},{10,11},{12,13},{... | collective-permute-start | bytes 12296 | tf_op jit(solution)/shard_map/ppermute | solution.py:359
  9.2 5.5 %collective-permute-start.1 = (f32[1,8,128]{2,1,0:T(8,128)S(1)}, f32[1,8,128]{2,1,0:T(8,128)S(1)}, u32[]{:S(2)}, u32[]{:S(2)}) collective-permute-start(f32[1,8,128]{2,1,0:T(8,128)S(1)} %get-tuple-element.16), channel_id=1, source_target_pairs={{1,0},{2,1},{3,2},{5,4},{6,5},{7,6},{9,8},{10,9},{11,10},{13,12},{... | collective-permute-start | bytes 12296 | tf_op jit(solution)/shard_map/ppermute | solution.py:359
  32.3 0.7 %copy-start.10 = (f32[4]{0:T(128)S(1)}, f32[4]{0:T(128)}, u32[]{:S(2)}) copy-start(f32[4]{0:T(128)} %shear.3) | copy-start | bytes 52
  32.3 0.7 %copy-start.11 = (f32[4]{0:T(128)S(1)}, f32[4]{0:T(128)}, u32[]{:S(2)}) copy-start(f32[4]{0:T(128)} %ratio.3) | copy-start | bytes 52
  32.3 0.7 %copy-start.12 = (f32[4]{0:T(128)S(1)}, f32[4]{0:T(128)}, u32[]{:S(2)}) copy-start(f32[4]{0:T(128)} %scale.3) | copy-start | bytes 52
  33.0 15.7 %copy-start = (f32[6,6,2,8,128]{4,3,2,1,0:T(8,128)S(1)}, f32[6,6,2,8,128]{4,3,2,1,0:T(8,128)}, u32[]{:S(2)}) copy-start(f32[6,6,2,8,128]{4,3,2,1,0:T(8,128)} %visco.1) | copy-start | bytes 884740
  47.8 0.8 %copy-start.2 = (f32[2,8,128]{2,1,0:T(8,128)S(1)}, f32[2,8,128]{2,1,0:T(8,128)}, u32[]{:S(2)}) copy-start(f32[2,8,128]{2,1,0:T(8,128)} %energy_max.3) | copy-start | bytes 24580
  47.8 0.8 %copy-start.4 = (s32[2,8,128]{2,1,0:T(8,128)S(1)}, s32[2,8,128]{2,1,0:T(8,128)}, u32[]{:S(2)}) copy-start(s32[2,8,128]{2,1,0:T(8,128)} %region.3) | copy-start | bytes 24580
  47.8 0.9 %copy-start.8 = (f32[4,6]{1,0:T(4,128)S(1)}, f32[4,6]{1,0:T(4,128)}, u32[]{:S(2)}) copy-start(f32[4,6]{1,0:T(4,128)} %moduli.1) | copy-start | bytes 292
  47.8 0.9 %copy-start.9 = (f32[4,6]{1,0:T(4,128)S(1)}, f32[4,6]{1,0:T(4,128)}, u32[]{:S(2)}) copy-start(f32[4,6]{1,0:T(4,128)} %times.1) | copy-start | bytes 292

commit v2 on v1

--- a/solution.py
+++ b/solution.py
@@ -72,7 +72,41 @@
     return lax.broadcasted_iota(jnp.int32, shape, dim)
 
 
-def pack_kernel(geo, new, old, energy_max, region, dirichlet, main, slab):
+def pack_kernel(
+    geo,
+    new_hbm,
+    old_hbm,
+    energy_hbm,
+    region_hbm,
+    dirichlet_hbm,
+    moduli_hbm,
+    times_hbm,
+    shear_hbm,
+    ratio_hbm,
+    scale_hbm,
+    main,
+    slab,
+    tables,
+    new,
+    old,
+    energy_max,
+    region,
+    dirichlet,
+    moduli,
+    times,
+    shear,
+    ratio,
+    scale,
+    arrived,
+):
+    sources = (new_hbm, old_hbm, energy_hbm, region_hbm, dirichlet_hbm)
+    sources += (moduli_hbm, times_hbm, shear_hbm, ratio_hbm, scale_hbm)
+    targets = (new, old, energy_max, region, dirichlet, moduli, times, shear, ratio, scale)
+    copies = [pltpu.make_async_copy(a, b, arrived.at[n]) for n, (a, b) in enumerate(zip(sources, targets))]
+    for copy in copies:
+        copy.start()
+    for copy in copies:
+        copy.wait()
     spots, tiles = places(geo)
     lane = iota((geo.ly, geo.lz), 1)
     edges = [jnp.zeros((geo.ly, geo.lz), jnp.float32)] * tiles
@@ -88,12 +122,21 @@
             edges[tile] = jnp.where(inside, pltpu.roll(value, centre, 1), edges[tile])
     for tile in range(tiles):
         slab[tile] = edges[tile]
-
-
-def lookup(table, label):
-    value = jnp.full(label.shape, table[table.shape[0] - 1], jnp.float32)
-    for index in range(table.shape[0] - 1):
-        value = jnp.where(label == index, table[index], value)
+    regions, terms = moduli.shape
+    for r in range(regions):
+        entries = [shear[r], ratio[r], scale[r]]
+        entries += [moduli[r, k] for k in range(terms)] + [times[r, k] for k in range(terms)]
+        for k, entry in enumerate(entries):
+            tables[k, r : r + 1, :] = jnp.full((1, geo.lz), entry, jnp.float32)
+
+
+SHEAR, RATIO, SCALE, MODULI = range(4)
+
+
+def lookup(tables, entry, masks):
+    value = tables[entry, len(masks) : len(masks) + 1, :]
+    for r, mask in enumerate(masks):
+        value = jnp.where(mask, tables[entry, r : r + 1, :], value)
     return value
 
 
@@ -122,9 +165,10 @@
     return 1.0 - lax.erf((energy_next - energy) / scale) / ratio
 
 
-def basis_kernel(geo, shear, ratio, scale, blocks, basis, dev_own, grams, held, field, dev_all):
+def basis_kernel(geo, tables, blocks, basis, dev_own, grams, held, field, dev_all):
     lx, ly, lz = geo.lx, geo.ly, geo.lz
     planes, rows, lanes = geo.bx * lx, geo.by * ly, 2 * lz
+    regions = tables.shape[1]
     spots, _ = places(geo)
     row, lane = iota((rows, lanes), 0), iota((rows, lanes), 1)
     index_y, index_z = lax.axis_index("gy"), lax.axis_index("gz")
@@ -167,9 +211,14 @@
         for k in range(6):
             dev_all[k, p] = dev[k][:, :lz]
         label = whole_plane(4, p)
-        energy = lookup(shear, label) * contract(dev)
+        halves = []
+        for half in (slice(0, lz), slice(lz, lanes)):
+            masks = [label[:, half] == r for r in range(regions - 1)]
+            halves.append([lookup(tables, entry, masks) for entry in (SHEAR, SCALE, RATIO)])
+        shear_cells, scale_cells, ratio_cells = [jnp.concatenate(pair, axis=1) for pair in zip(*halves)]
+        energy = shear_cells * contract(dev)
         energy_next = jnp.maximum(whole_plane(3, p), energy)
-        softening = soften(energy, energy_next, lookup(scale, label), lookup(ratio, label))
+        softening = soften(energy, energy_next, scale_cells, ratio_cells)
         field[0, p] = softening * energy
     for j, shift in enumerate(SHIFTS):
         for p in range(planes):
@@ -197,7 +246,7 @@
 
 
 def visco_kernel(
-    geo, moduli, times, shear, ratio, scale, blocks, dev_own, visco, energy_max, region, stress, visco_next, energy_next
+    geo, tables, blocks, dev_own, visco, stress, visco_next, energy_next
 ):
     lx, ly, lz = geo.lx, geo.ly, geo.lz
     spots, _ = places(geo)
@@ -209,7 +258,7 @@
         return lax.rem(own_x + step_x + geo.bx, geo.bx) * geo.by + lax.rem(own_y + step_y + geo.by, geo.by)
 
     here, right, left, above, below = block(0, 0), block(1, 0), block(-1, 0), block(0, 1), block(0, -1)
-    regions, terms = moduli.shape
+    regions, terms = tables.shape[1], visco.shape[0]
     for i in range(lx):
         grad = []
         for a in range(3):
@@ -228,30 +277,18 @@
             grad.append([0.5 * (next_x - prev_x), 0.5 * (next_y - prev_y), 0.5 * (next_z - prev_z)])
         dev_old = deviator(grad)
         dev_new = [dev_own[k, i] for k in range(6)]
-        label = region[i]
-        masks = [label == index for index in range(regions - 1)]
-
-        def choose(entries):
-            value = jnp.full(label.shape, entries[-1], jnp.float32)
-            for mask, entry in zip(masks, entries):
-                value = jnp.where(mask, entry, value)
-            return value
-
-        shear_cells = choose([shear[r] for r in range(regions)])
+        label = blocks[here, 4 * lx + i]
+        masks = [label == r for r in range(regions - 1)]
+        shear_cells, ratio_cells, scale_cells = [lookup(tables, entry, masks) for entry in (SHEAR, RATIO, SCALE)]
         energy = shear_cells * contract(dev_new)
-        energy_after = jnp.maximum(energy_max[i], energy)
+        energy_after = jnp.maximum(blocks[here, 3 * lx + i], energy)
         energy_next[i] = energy_after
-        softening = soften(
-            energy,
-            energy_after,
-            choose([scale[r] for r in range(regions)]),
-            choose([ratio[r] for r in range(regions)]),
-        )
+        softening = soften(energy, energy_after, scale_cells, ratio_cells)
         jump = [2.0 * shear_cells * (dev_new[k] - dev_old[k]) for k in range(6)]
         totals, long_term = [0.0] * 6, 1.0
         for term in range(terms):
-            modulus = choose([moduli[r, term] for r in range(regions)])
-            time = choose([times[r, term] for r in range(regions)])
+            modulus = lookup(tables, MODULI + term, masks)
+            time = lookup(tables, MODULI + terms + term, masks)
             decay = jnp.exp(-1.0 / time)
             weight = modulus * (1.0 - decay) * time
             long_term = long_term - modulus
@@ -311,18 +348,17 @@
     return jax.ShapeDtypeStruct(shape, jnp.float32)
 
 
-def call(kernel, outs, tables, arrays, scratch=(), flops=0, vmem=32 * MB):
-    smem, vmem_spec = pl.BlockSpec(memory_space=pltpu.SMEM), pl.BlockSpec(memory_space=pltpu.VMEM)
+def call(kernel, outs, arrays, scratch=(), flops=0, space=pltpu.VMEM, vmem=32 * MB):
     moved = 4 * sum(int(np.prod(a.shape)) for a in list(arrays) + list(outs))
     return pl.pallas_call(
         kernel,
         out_shape=outs,
-        in_specs=[smem] * len(tables) + [vmem_spec] * len(arrays),
-        out_specs=[vmem_spec] * len(outs),
+        in_specs=[pl.BlockSpec(memory_space=space)] * len(arrays),
+        out_specs=[pl.BlockSpec(memory_space=pltpu.VMEM)] * len(outs),
         scratch_shapes=list(scratch),
         compiler_params=pltpu.CompilerParams(vmem_limit_bytes=vmem),
         cost_estimate=pl.CostEstimate(flops=flops, bytes_accessed=moved, transcendentals=0),
-    )(*tables, *arrays)
+    )(*arrays)
 
 
 def ring(shard, axis, hops):
@@ -330,6 +366,18 @@
     steps = list(range(hops + 1)) + list(range(-hops, 0))
     moved = [lax.ppermute(shard, axis, [((i + step) % count, i) for i in range(count)]) if step else shard for step in steps]
     return jnp.stack(moved)
+
+
+def summed(terms, axis):
+    count = lax.axis_size(axis)
+    if count & (count - 1):
+        return lax.psum(terms, axis)[None]
+    step, parts = 1, [terms]
+    while step < count:
+        total = functools.reduce(jnp.add, parts)
+        parts = [total, lax.ppermute(total, axis, [(i, i ^ step) for i in range(count)])]
+        step *= 2
+    return jnp.stack(parts)
 
 
 def on_device(
@@ -348,11 +396,18 @@
     geo = geometry(energy_max.shape)
     lx, ly, lz = energy_max.shape
     _, tiles = places(geo)
-    main, slab = call(
+    regions, terms = prony_moduli.shape
+    arguments = [displacement, displacement_old, energy_max, region, dirichlet]
+    parameters = [prony_moduli, prony_times, shear_modulus, mullins_ratio, mullins_scale]
+    main, slab, tables = call(
         functools.partial(pack_kernel, geo),
-        [shaped(FIELDS * lx, ly, lz), shaped(tiles, ly, lz)],
-        [],
-        [displacement, displacement_old, energy_max, region, dirichlet],
+        [shaped(FIELDS * lx, ly, lz), shaped(tiles, ly, lz), shaped(MODULI + 2 * terms, regions, lz)],
+        arguments + parameters,
+        [pltpu.VMEM(a.shape, a.dtype) for a in arguments]
+        + [pltpu.SMEM(a.shape, a.dtype) for a in parameters]
+        + [pltpu.SemaphoreType.DMA((len(arguments) + len(parameters),))],
+        space=pl.ANY,
+        vmem=56 * MB,
     )
     up = [(i, i + 1) for i in range(geo.gz - 1)]
     down = [(j, i) for i, j in up]
@@ -360,7 +415,8 @@
     edges = jnp.where(left_lanes(geo), from_left, from_right)
     payload = jnp.concatenate([main, edges], axis=0)
     if geo.full:
-        blocks = lax.all_gather(payload, ("gx", "gy"))
+        copies = jnp.broadcast_to(payload[None], (geo.gx * geo.gy,) + payload.shape)
+        blocks = lax.all_to_all(copies, ("gx", "gy"), 0, 0)
     else:
         blocks = ring(ring(payload, "gy", geo.hops_y), "gx", geo.hops_x)
         blocks = blocks.reshape((geo.bx * geo.by,) + payload.shape)
@@ -368,8 +424,7 @@
     basis, dev_own, grams = call(
         functools.partial(basis_kernel, geo),
         [shaped(ITERS + 1, lx, ly, lz), shaped(6, lx, ly, lz), shaped(-(-len(PAIRS) // 8) * 8, lz)],
-        [shear_modulus, mullins_ratio, mullins_scale],
-        [blocks],
+        [tables, blocks],
         [
             pltpu.VMEM((3, planes, rows, 2 * lz), jnp.float32),
             pltpu.VMEM((ITERS + 1, planes, rows, 2 * lz), jnp.float32),
@@ -378,20 +433,18 @@
         flops=planes * rows * lz * 500,
     )
     if geo.full:
-        sums = lax.all_gather(grams, "gz")
+        sums = summed(grams, "gz")
     else:
         sums = lax.psum(grams, ("gx", "gy", "gz"))[None]
     stress, visco_next, energy_next = call(
         functools.partial(visco_kernel, geo),
         [shaped(6, lx, ly, lz), shaped(*visco_state.shape), shaped(lx, ly, lz)],
-        [prony_moduli, prony_times, shear_modulus, mullins_ratio, mullins_scale],
-        [blocks, dev_own, visco_state, energy_max, region],
+        [tables, blocks, dev_own, visco_state],
         flops=lx * ly * lz * 500,
     )
     damage_field, residual = call(
         functools.partial(solve_kernel, geo),
         [shaped(lx, ly, lz), shaped(lx, ly, lz)],
-        [],
         [sums, basis],
     )
     return (stress, visco_next, energy_next, damage_field, residual)

time: 50.6 us -> 36.3 us (0.72)
  blocking collectives: 30.9 us -> 14 us
  starting transfers between devices: 6.22 us -> 12.2 us
  local copies, waits for them, and re-layouts: 4.26 us -> 0.05 us
  other arithmetic: 0.01 us -> 0.85 us
    all_gather x2 -> x0, blocking collectives: 30.9 us -> none  [the longest x1 17.5 us: on_device(): blocks = lax.all_gather(payload, ('gx', 'gy'))]
    all_to_all x0 -> x1, blocking collectives: none -> 14 us  [on_device(): blocks = lax.all_to_all(copies, ('gx', 'gy'), 0, 0)]
    ppermute x0 -> x2, starting transfers between devices: none -> 5.38 us  [summed(): lax.ppermute(total, axis, [(i, i ^ step) for i in range(count)])]
    unnamed x28 -> x6, local copies, waits for them, and re-layouts: 4.26 us -> 0.02 us
    ppermute x1, waiting for transfers between devices: 4.19 us -> 0.01 us  [on_device(): lax.ppermute(slab, 'gz', down)]
    ppermute x0 -> x2, waiting for transfers between devices: none -> 2.4 us  [summed(): lax.ppermute(total, axis, [(i, i ^ step) for i in range(count)])]
    ppermute x1, waiting for transfers between devices: 0.01 us -> 1.51 us  [on_device(): lax.ppermute(slab, 'gz', up)]
    concatenate x1, other arithmetic: 0.01 us -> 0.84 us  [on_device(): payload = jnp.concatenate([main, edges], axis=0)]
  transfers between devices with their start and end apart: 2 -> 4, of which waited for: 1 -> 3; matrix products, arithmetic and copies ran while one was open for 0% -> 0% of each run, Pallas kernels for 0% -> 2%
where the time goes in v2:
time: 36.3 us; the launch traced here: 36 us
  blocking collectives  14 us (39%)
  starting transfers between devices  12.2 us (34%)
  Pallas kernels  4.24 us (12%)
  waiting for transfers between devices  3.92 us (11%)
  other arithmetic  0.85 us (2%)
  between operations  0.7 us (2%)
    all_to_all x1, blocking collectives, on_device(): blocks = lax.all_to_all(copies, ('gx', 'gy'), 0, 0)  14 us
    ppermute x1, starting transfers between devices, on_device(): lax.ppermute(slab, 'gz', up)  5.56 us
    ppermute x2, starting transfers between devices, summed(): lax.ppermute(total, axis, [(i, i ^ step) for i in range(count)])  5.38 us
    pallas_call x4, Pallas kernels, call(): pl.pallas_call(kernel, out_shape=outs, in_specs=[pl.BlockSpec(memory_spac...  4.24 us
    ppermute x2, waiting for transfers between devices, summed(): lax.ppermute(total, axis, [(i, i ^ step) for i in range(count)])  2.4 us
    ppermute x1, waiting for transfers between devices, on_device(): lax.ppermute(slab, 'gz', up)  1.51 us
    ppermute x1, starting transfers between devices, on_device(): lax.ppermute(slab, 'gz', down)  1.29 us
    concatenate x1, other arithmetic, on_device(): payload = jnp.concatenate([main, edges], axis=0)  0.84 us
  transfers between devices with their start and end apart: 4, of which 3 were waited for; matrix products, arithmetic and copies ran while one was open for 0% of the time, Pallas kernels for 2%

profile of v2, /device:TPU:0, one launch (start us, length us, event | category | flops | bytes accessed | tf_op | source)
XLA Modules:
  0.0 36.0 jit_solution(1845591178526443201)
XLA Ops:
  0.6 1.7 %shard_map.155 = (f32[16,8,128]{2,1,0:T(8,128)}, f32[1,8,128]{2,1,0:T(8,128)}, f32[15,4,128]{2,1,0:T(4,128)}) custom-call(f32[3,2,8,128]{3,2,1,0:T(8,128)} %new_hbm.1, f32[3,2,8,128]{3,2,1,0:T(8,128)} %old_hbm.1, f32[2,8,128]{2,1,0:T(8,128)} %energy_hbm.1, s32[2,8,128]{2,1,0:T(8,128)} %region_hbm.1, s32[2,8,128]{2,1,0:T(8,128)} %dirichlet_hbm.1, ...), custom_call_target="tpu_custom_call" | custom-call | bytes 174320 | tf_op jit(solution)/shard_map/pallas_call | solution.py:353
  2.3 0.0 copy-start.2
  2.3 1.3 %collective-permute-start.1 = (f32[1,8,128]{2,1,0:T(8,128)}, f32[1,8,128]{2,1,0:T(8,128)S(1)}, u32[]{:S(2)}, u32[]{:S(2)}) collective-permute-start(f32[1,8,128]{2,1,0:T(8,128)} %get-tuple-element.18), channel_id=1, source_target_pairs={{1,0},{2,1},{3,2},{5,4},{6,5},{7,6},{9,8},{10,9},{11,10},{13,12},{... | collective-permute-start | bytes 12296 | tf_op jit(solution)/shard_map/ppermute | solution.py:414
  3.6 5.6 %collective-permute-start = (f32[1,8,128]{2,1,0:T(8,128)}, f32[1,8,128]{2,1,0:T(8,128)S(1)}, u32[]{:S(2)}, u32[]{:S(2)}) collective-permute-start(f32[1,8,128]{2,1,0:T(8,128)} %get-tuple-element.18), channel_id=1, source_target_pairs={{0,1},{1,2},{2,3},{4,5},{5,6},{6,7},{8,9},{9,10},{10,11},{12,13},{... | collective-permute-start | bytes 12296 | tf_op jit(solution)/shard_map/ppermute | solution.py:414
  9.2 0.0 collective-permute-done.1
  9.2 1.5 %collective-permute-done = f32[1,8,128]{2,1,0:T(8,128)S(1)} collective-permute-done((f32[1,8,128]{2,1,0:T(8,128)}, f32[1,8,128]{2,1,0:T(8,128)S(1)}, u32[]{:S(2)}, u32[]{:S(2)}) %collective-permute-start) | collective-permute-done | bytes 4128 | tf_op jit(solution)/shard_map/ppermute | solution.py:414
  10.7 0.0 copy-done.2
  10.7 0.8 %pad_maximum_fusion = f32[17,8,128]{2,1,0:T(8,128)S(1)} fusion(f32[1,8,128]{2,1,0:T(8,128)S(1)} %broadcast_select_fusion, f32[16,8,128]{2,1,0:T(8,128)} %get-tuple-element.17), kind=kLoop, calls=%fused_computation | loop fusion | flops 17408 | bytes 139264 | tf_op jit(solution)/shard_map/concatenate | solution.py:416
  11.6 0.0 copy-start.1
  11.6 14.0 %all_to_all.5.blocks = f32[8,17,8,128]{3,2,1,0:T(8,128)S(1)} all-to-all(f32[8,17,8,128]{3,2,1,0:T(8,128)S(1)} %broadcast_in_dim.18), channel_id=1, replica_groups=mesh['gx'=4,'gy'=2,'gz'=4] {'gx','gy'}, dimensions={0} | all-to-all | bytes 1114112 | tf_op jit(solution)/shard_map/all_to_all | solution.py:419
  25.6 0.0 copy-done.1
  25.6 0.0 copy-start
  25.6 0.9 %shard_map.156 = (f32[5,2,8,128]{3,2,1,0:T(8,128)S(1)}, f32[6,2,8,128]{3,2,1,0:T(8,128)S(1)}, f32[16,128]{1,0:T(8,128)S(1)}) custom-call(f32[15,4,128]{2,1,0:T(4,128)S(1)} %copy-done.1, f32[8,17,8,128]{3,2,1,0:T(8,128)S(1)} %all_to_all.5.blocks), custom_call_target="tpu_custom_call" | custom-call | flops 8192000 | bytes 686080 | tf_op jit(solution)/shard_map/pallas_call | solution.py:353
  26.5 2.3 %collective-permute-start.2 = (f32[16,128]{1,0:T(8,128)S(1)}, f32[16,128]{1,0:T(8,128)S(1)}, u32[]{:S(2)}, u32[]{:S(2)}) collective-permute-start(f32[16,128]{1,0:T(8,128)S(1)} %get-tuple-element.23), channel_id=1, source_target_pairs={{0,1},{1,0},{2,3},{3,2},{4,5},{5,4},{6,7},{7,6},{8,9},{9,8},{10,11... | collective-permute-start | bytes 24584 | tf_op jit(solution)/shard_map/ppermute | solution.py:378
  28.8 1.6 %collective-permute-done.2 = f32[16,128]{1,0:T(8,128)S(1)} collective-permute-done((f32[16,128]{1,0:T(8,128)S(1)}, f32[16,128]{1,0:T(8,128)S(1)}, u32[]{:S(2)}, u32[]{:S(2)}) %collective-permute-start.2) | collective-permute-done | bytes 8224 | tf_op jit(solution)/shard_map/ppermute | solution.py:378
  30.5 3.0 %collective-permute-start.3 = (f32[16,128]{1,0:T(8,128)S(1)}, f32[16,128]{1,0:T(8,128)S(1)}, u32[]{:S(2)}, u32[]{:S(2)}) collective-permute-start(f32[16,128]{1,0:T(8,128)S(1)} %add.3), channel_id=1, source_target_pairs={{0,2},{1,3},{2,0},{3,1},{4,6},{5,7},{6,4},{7,5},{8,10},{9,11},{10,... | collective-permute-start | bytes 24584 | tf_op jit(solution)/shard_map/ppermute | solution.py:378
  33.5 0.0 copy-done
  33.5 0.9 %shard_map.157 = (f32[6,2,8,128]{3,2,1,0:T(8,128)}, f32[6,6,2,8,128]{4,3,2,1,0:T(8,128)}, f32[2,8,128]{2,1,0:T(8,128)}) custom-call(f32[15,4,128]{2,1,0:T(4,128)S(1)} %copy-done.1, f32[8,17,8,128]{3,2,1,0:T(8,128)S(1)} %all_to_all.5.blocks, f32[6,2,8,128]{3,2,1,0:T(8,128)S(1)} %get-tuple-element.19.dev_own, f32[6,6,2,8,128]{4,3,2,1,0:T(8,128)S(1)} %copy-done), custom_call_target="tpu_custom_call" | custom-call | flops 1024000 | bytes 1284096 | tf_op jit(solution)/shard_map/pallas_call | solution.py:353
  34.3 0.8 %collective-permute-done.3 = f32[16,128]{1,0:T(8,128)S(1)} collective-permute-done((f32[16,128]{1,0:T(8,128)S(1)}, f32[16,128]{1,0:T(8,128)S(1)}, u32[]{:S(2)}, u32[]{:S(2)}) %collective-permute-start.3) | collective-permute-done | bytes 8224 | tf_op jit(solution)/shard_map/ppermute | solution.py:378
  35.1 0.8 %shard_map.158 = (f32[2,8,128]{2,1,0:T(8,128)}, f32[2,8,128]{2,1,0:T(8,128)}) custom-call(f32[2,16,128]{2,1,0:T(8,128)S(1)} %pad_maximum_fusion.1.grams, f32[5,2,8,128]{3,2,1,0:T(8,128)S(1)} %get-tuple-element.24.basis), custom_call_target="tpu_custom_call" | custom-call | bytes 73728 | tf_op jit(solution)/shard_map/pallas_call | solution.py:353
  (4 shorter events, 0.0 us)
Async XLA Ops:
  2.3 8.4 %copy-start.2 = (pred[128]{0:T(512)(128)(4,1)S(1)}, pred[128]{0:T(512)(128)(4,1)}, u32[]{:S(2)}) copy-start(pred[128]{0:T(512)(128)(4,1)} %constant.9) | copy-start | bytes 388
  2.3 6.9 %collective-permute-start.1 = (f32[1,8,128]{2,1,0:T(8,128)}, f32[1,8,128]{2,1,0:T(8,128)S(1)}, u32[]{:S(2)}, u32[]{:S(2)}) collective-permute-start(f32[1,8,128]{2,1,0:T(8,128)} %get-tuple-element.18), channel_id=1, source_target_pairs={{1,0},{2,1},{3,2},{5,4},{6,5},{7,6},{9,8},{10,9},{11,10},{13,12},{... | collective-permute-start | bytes 12296 | tf_op jit(solution)/shard_map/ppermute | solution.py:414
  3.6 7.1 %collective-permute-start = (f32[1,8,128]{2,1,0:T(8,128)}, f32[1,8,128]{2,1,0:T(8,128)S(1)}, u32[]{:S(2)}, u32[]{:S(2)}) collective-permute-start(f32[1,8,128]{2,1,0:T(8,128)} %get-tuple-element.18), channel_id=1, source_target_pairs={{0,1},{1,2},{2,3},{4,5},{5,6},{6,7},{8,9},{9,10},{10,11},{12,13},{... | collective-permute-start | bytes 12296 | tf_op jit(solution)/shard_map/ppermute | solution.py:414
  11.6 14.0 %copy-start.1 = (f32[15,4,128]{2,1,0:T(4,128)S(1)}, f32[15,4,128]{2,1,0:T(4,128)}, u32[]{:S(2)}) copy-start(f32[15,4,128]{2,1,0:T(4,128)} %get-tuple-element.16.tables) | copy-start | bytes 92164
  25.6 7.9 %copy-start = (f32[6,6,2,8,128]{4,3,2,1,0:T(8,128)S(1)}, f32[6,6,2,8,128]{4,3,2,1,0:T(8,128)}, u32[]{:S(2)}) copy-start(f32[6,6,2,8,128]{4,3,2,1,0:T(8,128)} %visco.1) | copy-start | bytes 884740
  26.5 4.0 %collective-permute-start.2 = (f32[16,128]{1,0:T(8,128)S(1)}, f32[16,128]{1,0:T(8,128)S(1)}, u32[]{:S(2)}, u32[]{:S(2)}) collective-permute-start(f32[16,128]{1,0:T(8,128)S(1)} %get-tuple-element.23), channel_id=1, source_target_pairs={{0,1},{1,0},{2,3},{3,2},{4,5},{5,4},{6,7},{7,6},{8,9},{9,8},{10,11... | collective-permute-start | bytes 24584 | tf_op jit(solution)/shard_map/ppermute | solution.py:378
  30.5 4.7 %collective-permute-start.3 = (f32[16,128]{1,0:T(8,128)S(1)}, f32[16,128]{1,0:T(8,128)S(1)}, u32[]{:S(2)}, u32[]{:S(2)}) collective-permute-start(f32[16,128]{1,0:T(8,128)S(1)} %add.3), channel_id=1, source_target_pairs={{0,2},{1,3},{2,0},{3,1},{4,6},{5,7},{6,4},{7,5},{8,10},{9,11},{10,... | collective-permute-start | bytes 24584 | tf_op jit(solution)/shard_map/ppermute | solution.py:378

commit v3 on v2

--- a/solution.py
+++ b/solution.py
@@ -40,12 +40,17 @@
     def by(self):
         return self.gy if self.full else 2 * self.hops_y + 1
 
+    def beside(self, code, step, index_x):
+        if not self.full:
+            return (code + step) % self.bx
+        return (((index_x ^ code) + step) & (self.gx - 1)) ^ index_x
+
 
 def geometry(block):
     lx, ly, lz = block
     gx, gy, gz = (lax.axis_size(name) for name in ("gx", "gy", "gz"))
     hops_x, hops_y = -(-(ITERS + 1) // lx), -(-(ITERS + 1) // ly)
-    full = gx <= 2 * hops_x + 1 and gy <= hops_y + 1
+    full = gx <= 2 * hops_x + 1 and not gx & (gx - 1) and gy <= 2
     return Geometry(lx, ly, lz, gx, gy, gz, hops_x, hops_y, full)
 
 
@@ -165,30 +170,36 @@
     return 1.0 - lax.erf((energy_next - energy) / scale) / ratio
 
 
-def basis_kernel(geo, tables, blocks, basis, dev_own, grams, held, field, dev_all):
+def basis_kernel(geo, where, *refs):
+    tables, blocks = refs[0], refs[1:-5]
+    basis, dev_own, grams, held, field = refs[-5:]
     lx, ly, lz = geo.lx, geo.ly, geo.lz
     planes, rows, lanes = geo.bx * lx, geo.by * ly, 2 * lz
     regions = tables.shape[1]
     spots, _ = places(geo)
     row, lane = iota((rows, lanes), 0), iota((rows, lanes), 1)
-    index_y, index_z = lax.axis_index("gy"), lax.axis_index("gz")
+    index_x, index_y, index_z = (lax.axis_index(name) for name in ("gx", "gy", "gz"))
     if geo.full:
-        grid_row = row
-        own_x, own_y = lax.axis_index("gx") * lx, pl.multiple_of(index_y * ly, ly)
+        grid_row = jnp.where(row < ly, row + index_y * ly, row - index_y * ly)
     else:
         grid_row = index_y * ly + jnp.where(row < (1 + geo.hops_y) * ly, row, row - rows)
-        own_x, own_y = 0, 0
     end_y, start_y = grid_row == geo.gy * ly - 1, grid_row == 0
     end_z = (lane == lz - 1) & (index_z == geo.gz - 1)
     start_z = (lane == 0) & (index_z == 0)
+
+    def next_plane(p):
+        return p + 1 if p % lx + 1 < lx else geo.beside(p // lx, 1, index_x) * lx
+
+    def prev_plane(p):
+        return p - 1 if p % lx else geo.beside(p // lx, -1, index_x) * lx + lx - 1
 
     def whole_plane(f, p):
         tile, centre = spots[f * lx + p % lx]
         parts = []
         for b in range(geo.by):
-            at = (p // lx) * geo.by + b
-            edge = pltpu.roll(blocks[at, FIELDS * lx + tile], lz - centre, 1)
-            parts.append(jnp.concatenate([blocks[at, f * lx + p % lx], edge], axis=1))
+            array, at = where[p // lx, b]
+            edge = pltpu.roll(blocks[array][at, FIELDS * lx + tile], lz - centre, 1)
+            parts.append(jnp.concatenate([blocks[array][at, f * lx + p % lx], edge], axis=1))
         return jnp.concatenate(parts, axis=0)
 
     def beside(value):
@@ -205,11 +216,12 @@
         grad = []
         for a in range(3):
             next_y, prev_y, next_z, prev_z = beside(held[a, p])
-            next_x, prev_x = held[a, (p + 1) % planes], held[a, (p - 1) % planes]
+            next_x, prev_x = held[a, next_plane(p)], held[a, prev_plane(p)]
             grad.append([0.5 * (next_x - prev_x), 0.5 * (next_y - prev_y), 0.5 * (next_z - prev_z)])
         dev = deviator(grad)
-        for k in range(6):
-            dev_all[k, p] = dev[k][:, :lz]
+        if p < lx:
+            for k in range(6):
+                dev_own[k, p] = dev[k][:ly, :lz]
         label = whole_plane(4, p)
         halves = []
         for half in (slice(0, lz), slice(lz, lanes)):
@@ -224,7 +236,7 @@
         for p in range(planes):
             value = field[j, p]
             next_y, prev_y, next_z, prev_z = beside(value)
-            next_x, prev_x = field[j, (p + 1) % planes], field[j, (p - 1) % planes]
+            next_x, prev_x = field[j, next_plane(p)], field[j, prev_plane(p)]
             image = (value - next_x) + (value - prev_x)
             image += (value - next_y) + (value - prev_y)
             image += (value - next_z) + (value - prev_z)
@@ -240,48 +252,57 @@
         grams[k : k + 1, :] = jnp.sum(total, axis=0, keepdims=True)
     for i in range(lx):
         for j in range(ITERS + 1):
-            basis[j, i] = field[j, own_x + i, pl.ds(own_y, ly), :lz]
-        for k in range(6):
-            dev_own[k, i] = dev_all[k, own_x + i, pl.ds(own_y, ly), :]
-
-
-def visco_kernel(
-    geo, tables, blocks, dev_own, visco, stress, visco_next, energy_next
-):
+            basis[j, i] = field[j, i, :ly, :lz]
+
+
+def visco_kernel(geo, where, *refs):
+    tables, dev_own, visco, blocks = refs[0], refs[1], refs[2], refs[3:-3]
+    stress, visco_next, energy_next = refs[-3:]
     lx, ly, lz = geo.lx, geo.ly, geo.lz
     spots, _ = places(geo)
     row, lane = iota((ly, lz), 0), iota((ly, lz), 1)
-    index_y = lax.axis_index("gy")
-    own_x, own_y = (lax.axis_index("gx"), index_y) if geo.full else (0, 0)
-
-    def block(step_x, step_y):
-        return lax.rem(own_x + step_x + geo.bx, geo.bx) * geo.by + lax.rem(own_y + step_y + geo.by, geo.by)
-
-    here, right, left, above, below = block(0, 0), block(1, 0), block(-1, 0), block(0, 1), block(0, -1)
+    index_x, index_y = lax.axis_index("gx"), lax.axis_index("gy")
     regions, terms = tables.shape[1], visco.shape[0]
+
+    def own(at, code_y=0):
+        array, place = where[0, code_y % geo.by]
+        return blocks[array][place, at]
+
+    def along_x(step, at):
+        target = geo.beside(0, step, index_x)
+        if not geo.full:
+            array, place = where[target, 0]
+            return blocks[array][place, at]
+        value = None
+        for code in {geo.beside(0, step, index) for index in range(geo.gx)}:
+            array, place = where[code, 0]
+            found = blocks[array][place, at]
+            value = found if value is None else jnp.where(target == code, found, value)
+        return value
+
     for i in range(lx):
         grad = []
         for a in range(3):
             at = (WIDE + a) * lx + i
-            value = blocks[here, at]
-            next_x = blocks[here, at + 1] if i + 1 < lx else blocks[right, at + 1 - lx]
-            prev_x = blocks[here, at - 1] if i else blocks[left, at + lx - 1]
-            first = jnp.where(index_y == geo.gy - 1, 0.0, blocks[above, at])
-            last = jnp.where(index_y == 0, 0.0, blocks[below, at])
+            value = own(at)
+            next_x = own(at + 1) if i + 1 < lx else along_x(1, at + 1 - lx)
+            prev_x = own(at - 1) if i else along_x(-1, at + lx - 1)
+            first = jnp.where(index_y == geo.gy - 1, 0.0, own(at, 1))
+            last = jnp.where(index_y == 0, 0.0, own(at, -1))
             next_y = pltpu.roll(jnp.where(row == 0, first, value), ly - 1, 0)
             prev_y = pltpu.roll(jnp.where(row == ly - 1, last, value), 1, 0)
             tile, centre = spots[at]
-            edge = blocks[here, FIELDS * lx + tile]
+            edge = own(FIELDS * lx + tile)
             next_z = jnp.where(lane == lz - 1, pltpu.roll(edge, lz - 1 - centre, 1), pltpu.roll(value, lz - 1, 1))
             prev_z = jnp.where(lane == 0, pltpu.roll(edge, lz + 1 - centre, 1), pltpu.roll(value, 1, 1))
             grad.append([0.5 * (next_x - prev_x), 0.5 * (next_y - prev_y), 0.5 * (next_z - prev_z)])
         dev_old = deviator(grad)
         dev_new = [dev_own[k, i] for k in range(6)]
-        label = blocks[here, 4 * lx + i]
+        label = own(4 * lx + i)
         masks = [label == r for r in range(regions - 1)]
         shear_cells, ratio_cells, scale_cells = [lookup(tables, entry, masks) for entry in (SHEAR, RATIO, SCALE)]
         energy = shear_cells * contract(dev_new)
-        energy_after = jnp.maximum(blocks[here, 3 * lx + i], energy)
+        energy_after = jnp.maximum(own(3 * lx + i), energy)
         energy_next[i] = energy_after
         softening = soften(energy, energy_after, scale_cells, ratio_cells)
         jump = [2.0 * shear_cells * (dev_new[k] - dev_old[k]) for k in range(6)]
@@ -300,10 +321,9 @@
             stress[k, i] = softening * (long_term * 2.0 * shear_cells * dev_new[k] + totals[k])
 
 
-def solve_kernel(geo, grams, basis, damage, residual):
-    total = grams[0]
-    for n in range(1, grams.shape[0]):
-        total = total + grams[n]
+def solve_kernel(geo, basis, *refs):
+    grams, damage, residual = refs[:-2], refs[-2], refs[-1]
+    total = functools.reduce(jnp.add, [part[...] for part in grams])
     column = jnp.sum(total, axis=1, keepdims=True)
     gram = {}
     for k, (i, j) in enumerate(PAIRS):
@@ -361,23 +381,38 @@
     )(*arrays)
 
 
+def moved(shard, axis, target):
+    return lax.ppermute(shard, axis, [(i, target(i)) for i in range(lax.axis_size(axis))])
+
+
 def ring(shard, axis, hops):
     count = lax.axis_size(axis)
     steps = list(range(hops + 1)) + list(range(-hops, 0))
-    moved = [lax.ppermute(shard, axis, [((i + step) % count, i) for i in range(count)]) if step else shard for step in steps]
-    return jnp.stack(moved)
+    return jnp.stack([moved(shard, axis, lambda i: (i - step) % count) if step else shard for step in steps])
+
+
+def gathered(payload, geo):
+    if not geo.full:
+        blocks = ring(ring(payload, "gy", geo.hops_y), "gx", geo.hops_x)
+        where = {(x, y): (0, x * geo.by + y) for x in range(geo.bx) for y in range(geo.by)}
+        return [blocks.reshape((geo.bx * geo.by,) + payload.shape)], where
+    steps = [("gy", 0, 1)] * (geo.gy - 1)
+    steps += [("gx", 1 << bit, 0) for bit in reversed(range(geo.gx.bit_length() - 1))]
+    arrays, codes = [payload[None]], [[(0, 0)]]
+    for axis, step_x, step_y in steps:
+        if len(arrays) == 2:
+            arrays, codes = [jnp.concatenate(arrays, axis=0)], [codes[0] + codes[1]]
+        arrays.append(moved(arrays[0], axis, lambda i: i ^ (step_x + step_y)))
+        codes.append([(x ^ step_x, y ^ step_y) for x, y in codes[0]])
+    where = {code: (n, place) for n, held in enumerate(codes) for place, code in enumerate(held)}
+    return arrays, where
 
 
 def summed(terms, axis):
     count = lax.axis_size(axis)
-    if count & (count - 1):
-        return lax.psum(terms, axis)[None]
-    step, parts = 1, [terms]
-    while step < count:
-        total = functools.reduce(jnp.add, parts)
-        parts = [total, lax.ppermute(total, axis, [(i, i ^ step) for i in range(count)])]
-        step *= 2
-    return jnp.stack(parts)
+    if count > 4:
+        return [lax.psum(terms, axis)]
+    return [terms] + [moved(terms, axis, lambda i: (i + step) % count) for step in range(1, count)]
 
 
 def on_device(
@@ -406,46 +441,39 @@
         [pltpu.VMEM(a.shape, a.dtype) for a in arguments]
         + [pltpu.SMEM(a.shape, a.dtype) for a in parameters]
         + [pltpu.SemaphoreType.DMA((len(arguments) + len(parameters),))],
-        space=pl.ANY,
-        vmem=56 * MB,
+        space=pltpu.HBM,
     )
     up = [(i, i + 1) for i in range(geo.gz - 1)]
     down = [(j, i) for i, j in up]
     from_left, from_right = lax.ppermute(slab, "gz", up), lax.ppermute(slab, "gz", down)
     edges = jnp.where(left_lanes(geo), from_left, from_right)
     payload = jnp.concatenate([main, edges], axis=0)
-    if geo.full:
-        copies = jnp.broadcast_to(payload[None], (geo.gx * geo.gy,) + payload.shape)
-        blocks = lax.all_to_all(copies, ("gx", "gy"), 0, 0)
-    else:
-        blocks = ring(ring(payload, "gy", geo.hops_y), "gx", geo.hops_x)
-        blocks = blocks.reshape((geo.bx * geo.by,) + payload.shape)
+    blocks, where = gathered(payload, geo)
     planes, rows = geo.bx * lx, geo.by * ly
     basis, dev_own, grams = call(
-        functools.partial(basis_kernel, geo),
+        functools.partial(basis_kernel, geo, where),
         [shaped(ITERS + 1, lx, ly, lz), shaped(6, lx, ly, lz), shaped(-(-len(PAIRS) // 8) * 8, lz)],
-        [tables, blocks],
+        [tables, *blocks],
         [
             pltpu.VMEM((3, planes, rows, 2 * lz), jnp.float32),
             pltpu.VMEM((ITERS + 1, planes, rows, 2 * lz), jnp.float32),
-            pltpu.VMEM((6, planes, rows, lz), jnp.float32),
         ],
         flops=planes * rows * lz * 500,
     )
     if geo.full:
         sums = summed(grams, "gz")
     else:
-        sums = lax.psum(grams, ("gx", "gy", "gz"))[None]
+        sums = [lax.psum(grams, ("gx", "gy", "gz"))]
     stress, visco_next, energy_next = call(
-        functools.partial(visco_kernel, geo),
+        functools.partial(visco_kernel, geo, where),
         [shaped(6, lx, ly, lz), shaped(*visco_state.shape), shaped(lx, ly, lz)],
-        [tables, blocks, dev_own, visco_state],
+        [tables, dev_own, visco_state, *blocks],
         flops=lx * ly * lz * 500,
     )
     damage_field, residual = call(
         functools.partial(solve_kernel, geo),
         [shaped(lx, ly, lz), shaped(lx, ly, lz)],
-        [sums, basis],
+        [basis, *sums],
     )
     return (stress, visco_next, energy_next, damage_field, residual)
 

time: 36.3 us -> 39.2 us (1.080)
  blocking collectives: 14 us -> 0 us
  waiting for transfers between devices: 3.92 us -> 12.6 us
  local copies, waits for them, and re-layouts: 0.05 us -> 6.89 us
  starting transfers between devices: 12.2 us -> 15 us
  other arithmetic: 0.85 us -> 0.06 us
  Pallas kernels: 4.24 us -> 3.46 us
    all_to_all x1 -> x0, blocking collectives: 14 us -> none  [on_device(): blocks = lax.all_to_all(copies, ('gx', 'gy'), 0, 0)]
    unnamed x6 -> x24, local copies, waits for them, and re-layouts: 0.02 us -> 6.89 us
    ppermute x2 -> x6, waiting for transfers between devices: 2.4 us -> 8.42 us  [moved(): lax.ppermute(shard, axis, [(i, target(i)) for i in range(lax.axis_size(ax...]
    ppermute x1, waiting for transfers between devices: 0.01 us -> 4.19 us  [on_device(): lax.ppermute(slab, 'gz', down)]
    ppermute x2 -> x6, starting transfers between devices: 5.38 us -> 8.78 us  [moved(): lax.ppermute(shard, axis, [(i, target(i)) for i in range(lax.axis_size(ax...]
    ppermute x1, waiting for transfers between devices: 1.51 us -> 0.01 us  [on_device(): lax.ppermute(slab, 'gz', up)]
    concatenate x1 -> x2, other arithmetic: 0.84 us -> 0.04 us  [gathered(): arrays, codes = ([jnp.concatenate(arrays, axis=0)], [codes[0] + codes[1]])]
    pallas_call x4, Pallas kernels: 4.24 us -> 3.46 us  [call(): pl.pallas_call(kernel, out_shape=outs, in_specs=[pl.BlockSpec(memory_spac...]
  transfers between devices with their start and end apart: 4 -> 8, of which waited for: 3 -> 5; matrix products, arithmetic and copies ran while one was open for 0% -> 0% of each run, Pallas kernels for 2% -> 2%
where the time goes in v3:
time: 39.2 us; the launch traced here: 38.7 us
  starting transfers between devices  15 us (38%)
  waiting for transfers between devices  12.6 us (32%)
  local copies, waits for them, and re-layouts  6.89 us (18%)
  Pallas kernels  3.46 us (9%)
  between operations  0.71 us (2%)
    ppermute x6, starting transfers between devices, moved(): lax.ppermute(shard, axis, [(i, target(i)) for i in range(lax.axis_size(ax...  8.78 us
    ppermute x6, waiting for transfers between devices, moved(): lax.ppermute(shard, axis, [(i, target(i)) for i in range(lax.axis_size(ax...  8.42 us
    unnamed x24, local copies, waits for them, and re-layouts  6.89 us
    ppermute x1, starting transfers between devices, on_device(): lax.ppermute(slab, 'gz', up)  4.93 us
    ppermute x1, waiting for transfers between devices, on_device(): lax.ppermute(slab, 'gz', down)  4.19 us
    pallas_call x4, Pallas kernels, call(): pl.pallas_call(kernel, out_shape=outs, in_specs=[pl.BlockSpec(memory_spac...  3.46 us
    ppermute x1, starting transfers between devices, on_device(): lax.ppermute(slab, 'gz', down)  1.29 us
  transfers between devices with their start and end apart: 8, of which 5 were waited for; matrix products, arithmetic and copies ran while one was open for 0% of the time, Pallas kernels for 2%

profile of v3, /device:TPU:0, one launch (start us, length us, event | category | flops | bytes accessed | tf_op | source)
XLA Modules:
  0.0 38.7 jit_solution(13479934873226459376)
XLA Ops:
  0.6 0.7 %copy-done.1 = f32[3,2,8,128]{3,2,1,0:T(8,128)S(1)} copy-done((f32[3,2,8,128]{3,2,1,0:T(8,128)S(1)}, f32[3,2,8,128]{3,2,1,0:T(8,128)}, u32[]{:S(2)}) %copy-start.1) | copy-done | bytes 24600
  1.4 0.7 %copy-done.2 = f32[3,2,8,128]{3,2,1,0:T(8,128)S(1)} copy-done((f32[3,2,8,128]{3,2,1,0:T(8,128)S(1)}, f32[3,2,8,128]{3,2,1,0:T(8,128)}, u32[]{:S(2)}) %copy-start.2) | copy-done | bytes 24600
  2.1 0.7 %copy-done.3 = f32[2,8,128]{2,1,0:T(8,128)S(1)} copy-done((f32[2,8,128]{2,1,0:T(8,128)S(1)}, f32[2,8,128]{2,1,0:T(8,128)}, u32[]{:S(2)}) %copy-start.3) | copy-done | bytes 8216
  2.8 0.7 %copy-done.4 = s32[2,8,128]{2,1,0:T(8,128)S(1)} copy-done((s32[2,8,128]{2,1,0:T(8,128)S(1)}, s32[2,8,128]{2,1,0:T(8,128)}, u32[]{:S(2)}) %copy-start.4) | copy-done | bytes 8216
  3.5 0.7 %copy-done.5 = s32[2,8,128]{2,1,0:T(8,128)S(1)} copy-done((s32[2,8,128]{2,1,0:T(8,128)S(1)}, s32[2,8,128]{2,1,0:T(8,128)}, u32[]{:S(2)}) %copy-start.5) | copy-done | bytes 8216
  4.2 0.7 %copy-done.6 = f32[4,6]{1,0:T(4,128)S(1)} copy-done((f32[4,6]{1,0:T(4,128)S(1)}, f32[4,6]{1,0:T(4,128)}, u32[]{:S(2)}) %copy-start.6) | copy-done | bytes 120
  4.9 0.7 %copy-done.7 = f32[4,6]{1,0:T(4,128)S(1)} copy-done((f32[4,6]{1,0:T(4,128)S(1)}, f32[4,6]{1,0:T(4,128)}, u32[]{:S(2)}) %copy-start.7) | copy-done | bytes 120
  5.6 0.7 %copy-done.8 = f32[4]{0:T(128)S(1)} copy-done((f32[4]{0:T(128)S(1)}, f32[4]{0:T(128)}, u32[]{:S(2)}) %copy-start.8) | copy-done | bytes 40
  6.2 0.7 %copy-done.9 = f32[4]{0:T(128)S(1)} copy-done((f32[4]{0:T(128)S(1)}, f32[4]{0:T(128)}, u32[]{:S(2)}) %copy-start.9) | copy-done | bytes 40
  7.5 0.9 %shard_map.155 = (f32[16,8,128]{2,1,0:T(8,128)S(1)}, f32[1,8,128]{2,1,0:T(8,128)S(1)}, f32[15,4,128]{2,1,0:T(4,128)S(1)}) custom-call(f32[3,2,8,128]{3,2,1,0:T(8,128)S(1)} %copy-done.1, f32[3,2,8,128]{3,2,1,0:T(8,128)S(1)} %copy-done.2, f32[2,8,128]{2,1,0:T(8,128)S(1)} %copy-done.3, s32[2,8,128]{2,1,0:T(8,128)S(1)} %copy-done.4, s32[2,8,128]{2,1,0:T(8,128)S(1)} %copy-done.5, ...), custom_call_target="tpu_custom_call" | custom-call | bytes 174320 | tf_op jit(solution)/shard_map/pallas_call | solution.py:373
  8.4 4.9 %collective-permute-start = (f32[1,8,128]{2,1,0:T(8,128)S(1)}, f32[1,8,128]{2,1,0:T(8,128)S(1)}, u32[]{:S(2)}, u32[]{:S(2)}) collective-permute-start(f32[1,8,128]{2,1,0:T(8,128)S(1)} %get-tuple-element.18), channel_id=1, source_target_pairs={{0,1},{1,2},{2,3},{4,5},{5,6},{6,7},{8,9},{9,10},{10,11},{12,13},{... | collective-permute-start | bytes 12296 | tf_op jit(solution)/shard_map/ppermute | solution.py:448
  13.3 1.3 %collective-permute-start.1 = (f32[1,8,128]{2,1,0:T(8,128)S(1)}, f32[1,8,128]{2,1,0:T(8,128)S(1)}, u32[]{:S(2)}, u32[]{:S(2)}) collective-permute-start(f32[1,8,128]{2,1,0:T(8,128)S(1)} %get-tuple-element.18), channel_id=1, source_target_pairs={{1,0},{2,1},{3,2},{5,4},{6,5},{7,6},{9,8},{10,9},{11,10},{13,12},{... | collective-permute-start | bytes 12296 | tf_op jit(solution)/shard_map/ppermute | solution.py:448
  14.7 4.2 %collective-permute-done.1 = f32[1,8,128]{2,1,0:T(8,128)S(1)} collective-permute-done((f32[1,8,128]{2,1,0:T(8,128)S(1)}, f32[1,8,128]{2,1,0:T(8,128)S(1)}, u32[]{:S(2)}, u32[]{:S(2)}) %collective-permute-start.1) | collective-permute-done | bytes 4128 | tf_op jit(solution)/shard_map/ppermute | solution.py:448
  18.9 1.6 %collective-permute-start.2 = (f32[1,17,8,128]{3,2,1,0:T(8,128)S(1)}, f32[1,17,8,128]{3,2,1,0:T(8,128)S(1)}, u32[]{:S(2)}, u32[]{:S(2)}) collective-permute-start(f32[1,17,8,128]{3,2,1,0:T(8,128)S(1)} %maximum_bitcast_fusion), channel_id=1, source_target_pairs={{0,4},{4,0},{1,5},{5,1},{2,6},{6,2},{3,7},{7,3},{8,12},{12,8},{9,1... | collective-permute-start | bytes 208904 | tf_op jit(solution)/shard_map/ppermute | solution.py:385
  20.4 2.8 %collective-permute-done.2 = f32[1,17,8,128]{3,2,1,0:T(8,128)S(1)} collective-permute-done((f32[1,17,8,128]{3,2,1,0:T(8,128)S(1)}, f32[1,17,8,128]{3,2,1,0:T(8,128)S(1)}, u32[]{:S(2)}, u32[]{:S(2)}) %collective-permute-start.2) | collective-permute-done | bytes 69664 | tf_op jit(solution)/shard_map/ppermute | solution.py:385
  23.3 1.6 %collective-permute-start.3 = (f32[2,17,8,128]{3,2,1,0:T(8,128)S(1)}, f32[2,17,8,128]{3,2,1,0:T(8,128)S(1)}, u32[]{:S(2)}, u32[]{:S(2)}) collective-permute-start(f32[2,17,8,128]{3,2,1,0:T(8,128)S(1)} %pad_maximum_fusion.1), channel_id=1, source_target_pairs={{0,16},{8,24},{16,0},{24,8},{1,17},{9,25},{17,1},{25,9},{2,18},{10... | collective-permute-start | bytes 417800 | tf_op jit(solution)/shard_map/ppermute | solution.py:385
  24.8 3.5 %collective-permute-done.3 = f32[2,17,8,128]{3,2,1,0:T(8,128)S(1)} collective-permute-done((f32[2,17,8,128]{3,2,1,0:T(8,128)S(1)}, f32[2,17,8,128]{3,2,1,0:T(8,128)S(1)}, u32[]{:S(2)}, u32[]{:S(2)}) %collective-permute-start.3) | collective-permute-done | bytes 139296 | tf_op jit(solution)/shard_map/ppermute | solution.py:385
  28.5 1.5 %collective-permute-done.4.refs_2_.refs_4_ = f32[4,17,8,128]{3,2,1,0:T(8,128)S(1)} collective-permute-done((f32[4,17,8,128]{3,2,1,0:T(8,128)S(1)}, f32[4,17,8,128]{3,2,1,0:T(8,128)S(1)}, u32[]{:S(2)}, u32[]{:S(2)}) %collective-permute-start.4) | collective-permute-done | bytes 278560 | tf_op jit(solution)/shard_map/ppermute | solution.py:385
  30.0 0.9 %shard_map.156 = (f32[5,2,8,128]{3,2,1,0:T(8,128)S(1)}, f32[6,2,8,128]{3,2,1,0:T(8,128)S(1)}, f32[16,128]{1,0:T(8,128)S(1)}) custom-call(f32[15,4,128]{2,1,0:T(4,128)S(1)} %get-tuple-element.16.refs_0_, f32[4,17,8,128]{3,2,1,0:T(8,128)S(1)} %pad_maximum_fusion.refs_1_.refs_3_, f32[4,17,8,128]{3,2,1,0:T(8,128)S(1)} %collective-permute-done.4.refs_2_.refs_4_), custom_call_target="tpu_custom_call" | custom-call | flops 8192000 | bytes 686080 | tf_op jit(solution)/shard_map/pallas_call | solution.py:373
  31.0 1.6 %collective-permute-start.5 = (f32[16,128]{1,0:T(8,128)S(1)}, f32[16,128]{1,0:T(8,128)S(1)}, u32[]{:S(2)}, u32[]{:S(2)}) collective-permute-start(f32[16,128]{1,0:T(8,128)S(1)} %get-tuple-element.24.refs_0_), channel_id=1, source_target_pairs={{0,1},{1,2},{2,3},{3,0},{4,5},{5,6},{6,7},{7,4},{8,9},{9,10},{10,1... | collective-permute-start | bytes 24584 | tf_op jit(solution)/shard_map/ppermute | solution.py:385
  32.6 1.1 %collective-permute-start.6 = (f32[16,128]{1,0:T(8,128)S(1)}, f32[16,128]{1,0:T(8,128)S(1)}, u32[]{:S(2)}, u32[]{:S(2)}) collective-permute-start(f32[16,128]{1,0:T(8,128)S(1)} %get-tuple-element.24.refs_0_), channel_id=1, source_target_pairs={{0,2},{1,3},{2,0},{3,1},{4,6},{5,7},{6,4},{7,5},{8,10},{9,11},{10,... | collective-permute-start | bytes 24584 | tf_op jit(solution)/shard_map/ppermute | solution.py:385
  33.7 2.8 %collective-permute-start.7 = (f32[16,128]{1,0:T(8,128)S(1)}, f32[16,128]{1,0:T(8,128)S(1)}, u32[]{:S(2)}, u32[]{:S(2)}) collective-permute-start(f32[16,128]{1,0:T(8,128)S(1)} %get-tuple-element.24.refs_0_), channel_id=1, source_target_pairs={{0,3},{1,0},{2,1},{3,2},{4,7},{5,4},{6,5},{7,6},{8,11},{9,8},{10,9... | collective-permute-start | bytes 24584 | tf_op jit(solution)/shard_map/ppermute | solution.py:385
  36.5 0.8 %shard_map.157 = (f32[6,2,8,128]{3,2,1,0:T(8,128)}, f32[6,6,2,8,128]{4,3,2,1,0:T(8,128)}, f32[2,8,128]{2,1,0:T(8,128)}) custom-call(f32[15,4,128]{2,1,0:T(4,128)S(1)} %get-tuple-element.16.refs_0_, f32[6,2,8,128]{3,2,1,0:T(8,128)S(1)} %get-tuple-element.19.refs_1_, f32[6,6,2,8,128]{4,3,2,1,0:T(8,128)S(1)} %copy-done, ...), custom_call_target="tpu_custom_call" | custom-call | flops 1024000 | bytes 1284096 | tf_op jit(solution)/shard_map/pallas_call | solution.py:373
  37.9 0.8 %shard_map.158 = (f32[2,8,128]{2,1,0:T(8,128)}, f32[2,8,128]{2,1,0:T(8,128)}) custom-call(f32[5,2,8,128]{3,2,1,0:T(8,128)S(1)} %get-tuple-element.23.basis, f32[16,128]{1,0:T(8,128)S(1)} %get-tuple-element.24.refs_0_, f32[16,128]{1,0:T(8,128)S(1)} %collective-permute-done.5.refs_1_, f32[16,128]{1,0:T(8,128)S(1)} %collective-permute-done.6.refs_2_, ...), custom_call_target="tpu_custom_call" | custom-call | bytes 90112 | tf_op jit(solution)/shard_map/pallas_call | solution.py:373
  (24 shorter events, 1.3 us)
Async XLA Ops:
  0.6 0.7 %copy-start.1 = (f32[3,2,8,128]{3,2,1,0:T(8,128)S(1)}, f32[3,2,8,128]{3,2,1,0:T(8,128)}, u32[]{:S(2)}) copy-start(f32[3,2,8,128]{3,2,1,0:T(8,128)} %new_hbm.1) | copy-start | bytes 73732
  1.4 0.7 %copy-start.2 = (f32[3,2,8,128]{3,2,1,0:T(8,128)S(1)}, f32[3,2,8,128]{3,2,1,0:T(8,128)}, u32[]{:S(2)}) copy-start(f32[3,2,8,128]{3,2,1,0:T(8,128)} %old_hbm.1) | copy-start | bytes 73732
  2.1 0.7 %copy-start.3 = (f32[2,8,128]{2,1,0:T(8,128)S(1)}, f32[2,8,128]{2,1,0:T(8,128)}, u32[]{:S(2)}) copy-start(f32[2,8,128]{2,1,0:T(8,128)} %energy_hbm.1) | copy-start | bytes 24580
  2.8 0.7 %copy-start.4 = (s32[2,8,128]{2,1,0:T(8,128)S(1)}, s32[2,8,128]{2,1,0:T(8,128)}, u32[]{:S(2)}) copy-start(s32[2,8,128]{2,1,0:T(8,128)} %region_hbm.1) | copy-start | bytes 24580
  3.5 0.7 %copy-start.5 = (s32[2,8,128]{2,1,0:T(8,128)S(1)}, s32[2,8,128]{2,1,0:T(8,128)}, u32[]{:S(2)}) copy-start(s32[2,8,128]{2,1,0:T(8,128)} %dirichlet_hbm.1) | copy-start | bytes 24580
  4.2 0.7 %copy-start.6 = (f32[4,6]{1,0:T(4,128)S(1)}, f32[4,6]{1,0:T(4,128)}, u32[]{:S(2)}) copy-start(f32[4,6]{1,0:T(4,128)} %moduli_hbm.1) | copy-start | bytes 292
  4.9 0.7 %copy-start.7 = (f32[4,6]{1,0:T(4,128)S(1)}, f32[4,6]{1,0:T(4,128)}, u32[]{:S(2)}) copy-start(f32[4,6]{1,0:T(4,128)} %times_hbm.1) | copy-start | bytes 292
  5.6 0.7 %copy-start.8 = (f32[4]{0:T(128)S(1)}, f32[4]{0:T(128)}, u32[]{:S(2)}) copy-start(f32[4]{0:T(128)} %shear_hbm.1) | copy-start | bytes 52
  6.2 0.7 %copy-start.9 = (f32[4]{0:T(128)S(1)}, f32[4]{0:T(128)}, u32[]{:S(2)}) copy-start(f32[4]{0:T(128)} %ratio_hbm.1) | copy-start | bytes 52
  6.9 0.7 %copy-start.10 = (f32[4]{0:T(128)S(1)}, f32[4]{0:T(128)}, u32[]{:S(2)}) copy-start(f32[4]{0:T(128)} %scale_hbm.1) | copy-start | bytes 52
  8.4 10.5 %copy-start.11 = (pred[128]{0:T(512)(128)(4,1)S(1)}, pred[128]{0:T(512)(128)(4,1)}, u32[]{:S(2)}) copy-start(pred[128]{0:T(512)(128)(4,1)} %constant.9) | copy-start | bytes 388
  8.4 6.2 %collective-permute-start = (f32[1,8,128]{2,1,0:T(8,128)S(1)}, f32[1,8,128]{2,1,0:T(8,128)S(1)}, u32[]{:S(2)}, u32[]{:S(2)}) collective-permute-start(f32[1,8,128]{2,1,0:T(8,128)S(1)} %get-tuple-element.18), channel_id=1, source_target_pairs={{0,1},{1,2},{2,3},{4,5},{5,6},{6,7},{8,9},{9,10},{10,11},{12,13},{... | collective-permute-start | bytes 12296 | tf_op jit(solution)/shard_map/ppermute | solution.py:448
  13.3 5.5 %collective-permute-start.1 = (f32[1,8,128]{2,1,0:T(8,128)S(1)}, f32[1,8,128]{2,1,0:T(8,128)S(1)}, u32[]{:S(2)}, u32[]{:S(2)}) collective-permute-start(f32[1,8,128]{2,1,0:T(8,128)S(1)} %get-tuple-element.18), channel_id=1, source_target_pairs={{1,0},{2,1},{3,2},{5,4},{6,5},{7,6},{9,8},{10,9},{11,10},{13,12},{... | collective-permute-start | bytes 12296 | tf_op jit(solution)/shard_map/ppermute | solution.py:448
  18.9 4.4 %collective-permute-start.2 = (f32[1,17,8,128]{3,2,1,0:T(8,128)S(1)}, f32[1,17,8,128]{3,2,1,0:T(8,128)S(1)}, u32[]{:S(2)}, u32[]{:S(2)}) collective-permute-start(f32[1,17,8,128]{3,2,1,0:T(8,128)S(1)} %maximum_bitcast_fusion), channel_id=1, source_target_pairs={{0,4},{4,0},{1,5},{5,1},{2,6},{6,2},{3,7},{7,3},{8,12},{12,8},{9,1... | collective-permute-start | bytes 208904 | tf_op jit(solution)/shard_map/ppermute | solution.py:385
  23.3 5.1 %collective-permute-start.3 = (f32[2,17,8,128]{3,2,1,0:T(8,128)S(1)}, f32[2,17,8,128]{3,2,1,0:T(8,128)S(1)}, u32[]{:S(2)}, u32[]{:S(2)}) collective-permute-start(f32[2,17,8,128]{3,2,1,0:T(8,128)S(1)} %pad_maximum_fusion.1), channel_id=1, source_target_pairs={{0,16},{8,24},{16,0},{24,8},{1,17},{9,25},{17,1},{25,9},{2,18},{10... | collective-permute-start | bytes 417800 | tf_op jit(solution)/shard_map/ppermute | solution.py:385
  28.4 1.6 %collective-permute-start.4 = (f32[4,17,8,128]{3,2,1,0:T(8,128)S(1)}, f32[4,17,8,128]{3,2,1,0:T(8,128)S(1)}, u32[]{:S(2)}, u32[]{:S(2)}) collective-permute-start(f32[4,17,8,128]{3,2,1,0:T(8,128)S(1)} %pad_maximum_fusion.refs_1_.refs_3_), channel_id=1, source_target_pairs={{0,8},{8,0},{16,24},{24,16},{1,9},{9,1},{17,25},{25,17},{2,10},{10... | collective-permute-start | bytes 835592 | tf_op jit(solution)/shard_map/ppermute | solution.py:385
  30.0 6.5 %copy-start = (f32[6,6,2,8,128]{4,3,2,1,0:T(8,128)S(1)}, f32[6,6,2,8,128]{4,3,2,1,0:T(8,128)}, u32[]{:S(2)}) copy-start(f32[6,6,2,8,128]{4,3,2,1,0:T(8,128)} %refs_2_.1) | copy-start | bytes 884740
  31.0 6.4 %collective-permute-start.5 = (f32[16,128]{1,0:T(8,128)S(1)}, f32[16,128]{1,0:T(8,128)S(1)}, u32[]{:S(2)}, u32[]{:S(2)}) collective-permute-start(f32[16,128]{1,0:T(8,128)S(1)} %get-tuple-element.24.refs_0_), channel_id=1, source_target_pairs={{0,1},{1,2},{2,3},{3,0},{4,5},{5,6},{6,7},{7,4},{8,9},{9,10},{10,1... | collective-permute-start | bytes 24584 | tf_op jit(solution)/shard_map/ppermute | solution.py:385
  32.6 4.8 %collective-permute-start.6 = (f32[16,128]{1,0:T(8,128)S(1)}, f32[16,128]{1,0:T(8,128)S(1)}, u32[]{:S(2)}, u32[]{:S(2)}) collective-permute-start(f32[16,128]{1,0:T(8,128)S(1)} %get-tuple-element.24.refs_0_), channel_id=1, source_target_pairs={{0,2},{1,3},{2,0},{3,1},{4,6},{5,7},{6,4},{7,5},{8,10},{9,11},{10,... | collective-permute-start | bytes 24584 | tf_op jit(solution)/shard_map/ppermute | solution.py:385
  33.7 4.2 %collective-permute-start.7 = (f32[16,128]{1,0:T(8,128)S(1)}, f32[16,128]{1,0:T(8,128)S(1)}, u32[]{:S(2)}, u32[]{:S(2)}) collective-permute-start(f32[16,128]{1,0:T(8,128)S(1)} %get-tuple-element.24.refs_0_), channel_id=1, source_target_pairs={{0,3},{1,0},{2,1},{3,2},{4,7},{5,4},{6,5},{7,6},{8,11},{9,8},{10,9... | collective-permute-start | bytes 24584 | tf_op jit(solution)/shard_map/ppermute | solution.py:385

commit v4 on v3

--- a/solution.py
+++ b/solution.py
@@ -63,14 +63,6 @@
             result.append((tile, at + reach))
             at += 2 * reach
     return result, tile + 1
-
-
-def left_lanes(geo):
-    spots, tiles = places(geo)
-    mask = np.zeros((tiles, 1, geo.lz), np.bool_)
-    for index, (tile, centre) in enumerate(spots):
-        mask[tile, 0, centre - REACHES[index // geo.lx] : centre] = True
-    return mask
 
 
 def iota(shape, dim):
@@ -89,8 +81,7 @@
     shear_hbm,
     ratio_hbm,
     scale_hbm,
-    main,
-    slab,
+    payload,
     tables,
     new,
     old,
@@ -121,12 +112,12 @@
         values += [energy_max[i], region[i].astype(jnp.float32)]
         values += [old[a, i] * share for a in range(3)]
         for f, value in enumerate(values):
-            main[f * geo.lx + i] = value
+            payload[f * geo.lx + i] = value
             tile, centre = spots[f * geo.lx + i]
             inside = (lane >= centre - REACHES[f]) & (lane < centre + REACHES[f])
             edges[tile] = jnp.where(inside, pltpu.roll(value, centre, 1), edges[tile])
     for tile in range(tiles):
-        slab[tile] = edges[tile]
+        payload[FIELDS * geo.lx + tile] = edges[tile]
     regions, terms = moduli.shape
     for r in range(regions):
         entries = [shear[r], ratio[r], scale[r]]
@@ -171,7 +162,7 @@
 
 
 def basis_kernel(geo, where, *refs):
-    tables, blocks = refs[0], refs[1:-5]
+    tables, blocks, halos = refs[0], refs[1:-5:2], refs[2:-5:2]
     basis, dev_own, grams, held, field = refs[-5:]
     lx, ly, lz = geo.lx, geo.ly, geo.lz
     planes, rows, lanes = geo.bx * lx, geo.by * ly, 2 * lz
@@ -198,7 +189,8 @@
         parts = []
         for b in range(geo.by):
             array, at = where[p // lx, b]
-            edge = pltpu.roll(blocks[array][at, FIELDS * lx + tile], lz - centre, 1)
+            left, right = halos[array][0, at, tile], halos[array][1, at, tile]
+            edge = pltpu.roll(jnp.where(lane[:ly, :lz] < centre, left, right), lz - centre, 1)
             parts.append(jnp.concatenate([blocks[array][at, f * lx + p % lx], edge], axis=1))
         return jnp.concatenate(parts, axis=0)
 
@@ -256,7 +248,7 @@
 
 
 def visco_kernel(geo, where, *refs):
-    tables, dev_own, visco, blocks = refs[0], refs[1], refs[2], refs[3:-3]
+    tables, dev_own, visco, blocks, halos = refs[0], refs[1], refs[2], refs[3:-3:2], refs[4:-3:2]
     stress, visco_next, energy_next = refs[-3:]
     lx, ly, lz = geo.lx, geo.ly, geo.lz
     spots, _ = places(geo)
@@ -292,9 +284,9 @@
             next_y = pltpu.roll(jnp.where(row == 0, first, value), ly - 1, 0)
             prev_y = pltpu.roll(jnp.where(row == ly - 1, last, value), 1, 0)
             tile, centre = spots[at]
-            edge = own(FIELDS * lx + tile)
-            next_z = jnp.where(lane == lz - 1, pltpu.roll(edge, lz - 1 - centre, 1), pltpu.roll(value, lz - 1, 1))
-            prev_z = jnp.where(lane == 0, pltpu.roll(edge, lz + 1 - centre, 1), pltpu.roll(value, 1, 1))
+            left, right = halos[0][0, 0, tile], halos[0][1, 0, tile]
+            next_z = jnp.where(lane == lz - 1, pltpu.roll(right, lz - 1 - centre, 1), pltpu.roll(value, lz - 1, 1))
+            prev_z = jnp.where(lane == 0, pltpu.roll(left, lz + 1 - centre, 1), pltpu.roll(value, 1, 1))
             grad.append([0.5 * (next_x - prev_x), 0.5 * (next_y - prev_y), 0.5 * (next_z - prev_z)])
         dev_old = deviator(grad)
         dev_new = [dev_own[k, i] for k in range(6)]
@@ -391,21 +383,33 @@
     return jnp.stack([moved(shard, axis, lambda i: (i - step) % count) if step else shard for step in steps])
 
 
+def edges_along_z(parts, geo):
+    slabs = jnp.concatenate([part[FIELDS * geo.lx :] for part in parts])
+    up = [(i, i + 1) for i in range(geo.gz - 1)]
+    down = [(j, i) for i, j in up]
+    pair = jnp.concatenate([lax.ppermute(slabs, "gz", up), lax.ppermute(slabs, "gz", down)])
+    return pair.reshape((2, len(parts), -1) + pair.shape[1:])
+
+
 def gathered(payload, geo):
     if not geo.full:
         blocks = ring(ring(payload, "gy", geo.hops_y), "gx", geo.hops_x)
+        blocks = blocks.reshape((geo.bx * geo.by,) + payload.shape)
         where = {(x, y): (0, x * geo.by + y) for x in range(geo.bx) for y in range(geo.by)}
-        return [blocks.reshape((geo.bx * geo.by,) + payload.shape)], where
-    steps = [("gy", 0, 1)] * (geo.gy - 1)
-    steps += [("gx", 1 << bit, 0) for bit in reversed(range(geo.gx.bit_length() - 1))]
-    arrays, codes = [payload[None]], [[(0, 0)]]
-    for axis, step_x, step_y in steps:
-        if len(arrays) == 2:
-            arrays, codes = [jnp.concatenate(arrays, axis=0)], [codes[0] + codes[1]]
-        arrays.append(moved(arrays[0], axis, lambda i: i ^ (step_x + step_y)))
-        codes.append([(x ^ step_x, y ^ step_y) for x, y in codes[0]])
-    where = {code: (n, place) for n, held in enumerate(codes) for place, code in enumerate(held)}
-    return arrays, where
+        return [blocks, edges_along_z(list(blocks), geo)], where
+    codes = [(x, y) for x in range(0, geo.gx, 2) for y in range(geo.gy)]
+    parts = [payload]
+    for x, y in codes[1:]:
+        parts.append(moved(payload, ("gx", "gy"), lambda i: (i // geo.gy ^ x) * geo.gy + (i % geo.gy ^ y)))
+    blocks = jnp.concatenate(parts)
+    halos = edges_along_z(parts, geo)
+    where = {code: (0, place) for place, code in enumerate(codes)}
+    shape = (len(parts),) + payload.shape
+    if geo.gx == 1:
+        return [blocks.reshape(shape), halos], where
+    where.update({(x + 1, y): (1, place) for place, (x, y) in enumerate(codes)})
+    other, other_halos = moved(blocks, "gx", lambda i: i ^ 1), moved(halos, "gx", lambda i: i ^ 1)
+    return [blocks.reshape(shape), halos, other.reshape(shape), other_halos], where
 
 
 def summed(terms, axis):
@@ -434,20 +438,16 @@
     regions, terms = prony_moduli.shape
     arguments = [displacement, displacement_old, energy_max, region, dirichlet]
     parameters = [prony_moduli, prony_times, shear_modulus, mullins_ratio, mullins_scale]
-    main, slab, tables = call(
+    payload, tables = call(
         functools.partial(pack_kernel, geo),
-        [shaped(FIELDS * lx, ly, lz), shaped(tiles, ly, lz), shaped(MODULI + 2 * terms, regions, lz)],
+        [shaped(FIELDS * lx + tiles, ly, lz), shaped(MODULI + 2 * terms, regions, lz)],
         arguments + parameters,
         [pltpu.VMEM(a.shape, a.dtype) for a in arguments]
         + [pltpu.SMEM(a.shape, a.dtype) for a in parameters]
         + [pltpu.SemaphoreType.DMA((len(arguments) + len(parameters),))],
-        space=pltpu.HBM,
-    )
-    up = [(i, i + 1) for i in range(geo.gz - 1)]
-    down = [(j, i) for i, j in up]
-    from_left, from_right = lax.ppermute(slab, "gz", up), lax.ppermute(slab, "gz", down)
-    edges = jnp.where(left_lanes(geo), from_left, from_right)
-    payload = jnp.concatenate([main, edges], axis=0)
+        space=pl.ANY,
+        vmem=56 * MB,
+    )
     blocks, where = gathered(payload, geo)
     planes, rows = geo.bx * lx, geo.by * ly
     basis, dev_own, grams = call(

time: 39.2 us -> 33.2 us (0.85)
  local copies, waits for them, and re-layouts: 6.89 us -> 2.33 us
  waiting for transfers between devices: 12.6 us -> 10.5 us
  Pallas kernels: 3.46 us -> 4.3 us
    unnamed x24 -> x11, local copies, waits for them, and re-layouts: 6.89 us -> 0.96 us
    ppermute x6 -> x8, waiting for transfers between devices: 8.42 us -> 6.17 us  [moved(): lax.ppermute(shard, axis, [(i, target(i)) for i in range(lax.axis_size(ax...]
    slice x0 -> x6, local copies, waits for them, and re-layouts: none -> 1.36 us  [edges_along_z(): slabs = jnp.concatenate([part[FIELDS * geo.lx:] for part in parts])]
    ppermute x6 -> x8, starting transfers between devices: 8.78 us -> 10.1 us  [moved(): lax.ppermute(shard, axis, [(i, target(i)) for i in range(lax.axis_size(ax...]
    ppermute x2, starting transfers between devices: 6.22 us -> 4.9 us  [the longest x1 3.61 us: edges_along_z(): lax.ppermute(slabs, 'gz', up)]
    pallas_call x4, Pallas kernels: 3.46 us -> 4.3 us  [call(): pl.pallas_call(kernel, out_shape=outs, in_specs=[pl.BlockSpec(memory_spac...]
  transfers between devices with their start and end apart: 8 -> 10, of which waited for: 5 -> 7; matrix products, arithmetic and copies ran while one was open for 0% -> 5% of each run, Pallas kernels for 2% -> 3%
where the time goes in v4:
time: 33.2 us; the launch traced here: 32.9 us
  starting transfers between devices  15 us (45%)
  waiting for transfers between devices  10.5 us (32%)
  Pallas kernels  4.3 us (13%)
  local copies, waits for them, and re-layouts  2.33 us (7%)
  between operations  0.71 us (2%)
    ppermute x8, starting transfers between devices, moved(): lax.ppermute(shard, axis, [(i, target(i)) for i in range(lax.axis_size(ax...  10.1 us
    ppermute x8, waiting for transfers between devices, moved(): lax.ppermute(shard, axis, [(i, target(i)) for i in range(lax.axis_size(ax...  6.17 us
    pallas_call x4, Pallas kernels, call(): pl.pallas_call(kernel, out_shape=outs, in_specs=[pl.BlockSpec(memory_spac...  4.3 us
    ppermute x1, waiting for transfers between devices, edges_along_z(): lax.ppermute(slabs, 'gz', down)  4.21 us
    ppermute x1, starting transfers between devices, edges_along_z(): lax.ppermute(slabs, 'gz', up)  3.61 us
    slice x6, local copies, waits for them, and re-layouts, edges_along_z(): slabs = jnp.concatenate([part[FIELDS * geo.lx:] for part in parts])  1.36 us
    ppermute x1, starting transfers between devices, edges_along_z(): lax.ppermute(slabs, 'gz', down)  1.29 us
    unnamed x11, local copies, waits for them, and re-layouts  0.96 us
  transfers between devices with their start and end apart: 10, of which 7 were waited for; matrix products, arithmetic and copies ran while one was open for 5% of the time, Pallas kernels for 3%

profile of v4, /device:TPU:0, one launch (start us, length us, event | category | flops | bytes accessed | tf_op | source)
XLA Modules:
  0.0 32.9 jit_solution(6538474025585977165)
XLA Ops:
  0.6 1.7 %shard_map.146 = (f32[17,8,128]{2,1,0:T(8,128)}, f32[15,4,128]{2,1,0:T(4,128)}) custom-call(f32[3,2,8,128]{3,2,1,0:T(8,128)} %new_hbm.1, f32[3,2,8,128]{3,2,1,0:T(8,128)} %old_hbm.1, f32[2,8,128]{2,1,0:T(8,128)} %energy_hbm.1, s32[2,8,128]{2,1,0:T(8,128)} %region_hbm.1, s32[2,8,128]{2,1,0:T(8,128)} %dirichlet_hbm.1, f32[4,6]{1,0:T(4,128)} %moduli_hbm.1, ...), custom_call_target="tpu_custom_call" | custom-call | bytes 174320 | tf_op jit(solution)/shard_map/pallas_call | solution.py:365
  2.3 3.0 %collective-permute-start = (f32[17,8,128]{2,1,0:T(8,128)}, f32[17,8,128]{2,1,0:T(8,128)S(1)}, u32[]{:S(2)}, u32[]{:S(2)}) collective-permute-start(f32[17,8,128]{2,1,0:T(8,128)} %get-tuple-element.16), channel_id=1, source_target_pairs={{0,4},{4,0},{8,12},{12,8},{16,20},{20,16},{24,28},{28,24},{1,5},{5... | collective-permute-start | bytes 208904 | tf_op jit(solution)/shard_map/ppermute | solution.py:377
  5.3 1.5 %collective-permute-start.1 = (f32[17,8,128]{2,1,0:T(8,128)}, f32[17,8,128]{2,1,0:T(8,128)S(1)}, u32[]{:S(2)}, u32[]{:S(2)}) collective-permute-start(f32[17,8,128]{2,1,0:T(8,128)} %get-tuple-element.16), channel_id=1, source_target_pairs={{0,16},{4,20},{8,24},{12,28},{16,0},{20,4},{24,8},{28,12},{1,17},{... | collective-permute-start | bytes 208904 | tf_op jit(solution)/shard_map/ppermute | solution.py:377
  6.9 0.0 collective-permute-start.2
  6.9 0.9 %constant_dynamic-update-slice_fusion.3 = f32[68,8,128]{2,1,0:T(8,128)S(1)} fusion(f32[17,8,128]{2,1,0:T(8,128)} %get-tuple-element.16), kind=kLoop, calls=%fused_computation.5 | loop fusion | bytes 139264
  7.8 0.3 collective-permute-done
  8.1 1.8 %collective-permute-done.1 = f32[17,8,128]{2,1,0:T(8,128)S(1)} collective-permute-done((f32[17,8,128]{2,1,0:T(8,128)}, f32[17,8,128]{2,1,0:T(8,128)S(1)}, u32[]{:S(2)}, u32[]{:S(2)}) %collective-permute-start.1) | collective-permute-done | bytes 69664 | tf_op jit(solution)/shard_map/ppermute | solution.py:377
  9.9 2.4 %collective-permute-done.2 = f32[17,8,128]{2,1,0:T(8,128)S(1)} collective-permute-done((f32[17,8,128]{2,1,0:T(8,128)}, f32[17,8,128]{2,1,0:T(8,128)S(1)}, u32[]{:S(2)}, u32[]{:S(2)}) %collective-permute-start.2) | collective-permute-done | bytes 69664 | tf_op jit(solution)/shard_map/ppermute | solution.py:377
  12.3 0.7 %slice.12 = f32[1,8,128]{2,1,0:T(8,128)S(1)} slice(f32[17,8,128]{2,1,0:T(8,128)} %get-tuple-element.16), slice={[16:17], [0:8], [0:128]} | slice | bytes 8192 | tf_op jit(solution)/shard_map/slice | solution.py:387
  13.0 0.7 %slice-done = f32[1,8,128]{2,1,0:T(8,128)S(1)} async-done(((f32[17,8,128]{2,1,0:T(8,128)}), f32[1,8,128]{2,1,0:T(8,128)S(1)}, s32[]{:S(2)}) %slice-start) | async-done | bytes 4120 | tf_op jit(solution)/shard_map/slice | solution.py:387
  13.7 0.0 slice-done.1
  13.7 3.6 %collective-permute-start.3 = (f32[4,8,128]{2,1,0:T(8,128)S(1)}, f32[4,8,128]{2,1,0:T(8,128)S(1)}, u32[]{:S(2)}, u32[]{:S(2)}) collective-permute-start(f32[4,8,128]{2,1,0:T(8,128)S(1)} %pad_maximum_fusion.1), channel_id=1, source_target_pairs={{0,1},{1,2},{2,3},{4,5},{5,6},{6,7},{8,9},{9,10},{10,11},{12,13},{... | collective-permute-start | bytes 49160 | tf_op jit(solution)/shard_map/ppermute | solution.py:390
  17.3 1.3 %collective-permute-start.4 = (f32[4,8,128]{2,1,0:T(8,128)S(1)}, f32[4,8,128]{2,1,0:T(8,128)S(1)}, u32[]{:S(2)}, u32[]{:S(2)}) collective-permute-start(f32[4,8,128]{2,1,0:T(8,128)S(1)} %pad_maximum_fusion.1), channel_id=1, source_target_pairs={{1,0},{2,1},{3,2},{5,4},{6,5},{7,6},{9,8},{10,9},{11,10},{13,12},{... | collective-permute-start | bytes 49160 | tf_op jit(solution)/shard_map/ppermute | solution.py:390
  18.6 0.1 collective-permute-done.3
  18.7 4.2 %collective-permute-done.4 = f32[4,8,128]{2,1,0:T(8,128)S(1)} collective-permute-done((f32[4,8,128]{2,1,0:T(8,128)S(1)}, f32[4,8,128]{2,1,0:T(8,128)S(1)}, u32[]{:S(2)}, u32[]{:S(2)}) %collective-permute-start.4) | collective-permute-done | bytes 16416 | tf_op jit(solution)/shard_map/ppermute | solution.py:390
  22.9 0.0 collective-permute-start.6
  22.9 1.2 %collective-permute-done.6.refs_4_.refs_6_ = f32[2,4,1,8,128]{4,3,2,1,0:T(8,128)S(1)} collective-permute-done((f32[2,4,1,8,128]{4,3,2,1,0:T(8,128)S(1)}, f32[2,4,1,8,128]{4,3,2,1,0:T(8,128)S(1)}, u32[]{:S(2)}, u32[]{:S(2)}) %collective-permute-start.6) | collective-permute-done | bytes 32800 | tf_op jit(solution)/shard_map/ppermute | solution.py:377
  24.2 0.9 %shard_map.147 = (f32[5,2,8,128]{3,2,1,0:T(8,128)S(1)}, f32[6,2,8,128]{3,2,1,0:T(8,128)S(1)}, f32[16,128]{1,0:T(8,128)S(1)}) custom-call(f32[15,4,128]{2,1,0:T(4,128)S(1)} %copy-done.1, f32[4,17,8,128]{3,2,1,0:T(8,128)S(1)} %bitcast.3, f32[2,4,1,8,128]{4,3,2,1,0:T(8,128)S(1)} %bitcast.8, f32[4,17,8,128]{3,2,1,0:T(8,128)S(1)} %bitcast.5, ...), custom_call_target="tpu_custom_call" | custom-call | flops 8192000 | bytes 751616 | tf_op jit(solution)/shard_map/pallas_call | solution.py:365
  25.1 1.6 %collective-permute-start.7 = (f32[16,128]{1,0:T(8,128)S(1)}, f32[16,128]{1,0:T(8,128)S(1)}, u32[]{:S(2)}, u32[]{:S(2)}) collective-permute-start(f32[16,128]{1,0:T(8,128)S(1)} %get-tuple-element.22.refs_0_), channel_id=1, source_target_pairs={{0,1},{1,2},{2,3},{3,0},{4,5},{5,6},{6,7},{7,4},{8,9},{9,10},{10,1... | collective-permute-start | bytes 24584 | tf_op jit(solution)/shard_map/ppermute | solution.py:377
  26.7 1.1 %collective-permute-start.8 = (f32[16,128]{1,0:T(8,128)S(1)}, f32[16,128]{1,0:T(8,128)S(1)}, u32[]{:S(2)}, u32[]{:S(2)}) collective-permute-start(f32[16,128]{1,0:T(8,128)S(1)} %get-tuple-element.22.refs_0_), channel_id=1, source_target_pairs={{0,2},{1,3},{2,0},{3,1},{4,6},{5,7},{6,4},{7,5},{8,10},{9,11},{10,... | collective-permute-start | bytes 24584 | tf_op jit(solution)/shard_map/ppermute | solution.py:377
  27.8 2.8 %collective-permute-start.9 = (f32[16,128]{1,0:T(8,128)S(1)}, f32[16,128]{1,0:T(8,128)S(1)}, u32[]{:S(2)}, u32[]{:S(2)}) collective-permute-start(f32[16,128]{1,0:T(8,128)S(1)} %get-tuple-element.22.refs_0_), channel_id=1, source_target_pairs={{0,3},{1,0},{2,1},{3,2},{4,7},{5,4},{6,5},{7,6},{8,11},{9,8},{10,9... | collective-permute-start | bytes 24584 | tf_op jit(solution)/shard_map/ppermute | solution.py:377
  30.7 0.8 %shard_map.148 = (f32[6,2,8,128]{3,2,1,0:T(8,128)}, f32[6,6,2,8,128]{4,3,2,1,0:T(8,128)}, f32[2,8,128]{2,1,0:T(8,128)}) custom-call(f32[15,4,128]{2,1,0:T(4,128)S(1)} %copy-done.1, f32[6,2,8,128]{3,2,1,0:T(8,128)S(1)} %get-tuple-element.17.refs_1_, f32[6,6,2,8,128]{4,3,2,1,0:T(8,128)S(1)} %copy-done, f32[4,17,8,128]{3,2,1,0:T(8,128)S(1)} %bitcast.4, ...), custom_call_target="tpu_custom_call" | custom-call | flops 1024000 | bytes 1349632 | tf_op jit(solution)/shard_map/pallas_call | solution.py:365
  31.5 0.5 %collective-permute-done.9.refs_3_ = f32[16,128]{1,0:T(8,128)S(1)} collective-permute-done((f32[16,128]{1,0:T(8,128)S(1)}, f32[16,128]{1,0:T(8,128)S(1)}, u32[]{:S(2)}, u32[]{:S(2)}) %collective-permute-start.9) | collective-permute-done | bytes 8224 | tf_op jit(solution)/shard_map/ppermute | solution.py:377
  32.0 0.8 %shard_map.149 = (f32[2,8,128]{2,1,0:T(8,128)}, f32[2,8,128]{2,1,0:T(8,128)}) custom-call(f32[5,2,8,128]{3,2,1,0:T(8,128)S(1)} %get-tuple-element.21.basis, f32[16,128]{1,0:T(8,128)S(1)} %get-tuple-element.22.refs_0_, f32[16,128]{1,0:T(8,128)S(1)} %collective-permute-done.7.refs_1_, f32[16,128]{1,0:T(8,128)S(1)} %collective-permute-done.8.refs_2_, ...), custom_call_target="tpu_custom_call" | custom-call | bytes 90112 | tf_op jit(solution)/shard_map/pallas_call | solution.py:365
  (20 shorter events, 0.1 us)
Async XLA Ops:
  2.3 5.8 %collective-permute-start = (f32[17,8,128]{2,1,0:T(8,128)}, f32[17,8,128]{2,1,0:T(8,128)S(1)}, u32[]{:S(2)}, u32[]{:S(2)}) collective-permute-start(f32[17,8,128]{2,1,0:T(8,128)} %get-tuple-element.16), channel_id=1, source_target_pairs={{0,4},{4,0},{8,12},{12,8},{16,20},{20,16},{24,28},{28,24},{1,5},{5... | collective-permute-start | bytes 208904 | tf_op jit(solution)/shard_map/ppermute | solution.py:377
  5.3 4.5 %collective-permute-start.1 = (f32[17,8,128]{2,1,0:T(8,128)}, f32[17,8,128]{2,1,0:T(8,128)S(1)}, u32[]{:S(2)}, u32[]{:S(2)}) collective-permute-start(f32[17,8,128]{2,1,0:T(8,128)} %get-tuple-element.16), channel_id=1, source_target_pairs={{0,16},{4,20},{8,24},{12,28},{16,0},{20,4},{24,8},{28,12},{1,17},{... | collective-permute-start | bytes 208904 | tf_op jit(solution)/shard_map/ppermute | solution.py:377
  6.9 5.4 %collective-permute-start.2 = (f32[17,8,128]{2,1,0:T(8,128)}, f32[17,8,128]{2,1,0:T(8,128)S(1)}, u32[]{:S(2)}, u32[]{:S(2)}) collective-permute-start(f32[17,8,128]{2,1,0:T(8,128)} %get-tuple-element.16), channel_id=1, source_target_pairs={{0,20},{4,16},{8,28},{12,24},{16,4},{20,0},{24,12},{28,8},{1,21},{... | collective-permute-start | bytes 208904 | tf_op jit(solution)/shard_map/ppermute | solution.py:377
  8.1 4.9 %copy-start.2 = (f32[17,8,128]{2,1,0:T(8,128)}, f32[17,8,128]{2,1,0:T(8,128)S(1)}, u32[]{:S(2)}) copy-start(f32[17,8,128]{2,1,0:T(8,128)S(1)} %collective-permute-done) | copy-start | bytes 208900
  9.9 3.1 %copy-start.3 = (f32[17,8,128]{2,1,0:T(8,128)}, f32[17,8,128]{2,1,0:T(8,128)S(1)}, u32[]{:S(2)}) copy-start(f32[17,8,128]{2,1,0:T(8,128)S(1)} %collective-permute-done.1) | copy-start | bytes 208900
  12.3 11.9 %collective-permute-start.5 = (f32[68,8,128]{2,1,0:T(8,128)S(1)}, f32[68,8,128]{2,1,0:T(8,128)S(1)}, u32[]{:S(2)}, u32[]{:S(2)}) collective-permute-start(f32[68,8,128]{2,1,0:T(8,128)S(1)} %constant_dynamic-update-slice_fusion), channel_id=1, source_target_pairs={{0,8},{8,0},{16,24},{24,16},{1,9},{9,1},{17,25},{25,17},{2,10},{10... | collective-permute-start | bytes 835592 | tf_op jit(solution)/shard_map/ppermute | solution.py:377
  13.0 0.7 %slice-start = ((f32[17,8,128]{2,1,0:T(8,128)}), f32[1,8,128]{2,1,0:T(8,128)S(1)}, s32[]{:S(2)}) async-start(f32[17,8,128]{2,1,0:T(8,128)} %copy-done.2), calls=%async_computation | async-start | bytes 8192 | tf_op jit(solution)/shard_map/slice | solution.py:387
  13.0 0.7 %slice-start.1 = ((f32[17,8,128]{2,1,0:T(8,128)}), f32[1,8,128]{2,1,0:T(8,128)S(1)}, s32[]{:S(2)}) async-start(f32[17,8,128]{2,1,0:T(8,128)} %copy-done.3), calls=%async_computation.1 | async-start | bytes 8192 | tf_op jit(solution)/shard_map/slice | solution.py:387
  13.7 10.5 %copy-start.1 = (f32[15,4,128]{2,1,0:T(4,128)S(1)}, f32[15,4,128]{2,1,0:T(4,128)}, u32[]{:S(2)}) copy-start(f32[15,4,128]{2,1,0:T(4,128)} %get-tuple-element.15.refs_0_) | copy-start | bytes 92164
  13.7 5.0 %collective-permute-start.3 = (f32[4,8,128]{2,1,0:T(8,128)S(1)}, f32[4,8,128]{2,1,0:T(8,128)S(1)}, u32[]{:S(2)}, u32[]{:S(2)}) collective-permute-start(f32[4,8,128]{2,1,0:T(8,128)S(1)} %pad_maximum_fusion.1), channel_id=1, source_target_pairs={{0,1},{1,2},{2,3},{4,5},{5,6},{6,7},{8,9},{9,10},{10,11},{12,13},{... | collective-permute-start | bytes 49160 | tf_op jit(solution)/shard_map/ppermute | solution.py:390
  17.3 5.6 %collective-permute-start.4 = (f32[4,8,128]{2,1,0:T(8,128)S(1)}, f32[4,8,128]{2,1,0:T(8,128)S(1)}, u32[]{:S(2)}, u32[]{:S(2)}) collective-permute-start(f32[4,8,128]{2,1,0:T(8,128)S(1)} %pad_maximum_fusion.1), channel_id=1, source_target_pairs={{1,0},{2,1},{3,2},{5,4},{6,5},{7,6},{9,8},{10,9},{11,10},{13,12},{... | collective-permute-start | bytes 49160 | tf_op jit(solution)/shard_map/ppermute | solution.py:390
  22.9 1.2 %collective-permute-start.6 = (f32[2,4,1,8,128]{4,3,2,1,0:T(8,128)S(1)}, f32[2,4,1,8,128]{4,3,2,1,0:T(8,128)S(1)}, u32[]{:S(2)}, u32[]{:S(2)}) collective-permute-start(f32[2,4,1,8,128]{4,3,2,1,0:T(8,128)S(1)} %bitcast.7), channel_id=1, source_target_pairs={{0,8},{8,0},{16,24},{24,16},{1,9},{9,1},{17,25},{25,17},{2,10},{10... | collective-permute-start | bytes 98312 | tf_op jit(solution)/shard_map/ppermute | solution.py:377
  24.2 6.5 %copy-start = (f32[6,6,2,8,128]{4,3,2,1,0:T(8,128)S(1)}, f32[6,6,2,8,128]{4,3,2,1,0:T(8,128)}, u32[]{:S(2)}) copy-start(f32[6,6,2,8,128]{4,3,2,1,0:T(8,128)} %refs_2_.1) | copy-start | bytes 884740
  25.1 6.4 %collective-permute-start.7 = (f32[16,128]{1,0:T(8,128)S(1)}, f32[16,128]{1,0:T(8,128)S(1)}, u32[]{:S(2)}, u32[]{:S(2)}) collective-permute-start(f32[16,128]{1,0:T(8,128)S(1)} %get-tuple-element.22.refs_0_), channel_id=1, source_target_pairs={{0,1},{1,2},{2,3},{3,0},{4,5},{5,6},{6,7},{7,4},{8,9},{9,10},{10,1... | collective-permute-start | bytes 24584 | tf_op jit(solution)/shard_map/ppermute | solution.py:377
  26.7 4.8 %collective-permute-start.8 = (f32[16,128]{1,0:T(8,128)S(1)}, f32[16,128]{1,0:T(8,128)S(1)}, u32[]{:S(2)}, u32[]{:S(2)}) collective-permute-start(f32[16,128]{1,0:T(8,128)S(1)} %get-tuple-element.22.refs_0_), channel_id=1, source_target_pairs={{0,2},{1,3},{2,0},{3,1},{4,6},{5,7},{6,4},{7,5},{8,10},{9,11},{10,... | collective-permute-start | bytes 24584 | tf_op jit(solution)/shard_map/ppermute | solution.py:377
  27.8 4.2 %collective-permute-start.9 = (f32[16,128]{1,0:T(8,128)S(1)}, f32[16,128]{1,0:T(8,128)S(1)}, u32[]{:S(2)}, u32[]{:S(2)}) collective-permute-start(f32[16,128]{1,0:T(8,128)S(1)} %get-tuple-element.22.refs_0_), channel_id=1, source_target_pairs={{0,3},{1,0},{2,1},{3,2},{4,7},{5,4},{6,5},{7,6},{8,11},{9,8},{10,9... | collective-permute-start | bytes 24584 | tf_op jit(solution)/shard_map/ppermute | solution.py:377

commit v5 on v4

--- a/solution.py
+++ b/solution.py
@@ -69,43 +69,16 @@
     return lax.broadcasted_iota(jnp.int32, shape, dim)
 
 
+def first_kernel(zeros):
+    zeros[...] = jnp.zeros(zeros.shape, jnp.float32)
+
+
 def pack_kernel(
-    geo,
-    new_hbm,
-    old_hbm,
-    energy_hbm,
-    region_hbm,
-    dirichlet_hbm,
-    moduli_hbm,
-    times_hbm,
-    shear_hbm,
-    ratio_hbm,
-    scale_hbm,
-    payload,
-    tables,
-    new,
-    old,
-    energy_max,
-    region,
-    dirichlet,
-    moduli,
-    times,
-    shear,
-    ratio,
-    scale,
-    arrived,
+    geo, moduli, times, shear, ratio, scale, zeros, new, old, energy_max, region, dirichlet, payload, tables
 ):
-    sources = (new_hbm, old_hbm, energy_hbm, region_hbm, dirichlet_hbm)
-    sources += (moduli_hbm, times_hbm, shear_hbm, ratio_hbm, scale_hbm)
-    targets = (new, old, energy_max, region, dirichlet, moduli, times, shear, ratio, scale)
-    copies = [pltpu.make_async_copy(a, b, arrived.at[n]) for n, (a, b) in enumerate(zip(sources, targets))]
-    for copy in copies:
-        copy.start()
-    for copy in copies:
-        copy.wait()
     spots, tiles = places(geo)
     lane = iota((geo.ly, geo.lz), 1)
-    edges = [jnp.zeros((geo.ly, geo.lz), jnp.float32)] * tiles
+    edges = [zeros[...]] * tiles
     for i in range(geo.lx):
         share = (1 - dirichlet[i]).astype(jnp.float32)
         values = [new[a, i] * share for a in range(3)]
@@ -253,7 +226,7 @@
     lx, ly, lz = geo.lx, geo.ly, geo.lz
     spots, _ = places(geo)
     row, lane = iota((ly, lz), 0), iota((ly, lz), 1)
-    index_x, index_y = lax.axis_index("gx"), lax.axis_index("gy")
+    index_x, index_y, index_z = (lax.axis_index(name) for name in ("gx", "gy", "gz"))
     regions, terms = tables.shape[1], visco.shape[0]
 
     def own(at, code_y=0):
@@ -285,8 +258,10 @@
             prev_y = pltpu.roll(jnp.where(row == ly - 1, last, value), 1, 0)
             tile, centre = spots[at]
             left, right = halos[0][0, 0, tile], halos[0][1, 0, tile]
-            next_z = jnp.where(lane == lz - 1, pltpu.roll(right, lz - 1 - centre, 1), pltpu.roll(value, lz - 1, 1))
-            prev_z = jnp.where(lane == 0, pltpu.roll(left, lz + 1 - centre, 1), pltpu.roll(value, 1, 1))
+            right = jnp.where(index_z == geo.gz - 1, 0.0, pltpu.roll(right, lz - 1 - centre, 1))
+            left = jnp.where(index_z == 0, 0.0, pltpu.roll(left, lz + 1 - centre, 1))
+            next_z = jnp.where(lane == lz - 1, right, pltpu.roll(value, lz - 1, 1))
+            prev_z = jnp.where(lane == 0, left, pltpu.roll(value, 1, 1))
             grad.append([0.5 * (next_x - prev_x), 0.5 * (next_y - prev_y), 0.5 * (next_z - prev_z)])
         dev_old = deviator(grad)
         dev_new = [dev_own[k, i] for k in range(6)]
@@ -360,17 +335,19 @@
     return jax.ShapeDtypeStruct(shape, jnp.float32)
 
 
-def call(kernel, outs, arrays, scratch=(), flops=0, space=pltpu.VMEM, vmem=32 * MB):
-    moved = 4 * sum(int(np.prod(a.shape)) for a in list(arrays) + list(outs))
+def call(kernel, outs, arrays, scratch=(), flops=0, parameters=(), moved=None):
+    if moved is None:
+        moved = 4 * sum(int(np.prod(a.shape)) for a in list(arrays) + list(outs))
+    smem, vmem = pl.BlockSpec(memory_space=pltpu.SMEM), pl.BlockSpec(memory_space=pltpu.VMEM)
     return pl.pallas_call(
         kernel,
         out_shape=outs,
-        in_specs=[pl.BlockSpec(memory_space=space)] * len(arrays),
-        out_specs=[pl.BlockSpec(memory_space=pltpu.VMEM)] * len(outs),
+        in_specs=[smem] * len(parameters) + [vmem] * len(arrays),
+        out_specs=[vmem] * len(outs),
         scratch_shapes=list(scratch),
-        compiler_params=pltpu.CompilerParams(vmem_limit_bytes=vmem),
+        compiler_params=pltpu.CompilerParams(vmem_limit_bytes=32 * MB),
         cost_estimate=pl.CostEstimate(flops=flops, bytes_accessed=moved, transcendentals=0),
-    )(*arrays)
+    )(*parameters, *arrays)
 
 
 def moved(shard, axis, target):
@@ -383,12 +360,17 @@
     return jnp.stack([moved(shard, axis, lambda i: (i - step) % count) if step else shard for step in steps])
 
 
-def edges_along_z(parts, geo):
-    slabs = jnp.concatenate([part[FIELDS * geo.lx :] for part in parts])
-    up = [(i, i + 1) for i in range(geo.gz - 1)]
-    down = [(j, i) for i, j in up]
-    pair = jnp.concatenate([lax.ppermute(slabs, "gz", up), lax.ppermute(slabs, "gz", down)])
-    return pair.reshape((2, len(parts), -1) + pair.shape[1:])
+def edges_along_z(slabs, blocks, geo):
+    pair = jnp.concatenate([moved(slabs, "gz", lambda i: (i + step) % geo.gz) for step in (1, -1)])
+    return pair.reshape((2, blocks, -1) + pair.shape[1:])
+
+
+def assemble_kernel(geo, *refs):
+    parts, blocks, slabs = refs[:-2], refs[-2], refs[-1]
+    size, tiles = parts[0].shape[0], parts[0].shape[0] - FIELDS * geo.lx
+    for n, part in enumerate(parts):
+        blocks[n * size : (n + 1) * size] = part[...]
+        slabs[n * tiles : (n + 1) * tiles] = part[FIELDS * geo.lx :]
 
 
 def gathered(payload, geo):
@@ -396,13 +378,20 @@
         blocks = ring(ring(payload, "gy", geo.hops_y), "gx", geo.hops_x)
         blocks = blocks.reshape((geo.bx * geo.by,) + payload.shape)
         where = {(x, y): (0, x * geo.by + y) for x in range(geo.bx) for y in range(geo.by)}
-        return [blocks, edges_along_z(list(blocks), geo)], where
+        slabs = blocks[:, FIELDS * geo.lx :].reshape((-1,) + payload.shape[1:])
+        return [blocks, edges_along_z(slabs, blocks.shape[0], geo)], where
     codes = [(x, y) for x in range(0, geo.gx, 2) for y in range(geo.gy)]
     parts = [payload]
     for x, y in codes[1:]:
         parts.append(moved(payload, ("gx", "gy"), lambda i: (i // geo.gy ^ x) * geo.gy + (i % geo.gy ^ y)))
-    blocks = jnp.concatenate(parts)
-    halos = edges_along_z(parts, geo)
+    size, plane = payload.shape[0], payload.shape[1:]
+    tiles = size - FIELDS * geo.lx
+    blocks, slabs = call(
+        functools.partial(assemble_kernel, geo),
+        [shaped(len(parts) * size, *plane), shaped(len(parts) * tiles, *plane)],
+        parts,
+    )
+    halos = edges_along_z(slabs, len(parts), geo)
     where = {code: (0, place) for place, code in enumerate(codes)}
     shape = (len(parts),) + payload.shape
     if geo.gx == 1:
@@ -436,17 +425,12 @@
     lx, ly, lz = energy_max.shape
     _, tiles = places(geo)
     regions, terms = prony_moduli.shape
-    arguments = [displacement, displacement_old, energy_max, region, dirichlet]
-    parameters = [prony_moduli, prony_times, shear_modulus, mullins_ratio, mullins_scale]
+    (zeros,) = call(first_kernel, [shaped(ly, lz)], [], flops=1 << 34, moved=0)
     payload, tables = call(
         functools.partial(pack_kernel, geo),
         [shaped(FIELDS * lx + tiles, ly, lz), shaped(MODULI + 2 * terms, regions, lz)],
-        arguments + parameters,
-        [pltpu.VMEM(a.shape, a.dtype) for a in arguments]
-        + [pltpu.SMEM(a.shape, a.dtype) for a in parameters]
-        + [pltpu.SemaphoreType.DMA((len(arguments) + len(parameters),))],
-        space=pl.ANY,
-        vmem=56 * MB,
+        [zeros, displacement, displacement_old, energy_max, region, dirichlet],
+        parameters=[prony_moduli, prony_times, shear_modulus, mullins_ratio, mullins_scale],
     )
     blocks, where = gathered(payload, geo)
     planes, rows = geo.bx * lx, geo.by * ly

time: 33.2 us -> 28.8 us (0.87)
  local copies, waits for them, and re-layouts: 2.33 us -> 0.7 us
  starting transfers between devices: 15 us -> 13.7 us
  Pallas kernels: 4.3 us -> 3.34 us
  waiting for transfers between devices: 10.5 us -> 10.1 us
    ppermute x2 -> x0, starting transfers between devices: 4.9 us -> none  [the longest x1 3.61 us: edges_along_z(): lax.ppermute(slabs, 'gz', up)]
    ppermute x2 -> x0, waiting for transfers between devices: 4.33 us -> none  [the longest x1 4.21 us: edges_along_z(): lax.ppermute(slabs, 'gz', down)]
    ppermute x8 -> x10, waiting for transfers between devices: 6.17 us -> 10.1 us  [moved(): lax.ppermute(shard, axis, [(i, target(i)) for i in range(lax.axis_size(ax...]
    ppermute x8 -> x10, starting transfers between devices: 10.1 us -> 13.7 us  [moved(): lax.ppermute(shard, axis, [(i, target(i)) for i in range(lax.axis_size(ax...]
    slice x6 -> x0, local copies, waits for them, and re-layouts: 1.36 us -> none  [edges_along_z(): slabs = jnp.concatenate([part[FIELDS * geo.lx:] for part in parts])]
    pallas_call x4 -> x6, Pallas kernels: 4.3 us -> 3.34 us  [call(): pl.pallas_call(kernel, out_shape=outs, in_specs=[smem] * len(parameters)...]
    unnamed x11 -> x22, local copies, waits for them, and re-layouts: 0.96 us -> 0.7 us
  transfers between devices with their start and end apart: 10 -> 10, of which waited for: 7 -> 6; matrix products, arithmetic and copies ran while one was open for 5% -> 0% of each run, Pallas kernels for 3% -> 3%
where the time goes in v5:
time: 28.8 us; the launch traced here: 28.7 us
  starting transfers between devices  13.7 us (48%)
  waiting for transfers between devices  10.1 us (35%)
  Pallas kernels  3.34 us (12%)
  between operations  0.78 us (3%)
  local copies, waits for them, and re-layouts  0.7 us (2%)
    ppermute x10, starting transfers between devices, moved(): lax.ppermute(shard, axis, [(i, target(i)) for i in range(lax.axis_size(ax...  13.7 us
    ppermute x10, waiting for transfers between devices, moved(): lax.ppermute(shard, axis, [(i, target(i)) for i in range(lax.axis_size(ax...  10.1 us
    pallas_call x6, Pallas kernels, call(): pl.pallas_call(kernel, out_shape=outs, in_specs=[smem] * len(parameters)...  3.34 us
    unnamed x22, local copies, waits for them, and re-layouts  0.7 us
  transfers between devices with their start and end apart: 10, of which 6 were waited for; matrix products, arithmetic and copies ran while one was open for 0% of the time, Pallas kernels for 3%

profile of v5, /device:TPU:0, one launch (start us, length us, event | category | flops | bytes accessed | tf_op | source)
XLA Modules:
  0.0 28.7 jit_solution(6689350566971297783)
XLA Ops:
  0.7 0.6 %copy-done.1 = f32[3,2,8,128]{3,2,1,0:T(8,128)S(1)} copy-done((f32[3,2,8,128]{3,2,1,0:T(8,128)S(1)}, f32[3,2,8,128]{3,2,1,0:T(8,128)}, u32[]{:S(2)}) %copy-start.1) | copy-done | bytes 24600
  1.4 0.0 copy-done.2
  1.4 0.0 copy-done.7
  1.4 0.0 copy-done.10
  1.4 0.7 %shard_map.147 = (f32[17,8,128]{2,1,0:T(8,128)S(1)}, f32[15,4,128]{2,1,0:T(4,128)S(1)}) custom-call(f32[4,6]{1,0:T(4,128)S(1)} %copy-done.6, f32[4,6]{1,0:T(4,128)S(1)} %copy-done.7, f32[4]{0:T(128)S(1)} %copy-done.8, f32[4]{0:T(128)S(1)} %copy-done.9, f32[4]{0:T(128)S(1)} %copy-done.10, f32[8,128]{1,0:T(8,128)S(1)} %shard_map.146.zeros, ...), custom_call_target="tpu_custom_call" | custom-call | bytes 178176 | tf_op jit(solution)/shard_map/pallas_call | solution.py:342
  2.2 3.0 %collective-permute-start = (f32[17,8,128]{2,1,0:T(8,128)S(1)}, f32[17,8,128]{2,1,0:T(8,128)S(1)}, u32[]{:S(2)}, u32[]{:S(2)}) collective-permute-start(f32[17,8,128]{2,1,0:T(8,128)S(1)} %get-tuple-element.18.refs_0_), channel_id=1, source_target_pairs={{0,4},{4,0},{8,12},{12,8},{16,20},{20,16},{24,28},{28,24},{1,5},{5... | collective-permute-start | bytes 208904 | tf_op jit(solution)/shard_map/ppermute | solution.py:354
  5.2 1.5 %collective-permute-start.1 = (f32[17,8,128]{2,1,0:T(8,128)S(1)}, f32[17,8,128]{2,1,0:T(8,128)S(1)}, u32[]{:S(2)}, u32[]{:S(2)}) collective-permute-start(f32[17,8,128]{2,1,0:T(8,128)S(1)} %get-tuple-element.18.refs_0_), channel_id=1, source_target_pairs={{0,16},{4,20},{8,24},{12,28},{16,0},{20,4},{24,8},{28,12},{1,17},{... | collective-permute-start | bytes 208904 | tf_op jit(solution)/shard_map/ppermute | solution.py:354
  6.7 0.0 collective-permute-start.2
  6.7 0.9 %collective-permute-done.refs_1_ = f32[17,8,128]{2,1,0:T(8,128)S(1)} collective-permute-done((f32[17,8,128]{2,1,0:T(8,128)S(1)}, f32[17,8,128]{2,1,0:T(8,128)S(1)}, u32[]{:S(2)}, u32[]{:S(2)}) %collective-permute-start) | collective-permute-done | bytes 69664 | tf_op jit(solution)/shard_map/ppermute | solution.py:354
  7.6 1.9 %collective-permute-done.1.refs_2_ = f32[17,8,128]{2,1,0:T(8,128)S(1)} collective-permute-done((f32[17,8,128]{2,1,0:T(8,128)S(1)}, f32[17,8,128]{2,1,0:T(8,128)S(1)}, u32[]{:S(2)}, u32[]{:S(2)}) %collective-permute-start.1) | collective-permute-done | bytes 69664 | tf_op jit(solution)/shard_map/ppermute | solution.py:354
  9.5 2.4 %collective-permute-done.2.refs_3_ = f32[17,8,128]{2,1,0:T(8,128)S(1)} collective-permute-done((f32[17,8,128]{2,1,0:T(8,128)S(1)}, f32[17,8,128]{2,1,0:T(8,128)S(1)}, u32[]{:S(2)}, u32[]{:S(2)}) %collective-permute-start.2) | collective-permute-done | bytes 69664 | tf_op jit(solution)/shard_map/ppermute | solution.py:354
  11.9 0.1 collective-permute-start.5
  12.0 1.6 %collective-permute-start.3 = (f32[4,8,128]{2,1,0:T(8,128)S(1)}, f32[4,8,128]{2,1,0:T(8,128)S(1)}, u32[]{:S(2)}, u32[]{:S(2)}) collective-permute-start(f32[4,8,128]{2,1,0:T(8,128)S(1)} %get-tuple-element.20), channel_id=1, source_target_pairs={{0,1},{1,2},{2,3},{3,0},{4,5},{5,6},{6,7},{7,4},{8,9},{9,10},{10,1... | collective-permute-start | bytes 49160 | tf_op jit(solution)/shard_map/ppermute | solution.py:354
  13.6 2.2 %collective-permute-start.4 = (f32[4,8,128]{2,1,0:T(8,128)S(1)}, f32[4,8,128]{2,1,0:T(8,128)S(1)}, u32[]{:S(2)}, u32[]{:S(2)}) collective-permute-start(f32[4,8,128]{2,1,0:T(8,128)S(1)} %get-tuple-element.20), channel_id=1, source_target_pairs={{0,3},{1,0},{2,1},{3,2},{4,7},{5,4},{6,5},{7,6},{8,11},{9,8},{10,9... | collective-permute-start | bytes 49160 | tf_op jit(solution)/shard_map/ppermute | solution.py:354
  15.9 1.8 %collective-permute-done.3 = f32[4,8,128]{2,1,0:T(8,128)S(1)} collective-permute-done((f32[4,8,128]{2,1,0:T(8,128)S(1)}, f32[4,8,128]{2,1,0:T(8,128)S(1)}, u32[]{:S(2)}, u32[]{:S(2)}) %collective-permute-start.3) | collective-permute-done | bytes 16416 | tf_op jit(solution)/shard_map/ppermute | solution.py:354
  17.7 0.0 collective-permute-done.4
  17.7 1.2 %collective-permute-done.6.refs_4_.refs_6_ = f32[2,4,1,8,128]{4,3,2,1,0:T(8,128)S(1)} collective-permute-done((f32[2,4,1,8,128]{4,3,2,1,0:T(8,128)S(1)}, f32[2,4,1,8,128]{4,3,2,1,0:T(8,128)S(1)}, u32[]{:S(2)}, u32[]{:S(2)}) %collective-permute-start.6) | collective-permute-done | bytes 32800 | tf_op jit(solution)/shard_map/ppermute | solution.py:354
  18.9 0.9 %shard_map.149 = (f32[5,2,8,128]{3,2,1,0:T(8,128)S(1)}, f32[6,2,8,128]{3,2,1,0:T(8,128)S(1)}, f32[16,128]{1,0:T(8,128)S(1)}) custom-call(f32[15,4,128]{2,1,0:T(4,128)S(1)} %get-tuple-element.17.refs_0_, f32[4,17,8,128]{3,2,1,0:T(8,128)S(1)} %bitcast.3, f32[2,4,1,8,128]{4,3,2,1,0:T(8,128)S(1)} %bitcast.8, f32[4,17,8,128]{3,2,1,0:T(8,128)S(1)} %bitcast.5, ...), custom_call_target="tpu_custom_call" | custom-call | flops 8192000 | bytes 751616 | tf_op jit(solution)/shard_map/pallas_call | solution.py:342
  19.9 1.3 %collective-permute-start.7 = (f32[16,128]{1,0:T(8,128)S(1)}, f32[16,128]{1,0:T(8,128)S(1)}, u32[]{:S(2)}, u32[]{:S(2)}) collective-permute-start(f32[16,128]{1,0:T(8,128)S(1)} %get-tuple-element.26.refs_0_), channel_id=1, source_target_pairs={{0,1},{1,2},{2,3},{3,0},{4,5},{5,6},{6,7},{7,4},{8,9},{9,10},{10,1... | collective-permute-start | bytes 24584 | tf_op jit(solution)/shard_map/ppermute | solution.py:354
  21.1 3.0 %collective-permute-start.8 = (f32[16,128]{1,0:T(8,128)S(1)}, f32[16,128]{1,0:T(8,128)S(1)}, u32[]{:S(2)}, u32[]{:S(2)}) collective-permute-start(f32[16,128]{1,0:T(8,128)S(1)} %get-tuple-element.26.refs_0_), channel_id=1, source_target_pairs={{0,2},{1,3},{2,0},{3,1},{4,6},{5,7},{6,4},{7,5},{8,10},{9,11},{10,... | collective-permute-start | bytes 24584 | tf_op jit(solution)/shard_map/ppermute | solution.py:354
  24.2 0.9 %collective-permute-start.9 = (f32[16,128]{1,0:T(8,128)S(1)}, f32[16,128]{1,0:T(8,128)S(1)}, u32[]{:S(2)}, u32[]{:S(2)}) collective-permute-start(f32[16,128]{1,0:T(8,128)S(1)} %get-tuple-element.26.refs_0_), channel_id=1, source_target_pairs={{0,3},{1,0},{2,1},{3,2},{4,7},{5,4},{6,5},{7,6},{8,11},{9,8},{10,9... | collective-permute-start | bytes 24584 | tf_op jit(solution)/shard_map/ppermute | solution.py:354
  25.1 0.8 %shard_map.150 = (f32[6,2,8,128]{3,2,1,0:T(8,128)}, f32[6,6,2,8,128]{4,3,2,1,0:T(8,128)}, f32[2,8,128]{2,1,0:T(8,128)}) custom-call(f32[15,4,128]{2,1,0:T(4,128)S(1)} %get-tuple-element.17.refs_0_, f32[6,2,8,128]{3,2,1,0:T(8,128)S(1)} %get-tuple-element.21.refs_1_, f32[6,6,2,8,128]{4,3,2,1,0:T(8,128)S(1)} %copy-done, f32[4,17,8,128]{3,2,1,0:T(8,128)S(1)} %bitcast.4, ...), custom_call_target="tpu_custom_call" | custom-call | flops 1024000 | bytes 1349632 | tf_op jit(solution)/shard_map/pallas_call | solution.py:342
  25.9 1.9 %collective-permute-done.9.refs_3_ = f32[16,128]{1,0:T(8,128)S(1)} collective-permute-done((f32[16,128]{1,0:T(8,128)S(1)}, f32[16,128]{1,0:T(8,128)S(1)}, u32[]{:S(2)}, u32[]{:S(2)}) %collective-permute-start.9) | collective-permute-done | bytes 8224 | tf_op jit(solution)/shard_map/ppermute | solution.py:354
  27.8 0.8 %shard_map.151 = (f32[2,8,128]{2,1,0:T(8,128)}, f32[2,8,128]{2,1,0:T(8,128)}) custom-call(f32[5,2,8,128]{3,2,1,0:T(8,128)S(1)} %get-tuple-element.25.basis, f32[16,128]{1,0:T(8,128)S(1)} %get-tuple-element.26.refs_0_, f32[16,128]{1,0:T(8,128)S(1)} %collective-permute-done.7.refs_1_, f32[16,128]{1,0:T(8,128)S(1)} %collective-permute-done.8.refs_2_, ...), custom_call_target="tpu_custom_call" | custom-call | bytes 90112 | tf_op jit(solution)/shard_map/pallas_call | solution.py:342
  (25 shorter events, 0.1 us)
Async XLA Ops:
  0.6 0.7 %copy-start.1 = (f32[3,2,8,128]{3,2,1,0:T(8,128)S(1)}, f32[3,2,8,128]{3,2,1,0:T(8,128)}, u32[]{:S(2)}) copy-start(f32[3,2,8,128]{3,2,1,0:T(8,128)} %new.1) | copy-start | bytes 73732
  0.6 0.7 %copy-start.2 = (f32[3,2,8,128]{3,2,1,0:T(8,128)S(1)}, f32[3,2,8,128]{3,2,1,0:T(8,128)}, u32[]{:S(2)}) copy-start(f32[3,2,8,128]{3,2,1,0:T(8,128)} %old.1) | copy-start | bytes 73732
  0.7 0.7 %copy-start.3 = (f32[2,8,128]{2,1,0:T(8,128)S(1)}, f32[2,8,128]{2,1,0:T(8,128)}, u32[]{:S(2)}) copy-start(f32[2,8,128]{2,1,0:T(8,128)} %energy_max.1) | copy-start | bytes 24580
  0.7 0.7 %copy-start.4 = (s32[2,8,128]{2,1,0:T(8,128)S(1)}, s32[2,8,128]{2,1,0:T(8,128)}, u32[]{:S(2)}) copy-start(s32[2,8,128]{2,1,0:T(8,128)} %region.1) | copy-start | bytes 24580
  0.7 0.7 %copy-start.5 = (s32[2,8,128]{2,1,0:T(8,128)S(1)}, s32[2,8,128]{2,1,0:T(8,128)}, u32[]{:S(2)}) copy-start(s32[2,8,128]{2,1,0:T(8,128)} %dirichlet.1) | copy-start | bytes 24580
  0.7 0.7 %copy-start.6 = (f32[4,6]{1,0:T(4,128)S(1)}, f32[4,6]{1,0:T(4,128)}, u32[]{:S(2)}) copy-start(f32[4,6]{1,0:T(4,128)} %moduli.1) | copy-start | bytes 292
  0.7 0.7 %copy-start.7 = (f32[4,6]{1,0:T(4,128)S(1)}, f32[4,6]{1,0:T(4,128)}, u32[]{:S(2)}) copy-start(f32[4,6]{1,0:T(4,128)} %times.1) | copy-start | bytes 292
  0.7 0.7 %copy-start.8 = (f32[4]{0:T(128)S(1)}, f32[4]{0:T(128)}, u32[]{:S(2)}) copy-start(f32[4]{0:T(128)} %shear.1) | copy-start | bytes 52
  0.7 0.7 %copy-start.9 = (f32[4]{0:T(128)S(1)}, f32[4]{0:T(128)}, u32[]{:S(2)}) copy-start(f32[4]{0:T(128)} %ratio.1) | copy-start | bytes 52
  0.7 0.7 %copy-start.10 = (f32[4]{0:T(128)S(1)}, f32[4]{0:T(128)}, u32[]{:S(2)}) copy-start(f32[4]{0:T(128)} %scale.1) | copy-start | bytes 52
  2.2 5.4 %collective-permute-start = (f32[17,8,128]{2,1,0:T(8,128)S(1)}, f32[17,8,128]{2,1,0:T(8,128)S(1)}, u32[]{:S(2)}, u32[]{:S(2)}) collective-permute-start(f32[17,8,128]{2,1,0:T(8,128)S(1)} %get-tuple-element.18.refs_0_), channel_id=1, source_target_pairs={{0,4},{4,0},{8,12},{12,8},{16,20},{20,16},{24,28},{28,24},{1,5},{5... | collective-permute-start | bytes 208904 | tf_op jit(solution)/shard_map/ppermute | solution.py:354
  5.2 4.3 %collective-permute-start.1 = (f32[17,8,128]{2,1,0:T(8,128)S(1)}, f32[17,8,128]{2,1,0:T(8,128)S(1)}, u32[]{:S(2)}, u32[]{:S(2)}) collective-permute-start(f32[17,8,128]{2,1,0:T(8,128)S(1)} %get-tuple-element.18.refs_0_), channel_id=1, source_target_pairs={{0,16},{4,20},{8,24},{12,28},{16,0},{20,4},{24,8},{28,12},{1,17},{... | collective-permute-start | bytes 208904 | tf_op jit(solution)/shard_map/ppermute | solution.py:354
  6.7 5.2 %collective-permute-start.2 = (f32[17,8,128]{2,1,0:T(8,128)S(1)}, f32[17,8,128]{2,1,0:T(8,128)S(1)}, u32[]{:S(2)}, u32[]{:S(2)}) collective-permute-start(f32[17,8,128]{2,1,0:T(8,128)S(1)} %get-tuple-element.18.refs_0_), channel_id=1, source_target_pairs={{0,20},{4,16},{8,28},{12,24},{16,4},{20,0},{24,12},{28,8},{1,21},{... | collective-permute-start | bytes 208904 | tf_op jit(solution)/shard_map/ppermute | solution.py:354
  11.9 7.0 %collective-permute-start.5 = (f32[68,8,128]{2,1,0:T(8,128)S(1)}, f32[68,8,128]{2,1,0:T(8,128)S(1)}, u32[]{:S(2)}, u32[]{:S(2)}) collective-permute-start(f32[68,8,128]{2,1,0:T(8,128)S(1)} %get-tuple-element.19), channel_id=1, source_target_pairs={{0,8},{8,0},{16,24},{24,16},{1,9},{9,1},{17,25},{25,17},{2,10},{10... | collective-permute-start | bytes 835592 | tf_op jit(solution)/shard_map/ppermute | solution.py:354
  12.0 5.7 %collective-permute-start.3 = (f32[4,8,128]{2,1,0:T(8,128)S(1)}, f32[4,8,128]{2,1,0:T(8,128)S(1)}, u32[]{:S(2)}, u32[]{:S(2)}) collective-permute-start(f32[4,8,128]{2,1,0:T(8,128)S(1)} %get-tuple-element.20), channel_id=1, source_target_pairs={{0,1},{1,2},{2,3},{3,0},{4,5},{5,6},{6,7},{7,4},{8,9},{9,10},{10,1... | collective-permute-start | bytes 49160 | tf_op jit(solution)/shard_map/ppermute | solution.py:354
  13.6 4.1 %collective-permute-start.4 = (f32[4,8,128]{2,1,0:T(8,128)S(1)}, f32[4,8,128]{2,1,0:T(8,128)S(1)}, u32[]{:S(2)}, u32[]{:S(2)}) collective-permute-start(f32[4,8,128]{2,1,0:T(8,128)S(1)} %get-tuple-element.20), channel_id=1, source_target_pairs={{0,3},{1,0},{2,1},{3,2},{4,7},{5,4},{6,5},{7,6},{8,11},{9,8},{10,9... | collective-permute-start | bytes 49160 | tf_op jit(solution)/shard_map/ppermute | solution.py:354
  17.7 1.2 %collective-permute-start.6 = (f32[2,4,1,8,128]{4,3,2,1,0:T(8,128)S(1)}, f32[2,4,1,8,128]{4,3,2,1,0:T(8,128)S(1)}, u32[]{:S(2)}, u32[]{:S(2)}) collective-permute-start(f32[2,4,1,8,128]{4,3,2,1,0:T(8,128)S(1)} %bitcast.7), channel_id=1, source_target_pairs={{0,8},{8,0},{16,24},{24,16},{1,9},{9,1},{17,25},{25,17},{2,10},{10... | collective-permute-start | bytes 98312 | tf_op jit(solution)/shard_map/ppermute | solution.py:354
  18.9 6.2 %copy-start = (f32[6,6,2,8,128]{4,3,2,1,0:T(8,128)S(1)}, f32[6,6,2,8,128]{4,3,2,1,0:T(8,128)}, u32[]{:S(2)}) copy-start(f32[6,6,2,8,128]{4,3,2,1,0:T(8,128)} %refs_2_.1) | copy-start | bytes 884740
  19.9 6.1 %collective-permute-start.7 = (f32[16,128]{1,0:T(8,128)S(1)}, f32[16,128]{1,0:T(8,128)S(1)}, u32[]{:S(2)}, u32[]{:S(2)}) collective-permute-start(f32[16,128]{1,0:T(8,128)S(1)} %get-tuple-element.26.refs_0_), channel_id=1, source_target_pairs={{0,1},{1,2},{2,3},{3,0},{4,5},{5,6},{6,7},{7,4},{8,9},{9,10},{10,1... | collective-permute-start | bytes 24584 | tf_op jit(solution)/shard_map/ppermute | solution.py:354
  21.1 4.8 %collective-permute-start.8 = (f32[16,128]{1,0:T(8,128)S(1)}, f32[16,128]{1,0:T(8,128)S(1)}, u32[]{:S(2)}, u32[]{:S(2)}) collective-permute-start(f32[16,128]{1,0:T(8,128)S(1)} %get-tuple-element.26.refs_0_), channel_id=1, source_target_pairs={{0,2},{1,3},{2,0},{3,1},{4,6},{5,7},{6,4},{7,5},{8,10},{9,11},{10,... | collective-permute-start | bytes 24584 | tf_op jit(solution)/shard_map/ppermute | solution.py:354
  24.2 3.7 %collective-permute-start.9 = (f32[16,128]{1,0:T(8,128)S(1)}, f32[16,128]{1,0:T(8,128)S(1)}, u32[]{:S(2)}, u32[]{:S(2)}) collective-permute-start(f32[16,128]{1,0:T(8,128)S(1)} %get-tuple-element.26.refs_0_), channel_id=1, source_target_pairs={{0,3},{1,0},{2,1},{3,2},{4,7},{5,4},{6,5},{7,6},{8,11},{9,8},{10,9... | collective-permute-start | bytes 24584 | tf_op jit(solution)/shard_map/ppermute | solution.py:354

commit v6 on v5

--- a/solution.py
+++ b/solution.py
@@ -40,6 +40,10 @@
     def by(self):
         return self.gy if self.full else 2 * self.hops_y + 1
 
+    @property
+    def split(self):
+        return self.full and self.gx > 1
+
     def beside(self, code, step, index_x):
         if not self.full:
             return (code + step) % self.bx
@@ -73,9 +77,7 @@
     zeros[...] = jnp.zeros(zeros.shape, jnp.float32)
 
 
-def pack_kernel(
-    geo, moduli, times, shear, ratio, scale, zeros, new, old, energy_max, region, dirichlet, payload, tables
-):
+def pack_kernel(geo, zeros, new, old, energy_max, region, dirichlet, payload):
     spots, tiles = places(geo)
     lane = iota((geo.ly, geo.lz), 1)
     edges = [zeros[...]] * tiles
@@ -91,12 +93,15 @@
             edges[tile] = jnp.where(inside, pltpu.roll(value, centre, 1), edges[tile])
     for tile in range(tiles):
         payload[FIELDS * geo.lx + tile] = edges[tile]
+
+
+def tables_kernel(moduli, times, shear, ratio, scale, tables):
     regions, terms = moduli.shape
     for r in range(regions):
         entries = [shear[r], ratio[r], scale[r]]
         entries += [moduli[r, k] for k in range(terms)] + [times[r, k] for k in range(terms)]
         for k, entry in enumerate(entries):
-            tables[k, r : r + 1, :] = jnp.full((1, geo.lz), entry, jnp.float32)
+            tables[k, r : r + 1, :] = jnp.full((1, tables.shape[2]), entry, jnp.float32)
 
 
 SHEAR, RATIO, SCALE, MODULI = range(4)
@@ -134,8 +139,14 @@
     return 1.0 - lax.erf((energy_next - energy) / scale) / ratio
 
 
+def z_edges(geo, halos, array, at, tile):
+    count = halos[0].shape[0] // (2 if geo.split else 1)
+    theirs = 1 - array if geo.split else array
+    return halos[0][array * count + at, tile], halos[1][theirs * count + at, tile]
+
+
 def basis_kernel(geo, where, *refs):
-    tables, blocks, halos = refs[0], refs[1:-5:2], refs[2:-5:2]
+    tables, halos, blocks = refs[0], refs[1:3], refs[3:-5]
     basis, dev_own, grams, held, field = refs[-5:]
     lx, ly, lz = geo.lx, geo.ly, geo.lz
     planes, rows, lanes = geo.bx * lx, geo.by * ly, 2 * lz
@@ -151,6 +162,8 @@
     end_z = (lane == lz - 1) & (index_z == geo.gz - 1)
     start_z = (lane == 0) & (index_z == 0)
 
+    upward = (index_x & 1) == 0 if geo.split else True
+
     def next_plane(p):
         return p + 1 if p % lx + 1 < lx else geo.beside(p // lx, 1, index_x) * lx
 
@@ -162,8 +175,8 @@
         parts = []
         for b in range(geo.by):
             array, at = where[p // lx, b]
-            left, right = halos[array][0, at, tile], halos[array][1, at, tile]
-            edge = pltpu.roll(jnp.where(lane[:ly, :lz] < centre, left, right), lz - centre, 1)
+            mine, theirs = z_edges(geo, halos, array, at, tile)
+            edge = pltpu.roll(jnp.where((lane[:ly, :lz] < centre) ^ upward, theirs, mine), lz - centre, 1)
             parts.append(jnp.concatenate([blocks[array][at, f * lx + p % lx], edge], axis=1))
         return jnp.concatenate(parts, axis=0)
 
@@ -221,13 +234,14 @@
 
 
 def visco_kernel(geo, where, *refs):
-    tables, dev_own, visco, blocks, halos = refs[0], refs[1], refs[2], refs[3:-3:2], refs[4:-3:2]
+    tables, dev_own, visco, halos, blocks = refs[0], refs[1], refs[2], refs[3:5], refs[5:-3]
     stress, visco_next, energy_next = refs[-3:]
     lx, ly, lz = geo.lx, geo.ly, geo.lz
     spots, _ = places(geo)
     row, lane = iota((ly, lz), 0), iota((ly, lz), 1)
     index_x, index_y, index_z = (lax.axis_index(name) for name in ("gx", "gy", "gz"))
     regions, terms = tables.shape[1], visco.shape[0]
+    odd = (index_x & 1) == 1
 
     def own(at, code_y=0):
         array, place = where[0, code_y % geo.by]
@@ -257,7 +271,9 @@
             next_y = pltpu.roll(jnp.where(row == 0, first, value), ly - 1, 0)
             prev_y = pltpu.roll(jnp.where(row == ly - 1, last, value), 1, 0)
             tile, centre = spots[at]
-            left, right = halos[0][0, 0, tile], halos[0][1, 0, tile]
+            left, right = z_edges(geo, halos, 0, 0, tile)
+            if geo.split:
+                left, right = jnp.where(odd, right, left), jnp.where(odd, left, right)
             right = jnp.where(index_z == geo.gz - 1, 0.0, pltpu.roll(right, lz - 1 - centre, 1))
             left = jnp.where(index_z == 0, 0.0, pltpu.roll(left, lz + 1 - centre, 1))
             next_z = jnp.where(lane == lz - 1, right, pltpu.roll(value, lz - 1, 1))
@@ -360,11 +376,6 @@
     return jnp.stack([moved(shard, axis, lambda i: (i - step) % count) if step else shard for step in steps])
 
 
-def edges_along_z(slabs, blocks, geo):
-    pair = jnp.concatenate([moved(slabs, "gz", lambda i: (i + step) % geo.gz) for step in (1, -1)])
-    return pair.reshape((2, blocks, -1) + pair.shape[1:])
-
-
 def assemble_kernel(geo, *refs):
     parts, blocks, slabs = refs[:-2], refs[-2], refs[-1]
     size, tiles = parts[0].shape[0], parts[0].shape[0] - FIELDS * geo.lx
@@ -378,8 +389,8 @@
         blocks = ring(ring(payload, "gy", geo.hops_y), "gx", geo.hops_x)
         blocks = blocks.reshape((geo.bx * geo.by,) + payload.shape)
         where = {(x, y): (0, x * geo.by + y) for x in range(geo.bx) for y in range(geo.by)}
-        slabs = blocks[:, FIELDS * geo.lx :].reshape((-1,) + payload.shape[1:])
-        return [blocks, edges_along_z(slabs, blocks.shape[0], geo)], where
+        slabs = blocks[:, FIELDS * geo.lx :]
+        return [moved(slabs, "gz", lambda i: (i + step) % geo.gz) for step in (1, -1)] + [blocks], where
     codes = [(x, y) for x in range(0, geo.gx, 2) for y in range(geo.gy)]
     parts = [payload]
     for x, y in codes[1:]:
@@ -391,14 +402,18 @@
         [shaped(len(parts) * size, *plane), shaped(len(parts) * tiles, *plane)],
         parts,
     )
-    halos = edges_along_z(slabs, len(parts), geo)
     where = {code: (0, place) for place, code in enumerate(codes)}
-    shape = (len(parts),) + payload.shape
-    if geo.gx == 1:
-        return [blocks.reshape(shape), halos], where
+    shape, edge_shape = (len(parts),) + payload.shape, (-1, tiles) + plane
+    if not geo.split:
+        edges = [moved(slabs, "gz", lambda i: (i + step) % geo.gz) for step in (1, -1)]
+        return [edge.reshape(edge_shape) for edge in edges] + [blocks.reshape(shape)], where
     where.update({(x + 1, y): (1, place) for place, (x, y) in enumerate(codes)})
-    other, other_halos = moved(blocks, "gx", lambda i: i ^ 1), moved(halos, "gx", lambda i: i ^ 1)
-    return [blocks.reshape(shape), halos, other.reshape(shape), other_halos], where
+    both = jnp.concatenate([slabs, moved(slabs, "gx", lambda i: i ^ 1)])
+    other = moved(blocks, "gx", lambda i: i ^ 1)
+    mine = moved(both, ("gx", "gz"), lambda i: i - i % geo.gz + (i % geo.gz + 1 - 2 * (i // geo.gz % 2)) % geo.gz)
+    theirs = moved(mine, "gx", lambda i: i ^ 1)
+    edges = [mine.reshape(edge_shape), theirs.reshape(edge_shape)]
+    return edges + [blocks.reshape(shape), other.reshape(shape)], where
 
 
 def summed(terms, axis):
@@ -426,11 +441,17 @@
     _, tiles = places(geo)
     regions, terms = prony_moduli.shape
     (zeros,) = call(first_kernel, [shaped(ly, lz)], [], flops=1 << 34, moved=0)
-    payload, tables = call(
+    (payload,) = call(
         functools.partial(pack_kernel, geo),
-        [shaped(FIELDS * lx + tiles, ly, lz), shaped(MODULI + 2 * terms, regions, lz)],
+        [shaped(FIELDS * lx + tiles, ly, lz)],
         [zeros, displacement, displacement_old, energy_max, region, dirichlet],
+    )
+    (tables,) = call(
+        tables_kernel,
+        [shaped(MODULI + 2 * terms, regions, lz)],
+        [],
         parameters=[prony_moduli, prony_times, shear_modulus, mullins_ratio, mullins_scale],
+        flops=1 << 24,
     )
     blocks, where = gathered(payload, geo)
     planes, rows = geo.bx * lx, geo.by * ly

time: 28.8 us -> 28.4 us (0.986)
  starting transfers between devices: 13.7 us -> 10.6 us
  waiting for transfers between devices: 10.1 us -> 12.7 us
    ppermute x10, starting transfers between devices: 13.7 us -> 10.6 us  [moved(): lax.ppermute(shard, axis, [(i, target(i)) for i in range(lax.axis_size(ax...]
    ppermute x10, waiting for transfers between devices: 10.1 us -> 12.7 us  [moved(): lax.ppermute(shard, axis, [(i, target(i)) for i in range(lax.axis_size(ax...]
    pallas_call x6 -> x7, Pallas kernels: 3.34 us -> 3.39 us  [call(): pl.pallas_call(kernel, out_shape=outs, in_specs=[smem] * len(parameters)...]
  transfers between devices with their start and end apart: 10 -> 10, of which waited for: 6 -> 8; matrix products, arithmetic and copies ran while one was open for 0% -> 0% of each run, Pallas kernels for 3% -> 5%
where the time goes in v6:
time: 28.4 us; the launch traced here: 28.2 us
  waiting for transfers between devices  12.7 us (45%)
  starting transfers between devices  10.6 us (37%)
  Pallas kernels  3.39 us (12%)
  between operations  0.8 us (3%)
  local copies, waits for them, and re-layouts  0.75 us (3%)
    ppermute x10, waiting for transfers between devices, moved(): lax.ppermute(shard, axis, [(i, target(i)) for i in range(lax.axis_size(ax...  12.7 us
    ppermute x10, starting transfers between devices, moved(): lax.ppermute(shard, axis, [(i, target(i)) for i in range(lax.axis_size(ax...  10.6 us
    pallas_call x7, Pallas kernels, call(): pl.pallas_call(kernel, out_shape=outs, in_specs=[smem] * len(parameters)...  3.39 us
    unnamed x22, local copies, waits for them, and re-layouts  0.75 us
  transfers between devices with their start and end apart: 10, of which 8 were waited for; matrix products, arithmetic and copies ran while one was open for 0% of the time, Pallas kernels for 5%

profile of v6, /device:TPU:0, one launch (start us, length us, event | category | flops | bytes accessed | tf_op | source)
XLA Modules:
  0.0 28.2 jit_solution(16353010954475076594)
XLA Ops:
  0.7 0.7 %copy-done.1 = f32[3,2,8,128]{3,2,1,0:T(8,128)S(1)} copy-done((f32[3,2,8,128]{3,2,1,0:T(8,128)S(1)}, f32[3,2,8,128]{3,2,1,0:T(8,128)}, u32[]{:S(2)}) %copy-start.1) | copy-done | bytes 24600
  1.4 0.0 copy-done.2
  1.4 0.1 shard_map.148.refs_0_
  1.5 3.0 %collective-permute-start = (f32[17,8,128]{2,1,0:T(8,128)S(1)}, f32[17,8,128]{2,1,0:T(8,128)S(1)}, u32[]{:S(2)}, u32[]{:S(2)}) collective-permute-start(f32[17,8,128]{2,1,0:T(8,128)S(1)} %shard_map.148.refs_0_), channel_id=1, source_target_pairs={{0,4},{4,0},{8,12},{12,8},{16,20},{20,16},{24,28},{28,24},{1,5},{5... | collective-permute-start | bytes 208904 | tf_op jit(solution)/shard_map/ppermute | solution.py:370
  4.5 1.5 %collective-permute-start.1 = (f32[17,8,128]{2,1,0:T(8,128)S(1)}, f32[17,8,128]{2,1,0:T(8,128)S(1)}, u32[]{:S(2)}, u32[]{:S(2)}) collective-permute-start(f32[17,8,128]{2,1,0:T(8,128)S(1)} %shard_map.148.refs_0_), channel_id=1, source_target_pairs={{0,16},{4,20},{8,24},{12,28},{16,0},{20,4},{24,8},{28,12},{1,17},{... | collective-permute-start | bytes 208904 | tf_op jit(solution)/shard_map/ppermute | solution.py:370
  6.0 0.0 collective-permute-start.2
  6.0 0.9 %collective-permute-done.refs_1_ = f32[17,8,128]{2,1,0:T(8,128)S(1)} collective-permute-done((f32[17,8,128]{2,1,0:T(8,128)S(1)}, f32[17,8,128]{2,1,0:T(8,128)S(1)}, u32[]{:S(2)}, u32[]{:S(2)}) %collective-permute-start) | collective-permute-done | bytes 69664 | tf_op jit(solution)/shard_map/ppermute | solution.py:370
  6.9 1.9 %collective-permute-done.1.refs_2_ = f32[17,8,128]{2,1,0:T(8,128)S(1)} collective-permute-done((f32[17,8,128]{2,1,0:T(8,128)S(1)}, f32[17,8,128]{2,1,0:T(8,128)S(1)}, u32[]{:S(2)}, u32[]{:S(2)}) %collective-permute-start.1) | collective-permute-done | bytes 69664 | tf_op jit(solution)/shard_map/ppermute | solution.py:370
  8.8 2.4 %collective-permute-done.2.refs_3_ = f32[17,8,128]{2,1,0:T(8,128)S(1)} collective-permute-done((f32[17,8,128]{2,1,0:T(8,128)S(1)}, f32[17,8,128]{2,1,0:T(8,128)S(1)}, u32[]{:S(2)}, u32[]{:S(2)}) %collective-permute-start.2) | collective-permute-done | bytes 69664 | tf_op jit(solution)/shard_map/ppermute | solution.py:370
  11.2 0.1 collective-permute-start.6
  11.4 0.5 %collective-permute-start.3 = (f32[4,8,128]{2,1,0:T(8,128)S(1)}, f32[4,8,128]{2,1,0:T(8,128)S(1)}, u32[]{:S(2)}, u32[]{:S(2)}) collective-permute-start(f32[4,8,128]{2,1,0:T(8,128)S(1)} %get-tuple-element.15), channel_id=1, source_target_pairs={{0,8},{8,0},{16,24},{24,16},{1,9},{9,1},{17,25},{25,17},{2,10},{10... | collective-permute-start | bytes 49160 | tf_op jit(solution)/shard_map/ppermute | solution.py:370
  11.9 1.0 %collective-permute-done.3 = f32[4,8,128]{2,1,0:T(8,128)S(1)} collective-permute-done((f32[4,8,128]{2,1,0:T(8,128)S(1)}, f32[4,8,128]{2,1,0:T(8,128)S(1)}, u32[]{:S(2)}, u32[]{:S(2)}) %collective-permute-start.3) | collective-permute-done | bytes 16416 | tf_op jit(solution)/shard_map/ppermute | solution.py:370
  12.9 1.6 %collective-permute-start.4 = (f32[8,8,128]{2,1,0:T(8,128)S(1)}, f32[8,8,128]{2,1,0:T(8,128)S(1)}, u32[]{:S(2)}, u32[]{:S(2)}) collective-permute-start(f32[8,8,128]{2,1,0:T(8,128)S(1)} %pad_maximum_fusion), channel_id=1, source_target_pairs={{0,1},{1,2},{2,3},{3,0},{8,11},{9,8},{10,9},{11,10},{16,17},{17,18... | collective-permute-start | bytes 98312 | tf_op jit(solution)/shard_map/ppermute | solution.py:370
  14.5 4.1 %collective-permute-done.4 = f32[8,8,128]{2,1,0:T(8,128)S(1)} collective-permute-done((f32[8,8,128]{2,1,0:T(8,128)S(1)}, f32[8,8,128]{2,1,0:T(8,128)S(1)}, u32[]{:S(2)}, u32[]{:S(2)}) %collective-permute-start.4) | collective-permute-done | bytes 32800 | tf_op jit(solution)/shard_map/ppermute | solution.py:370
  18.7 0.6 %shard_map.146.refs_0_ = f32[15,4,128]{2,1,0:T(4,128)S(1)} custom-call(f32[4,6]{1,0:T(4,128)S(1)} %copy-done.6, f32[4,6]{1,0:T(4,128)S(1)} %copy-done.7, f32[4]{0:T(128)S(1)} %copy-done.8, f32[4]{0:T(128)S(1)} %copy-done.9, f32[4]{0:T(128)S(1)} %copy-done.10), custom_call_target="tpu_custom_call" | custom-call | flops 16777216 | bytes 30720 | tf_op jit(solution)/shard_map/pallas_call | solution.py:358
  19.3 0.5 %collective-permute-done.5 = f32[8,8,128]{2,1,0:T(8,128)S(1)} collective-permute-done((f32[8,8,128]{2,1,0:T(8,128)S(1)}, f32[8,8,128]{2,1,0:T(8,128)S(1)}, u32[]{:S(2)}, u32[]{:S(2)}) %collective-permute-start.5) | collective-permute-done | bytes 32800 | tf_op jit(solution)/shard_map/ppermute | solution.py:370
  19.8 1.0 %shard_map.150 = (f32[5,2,8,128]{3,2,1,0:T(8,128)S(1)}, f32[6,2,8,128]{3,2,1,0:T(8,128)S(1)}, f32[16,128]{1,0:T(8,128)S(1)}) custom-call(f32[15,4,128]{2,1,0:T(4,128)S(1)} %shard_map.146.refs_0_, f32[8,1,8,128]{3,2,1,0:T(8,128)S(1)} %bitcast.10, f32[8,1,8,128]{3,2,1,0:T(8,128)S(1)} %bitcast.12, f32[4,17,8,128]{3,2,1,0:T(8,128)S(1)} %bitcast.6, ...), custom_call_target="tpu_custom_call" | custom-call | flops 8192000 | bytes 751616 | tf_op jit(solution)/shard_map/pallas_call | solution.py:358
  20.8 0.1 collective-permute-start.7
  20.9 2.9 %collective-permute-start.8 = (f32[16,128]{1,0:T(8,128)S(1)}, f32[16,128]{1,0:T(8,128)S(1)}, u32[]{:S(2)}, u32[]{:S(2)}) collective-permute-start(f32[16,128]{1,0:T(8,128)S(1)} %get-tuple-element.22.refs_0_), channel_id=1, source_target_pairs={{0,2},{1,3},{2,0},{3,1},{4,6},{5,7},{6,4},{7,5},{8,10},{9,11},{10,... | collective-permute-start | bytes 24584 | tf_op jit(solution)/shard_map/ppermute | solution.py:370
  23.7 1.0 %collective-permute-start.9 = (f32[16,128]{1,0:T(8,128)S(1)}, f32[16,128]{1,0:T(8,128)S(1)}, u32[]{:S(2)}, u32[]{:S(2)}) collective-permute-start(f32[16,128]{1,0:T(8,128)S(1)} %get-tuple-element.22.refs_0_), channel_id=1, source_target_pairs={{0,3},{1,0},{2,1},{3,2},{4,7},{5,4},{6,5},{7,6},{8,11},{9,8},{10,9... | collective-permute-start | bytes 24584 | tf_op jit(solution)/shard_map/ppermute | solution.py:370
  24.7 0.9 %shard_map.151 = (f32[6,2,8,128]{3,2,1,0:T(8,128)}, f32[6,6,2,8,128]{4,3,2,1,0:T(8,128)}, f32[2,8,128]{2,1,0:T(8,128)}) custom-call(f32[15,4,128]{2,1,0:T(4,128)S(1)} %shard_map.146.refs_0_, f32[6,2,8,128]{3,2,1,0:T(8,128)S(1)} %get-tuple-element.17.refs_1_, f32[6,6,2,8,128]{4,3,2,1,0:T(8,128)S(1)} %copy-done, f32[8,1,8,128]{3,2,1,0:T(8,128)S(1)} %bitcast.11, ...), custom_call_target="tpu_custom_call" | custom-call | flops 1024000 | bytes 1349632 | tf_op jit(solution)/shard_map/pallas_call | solution.py:358
  25.5 0.8 %collective-permute-done.7.refs_1_ = f32[16,128]{1,0:T(8,128)S(1)} collective-permute-done((f32[16,128]{1,0:T(8,128)S(1)}, f32[16,128]{1,0:T(8,128)S(1)}, u32[]{:S(2)}, u32[]{:S(2)}) %collective-permute-start.7) | collective-permute-done | bytes 8224 | tf_op jit(solution)/shard_map/ppermute | solution.py:370
  26.3 1.1 %collective-permute-done.9.refs_3_ = f32[16,128]{1,0:T(8,128)S(1)} collective-permute-done((f32[16,128]{1,0:T(8,128)S(1)}, f32[16,128]{1,0:T(8,128)S(1)}, u32[]{:S(2)}, u32[]{:S(2)}) %collective-permute-start.9) | collective-permute-done | bytes 8224 | tf_op jit(solution)/shard_map/ppermute | solution.py:370
  27.4 0.8 %shard_map.152 = (f32[2,8,128]{2,1,0:T(8,128)}, f32[2,8,128]{2,1,0:T(8,128)}) custom-call(f32[5,2,8,128]{3,2,1,0:T(8,128)S(1)} %get-tuple-element.21.basis, f32[16,128]{1,0:T(8,128)S(1)} %get-tuple-element.22.refs_0_, f32[16,128]{1,0:T(8,128)S(1)} %collective-permute-done.7.refs_1_, f32[16,128]{1,0:T(8,128)S(1)} %collective-permute-done.8.refs_2_, ...), custom_call_target="tpu_custom_call" | custom-call | bytes 90112 | tf_op jit(solution)/shard_map/pallas_call | solution.py:358
  (26 shorter events, 0.1 us)
Async XLA Ops:
  0.6 0.7 %copy-start.1 = (f32[3,2,8,128]{3,2,1,0:T(8,128)S(1)}, f32[3,2,8,128]{3,2,1,0:T(8,128)}, u32[]{:S(2)}) copy-start(f32[3,2,8,128]{3,2,1,0:T(8,128)} %new.1) | copy-start | bytes 73732
  0.6 0.7 %copy-start.2 = (f32[3,2,8,128]{3,2,1,0:T(8,128)S(1)}, f32[3,2,8,128]{3,2,1,0:T(8,128)}, u32[]{:S(2)}) copy-start(f32[3,2,8,128]{3,2,1,0:T(8,128)} %old.1) | copy-start | bytes 73732
  0.7 0.7 %copy-start.3 = (f32[2,8,128]{2,1,0:T(8,128)S(1)}, f32[2,8,128]{2,1,0:T(8,128)}, u32[]{:S(2)}) copy-start(f32[2,8,128]{2,1,0:T(8,128)} %energy_max.1) | copy-start | bytes 24580
  0.7 0.7 %copy-start.4 = (s32[2,8,128]{2,1,0:T(8,128)S(1)}, s32[2,8,128]{2,1,0:T(8,128)}, u32[]{:S(2)}) copy-start(s32[2,8,128]{2,1,0:T(8,128)} %region.1) | copy-start | bytes 24580
  0.7 0.7 %copy-start.5 = (s32[2,8,128]{2,1,0:T(8,128)S(1)}, s32[2,8,128]{2,1,0:T(8,128)}, u32[]{:S(2)}) copy-start(s32[2,8,128]{2,1,0:T(8,128)} %dirichlet.1) | copy-start | bytes 24580
  1.5 5.4 %collective-permute-start = (f32[17,8,128]{2,1,0:T(8,128)S(1)}, f32[17,8,128]{2,1,0:T(8,128)S(1)}, u32[]{:S(2)}, u32[]{:S(2)}) collective-permute-start(f32[17,8,128]{2,1,0:T(8,128)S(1)} %shard_map.148.refs_0_), channel_id=1, source_target_pairs={{0,4},{4,0},{8,12},{12,8},{16,20},{20,16},{24,28},{28,24},{1,5},{5... | collective-permute-start | bytes 208904 | tf_op jit(solution)/shard_map/ppermute | solution.py:370
  4.5 4.3 %collective-permute-start.1 = (f32[17,8,128]{2,1,0:T(8,128)S(1)}, f32[17,8,128]{2,1,0:T(8,128)S(1)}, u32[]{:S(2)}, u32[]{:S(2)}) collective-permute-start(f32[17,8,128]{2,1,0:T(8,128)S(1)} %shard_map.148.refs_0_), channel_id=1, source_target_pairs={{0,16},{4,20},{8,24},{12,28},{16,0},{20,4},{24,8},{28,12},{1,17},{... | collective-permute-start | bytes 208904 | tf_op jit(solution)/shard_map/ppermute | solution.py:370
  6.0 5.2 %collective-permute-start.2 = (f32[17,8,128]{2,1,0:T(8,128)S(1)}, f32[17,8,128]{2,1,0:T(8,128)S(1)}, u32[]{:S(2)}, u32[]{:S(2)}) collective-permute-start(f32[17,8,128]{2,1,0:T(8,128)S(1)} %shard_map.148.refs_0_), channel_id=1, source_target_pairs={{0,20},{4,16},{8,28},{12,24},{16,4},{20,0},{24,12},{28,8},{1,21},{... | collective-permute-start | bytes 208904 | tf_op jit(solution)/shard_map/ppermute | solution.py:370
  11.2 8.6 %collective-permute-start.6 = (f32[68,8,128]{2,1,0:T(8,128)S(1)}, f32[68,8,128]{2,1,0:T(8,128)S(1)}, u32[]{:S(2)}, u32[]{:S(2)}) collective-permute-start(f32[68,8,128]{2,1,0:T(8,128)S(1)} %get-tuple-element.16), channel_id=1, source_target_pairs={{0,8},{8,0},{16,24},{24,16},{1,9},{9,1},{17,25},{25,17},{2,10},{10... | collective-permute-start | bytes 835592 | tf_op jit(solution)/shard_map/ppermute | solution.py:370
  11.3 7.3 %copy-start.6 = (f32[4,6]{1,0:T(4,128)S(1)}, f32[4,6]{1,0:T(4,128)}, u32[]{:S(2)}) copy-start(f32[4,6]{1,0:T(4,128)} %moduli.1) | copy-start | bytes 292
  11.3 7.3 %copy-start.7 = (f32[4,6]{1,0:T(4,128)S(1)}, f32[4,6]{1,0:T(4,128)}, u32[]{:S(2)}) copy-start(f32[4,6]{1,0:T(4,128)} %times.1) | copy-start | bytes 292
  11.4 7.3 %copy-start.8 = (f32[4]{0:T(128)S(1)}, f32[4]{0:T(128)}, u32[]{:S(2)}) copy-start(f32[4]{0:T(128)} %shear.1) | copy-start | bytes 52
  11.4 7.3 %copy-start.9 = (f32[4]{0:T(128)S(1)}, f32[4]{0:T(128)}, u32[]{:S(2)}) copy-start(f32[4]{0:T(128)} %ratio.1) | copy-start | bytes 52
  11.4 7.3 %copy-start.10 = (f32[4]{0:T(128)S(1)}, f32[4]{0:T(128)}, u32[]{:S(2)}) copy-start(f32[4]{0:T(128)} %scale.1) | copy-start | bytes 52
  11.4 1.5 %collective-permute-start.3 = (f32[4,8,128]{2,1,0:T(8,128)S(1)}, f32[4,8,128]{2,1,0:T(8,128)S(1)}, u32[]{:S(2)}, u32[]{:S(2)}) collective-permute-start(f32[4,8,128]{2,1,0:T(8,128)S(1)} %get-tuple-element.15), channel_id=1, source_target_pairs={{0,8},{8,0},{16,24},{24,16},{1,9},{9,1},{17,25},{25,17},{2,10},{10... | collective-permute-start | bytes 49160 | tf_op jit(solution)/shard_map/ppermute | solution.py:370
  12.9 5.7 %collective-permute-start.4 = (f32[8,8,128]{2,1,0:T(8,128)S(1)}, f32[8,8,128]{2,1,0:T(8,128)S(1)}, u32[]{:S(2)}, u32[]{:S(2)}) collective-permute-start(f32[8,8,128]{2,1,0:T(8,128)S(1)} %pad_maximum_fusion), channel_id=1, source_target_pairs={{0,1},{1,2},{2,3},{3,0},{8,11},{9,8},{10,9},{11,10},{16,17},{17,18... | collective-permute-start | bytes 98312 | tf_op jit(solution)/shard_map/ppermute | solution.py:370
  18.6 1.2 %collective-permute-start.5 = (f32[8,8,128]{2,1,0:T(8,128)S(1)}, f32[8,8,128]{2,1,0:T(8,128)S(1)}, u32[]{:S(2)}, u32[]{:S(2)}) collective-permute-start(f32[8,8,128]{2,1,0:T(8,128)S(1)} %collective-permute-done.4), channel_id=1, source_target_pairs={{0,8},{8,0},{16,24},{24,16},{1,9},{9,1},{17,25},{25,17},{2,10},{10... | collective-permute-start | bytes 98312 | tf_op jit(solution)/shard_map/ppermute | solution.py:370
  19.8 4.8 %copy-start = (f32[6,6,2,8,128]{4,3,2,1,0:T(8,128)S(1)}, f32[6,6,2,8,128]{4,3,2,1,0:T(8,128)}, u32[]{:S(2)}) copy-start(f32[6,6,2,8,128]{4,3,2,1,0:T(8,128)} %refs_2_.1) | copy-start | bytes 884740
  20.8 5.5 %collective-permute-start.7 = (f32[16,128]{1,0:T(8,128)S(1)}, f32[16,128]{1,0:T(8,128)S(1)}, u32[]{:S(2)}, u32[]{:S(2)}) collective-permute-start(f32[16,128]{1,0:T(8,128)S(1)} %get-tuple-element.22.refs_0_), channel_id=1, source_target_pairs={{0,1},{1,2},{2,3},{3,0},{4,5},{5,6},{6,7},{7,4},{8,9},{9,10},{10,1... | collective-permute-start | bytes 24584 | tf_op jit(solution)/shard_map/ppermute | solution.py:370
  20.9 5.4 %collective-permute-start.8 = (f32[16,128]{1,0:T(8,128)S(1)}, f32[16,128]{1,0:T(8,128)S(1)}, u32[]{:S(2)}, u32[]{:S(2)}) collective-permute-start(f32[16,128]{1,0:T(8,128)S(1)} %get-tuple-element.22.refs_0_), channel_id=1, source_target_pairs={{0,2},{1,3},{2,0},{3,1},{4,6},{5,7},{6,4},{7,5},{8,10},{9,11},{10,... | collective-permute-start | bytes 24584 | tf_op jit(solution)/shard_map/ppermute | solution.py:370
  23.7 3.7 %collective-permute-start.9 = (f32[16,128]{1,0:T(8,128)S(1)}, f32[16,128]{1,0:T(8,128)S(1)}, u32[]{:S(2)}, u32[]{:S(2)}) collective-permute-start(f32[16,128]{1,0:T(8,128)S(1)} %get-tuple-element.22.refs_0_), channel_id=1, source_target_pairs={{0,3},{1,0},{2,1},{3,2},{4,7},{5,4},{6,5},{7,6},{8,11},{9,8},{10,9... | collective-permute-start | bytes 24584 | tf_op jit(solution)/shard_map/ppermute | solution.py:370

commit v7 on v6

--- a/solution.py
+++ b/solution.py
@@ -140,9 +140,8 @@
 
 
 def z_edges(geo, halos, array, at, tile):
-    count = halos[0].shape[0] // (2 if geo.split else 1)
-    theirs = 1 - array if geo.split else array
-    return halos[0][array * count + at, tile], halos[1][theirs * count + at, tile]
+    place = array * (halos[0].shape[0] // (2 if geo.split else 1)) + at
+    return halos[0][place, tile], halos[1][place, tile]
 
 
 def basis_kernel(geo, where, *refs):
@@ -175,8 +174,8 @@
         parts = []
         for b in range(geo.by):
             array, at = where[p // lx, b]
-            mine, theirs = z_edges(geo, halos, array, at, tile)
-            edge = pltpu.roll(jnp.where((lane[:ly, :lz] < centre) ^ upward, theirs, mine), lz - centre, 1)
+            first, second = z_edges(geo, halos, array, at, tile)
+            edge = pltpu.roll(jnp.where((lane[:ly, :lz] < centre) ^ upward, second, first), lz - centre, 1)
             parts.append(jnp.concatenate([blocks[array][at, f * lx + p % lx], edge], axis=1))
         return jnp.concatenate(parts, axis=0)
 
@@ -376,12 +375,20 @@
     return jnp.stack([moved(shard, axis, lambda i: (i - step) % count) if step else shard for step in steps])
 
 
-def assemble_kernel(geo, *refs):
-    parts, blocks, slabs = refs[:-2], refs[-2], refs[-1]
-    size, tiles = parts[0].shape[0], parts[0].shape[0] - FIELDS * geo.lx
+def assemble_kernel(*refs):
+    parts, blocks = refs[:-1], refs[-1]
+    size = parts[0].shape[0]
     for n, part in enumerate(parts):
         blocks[n * size : (n + 1) * size] = part[...]
-        slabs[n * tiles : (n + 1) * tiles] = part[FIELDS * geo.lx :]
+
+
+def slabs_kernel(geo, *refs):
+    arrays, slabs = refs[:-1], refs[-1]
+    place = 0
+    for array in arrays:
+        for n in range(array.shape[0]):
+            slabs[place] = array[n, FIELDS * geo.lx :]
+            place += 1
 
 
 def gathered(payload, geo):
@@ -391,36 +398,36 @@
         where = {(x, y): (0, x * geo.by + y) for x in range(geo.bx) for y in range(geo.by)}
         slabs = blocks[:, FIELDS * geo.lx :]
         return [moved(slabs, "gz", lambda i: (i + step) % geo.gz) for step in (1, -1)] + [blocks], where
-    codes = [(x, y) for x in range(0, geo.gx, 2) for y in range(geo.gy)]
+    codes = [(0, 0)] + [(x, y) for x in range(0, geo.gx, 2) for y in range(geo.gy) if x or y][::-1]
     parts = [payload]
     for x, y in codes[1:]:
         parts.append(moved(payload, ("gx", "gy"), lambda i: (i // geo.gy ^ x) * geo.gy + (i % geo.gy ^ y)))
     size, plane = payload.shape[0], payload.shape[1:]
+    (blocks,) = call(assemble_kernel, [shaped(len(parts) * size, *plane)], parts)
+    where = {code: (0, place) for place, code in enumerate(codes)}
+    arrays = [blocks.reshape((len(parts),) + payload.shape)]
+    if geo.split:
+        where.update({(x + 1, y): (1, place) for place, (x, y) in enumerate(codes)})
+        arrays.append(moved(arrays[0], "gx", lambda i: i ^ 1))
     tiles = size - FIELDS * geo.lx
-    blocks, slabs = call(
-        functools.partial(assemble_kernel, geo),
-        [shaped(len(parts) * size, *plane), shaped(len(parts) * tiles, *plane)],
-        parts,
-    )
-    where = {code: (0, place) for place, code in enumerate(codes)}
-    shape, edge_shape = (len(parts),) + payload.shape, (-1, tiles) + plane
+    (slabs,) = call(functools.partial(slabs_kernel, geo), [shaped(len(arrays) * len(parts), tiles, *plane)], arrays)
     if not geo.split:
-        edges = [moved(slabs, "gz", lambda i: (i + step) % geo.gz) for step in (1, -1)]
-        return [edge.reshape(edge_shape) for edge in edges] + [blocks.reshape(shape)], where
-    where.update({(x + 1, y): (1, place) for place, (x, y) in enumerate(codes)})
-    both = jnp.concatenate([slabs, moved(slabs, "gx", lambda i: i ^ 1)])
-    other = moved(blocks, "gx", lambda i: i ^ 1)
-    mine = moved(both, ("gx", "gz"), lambda i: i - i % geo.gz + (i % geo.gz + 1 - 2 * (i // geo.gz % 2)) % geo.gz)
-    theirs = moved(mine, "gx", lambda i: i ^ 1)
-    edges = [mine.reshape(edge_shape), theirs.reshape(edge_shape)]
-    return edges + [blocks.reshape(shape), other.reshape(shape)], where
+        return [moved(slabs, "gz", lambda i: (i + step) % geo.gz) for step in (1, -1)] + arrays, where
+    ring_of_gz = []
+    for i in range(geo.gx * geo.gz):
+        x, z = divmod(i, geo.gz)
+        ahead = z + 1 - 2 * (x % 2)
+        ring_of_gz.append((i, x * geo.gz + ahead if 0 <= ahead < geo.gz else (x ^ 1) * geo.gz + z))
+    first = lax.ppermute(slabs, ("gx", "gz"), ring_of_gz)
+    second = lax.ppermute(slabs, ("gx", "gz"), [(b, a) for a, b in ring_of_gz])
+    return [first, second] + arrays, where
 
 
 def summed(terms, axis):
     count = lax.axis_size(axis)
-    if count > 4:
+    if count not in (1, 2, 4):
         return [lax.psum(terms, axis)]
-    return [terms] + [moved(terms, axis, lambda i: (i + step) % count) for step in range(1, count)]
+    return [terms] + [moved(terms, axis, lambda i: i ^ step) for step in reversed(range(1, count))]
 
 
 def on_device(

time: 28.4 us -> 26.2 us (0.923)
  waiting for transfers between devices: 12.7 us -> 10.4 us
    ppermute x10 -> x7, waiting for transfers between devices: 12.7 us -> 7.16 us  [moved(): lax.ppermute(shard, axis, [(i, target(i)) for i in range(lax.axis_size(ax...]
    ppermute x0 -> x2, waiting for transfers between devices: none -> 3.21 us  [the longest x1 2.32 us: gathered(): second = lax.ppermute(slabs, ('gx', 'gz'), [(b, a) for a, b in ring_of_gz])]
    ppermute x0 -> x2, starting transfers between devices: none -> 1.58 us  [the longest x1 1.58 us: gathered(): first = lax.ppermute(slabs, ('gx', 'gz'), ring_of_gz)]
    ppermute x10 -> x7, starting transfers between devices: 10.6 us -> 9.13 us  [moved(): lax.ppermute(shard, axis, [(i, target(i)) for i in range(lax.axis_size(ax...]
    pallas_call x7 -> x8, Pallas kernels: 3.39 us -> 3.39 us  [call(): pl.pallas_call(kernel, out_shape=outs, in_specs=[smem] * len(parameters)...]
  transfers between devices with their start and end apart: 10 -> 9, of which waited for: 8 -> 9; matrix products, arithmetic and copies ran while one was open for 0% -> 0% of each run, Pallas kernels for 5% -> 6%
where the time goes in v7:
time: 26.2 us; the launch traced here: 26 us
  starting transfers between devices  10.7 us (41%)
  waiting for transfers between devices  10.4 us (40%)
  Pallas kernels  3.39 us (13%)
  between operations  0.8 us (3%)
  local copies, waits for them, and re-layouts  0.75 us (3%)
    ppermute x7, starting transfers between devices, moved(): lax.ppermute(shard, axis, [(i, target(i)) for i in range(lax.axis_size(ax...  9.13 us
    ppermute x7, waiting for transfers between devices, moved(): lax.ppermute(shard, axis, [(i, target(i)) for i in range(lax.axis_size(ax...  7.16 us
    pallas_call x8, Pallas kernels, call(): pl.pallas_call(kernel, out_shape=outs, in_specs=[smem] * len(parameters)...  3.39 us
    ppermute x1, waiting for transfers between devices, gathered(): second = lax.ppermute(slabs, ('gx', 'gz'), [(b, a) for a, b in ring_of_gz])  2.32 us
    ppermute x1, starting transfers between devices, gathered(): first = lax.ppermute(slabs, ('gx', 'gz'), ring_of_gz)  1.58 us
    ppermute x1, waiting for transfers between devices, gathered(): first = lax.ppermute(slabs, ('gx', 'gz'), ring_of_gz)  0.9 us
    unnamed x22, local copies, waits for them, and re-layouts  0.75 us
  transfers between devices with their start and end apart: 9, of which 9 were waited for; matrix products, arithmetic and copies ran while one was open for 0% of the time, Pallas kernels for 6%

profile of v7, /device:TPU:0, one launch (start us, length us, event | category | flops | bytes accessed | tf_op | source)
XLA Modules:
  0.0 26.0 jit_solution(16651068338723921332)
XLA Ops:
  0.7 0.7 %copy-done.1 = f32[3,2,8,128]{3,2,1,0:T(8,128)S(1)} copy-done((f32[3,2,8,128]{3,2,1,0:T(8,128)S(1)}, f32[3,2,8,128]{3,2,1,0:T(8,128)}, u32[]{:S(2)}) %copy-start.1) | copy-done | bytes 24600
  1.4 0.0 copy-done.2
  1.4 0.1 shard_map.148.refs_0_
  1.5 4.0 %collective-permute-start = (f32[17,8,128]{2,1,0:T(8,128)S(1)}, f32[17,8,128]{2,1,0:T(8,128)S(1)}, u32[]{:S(2)}, u32[]{:S(2)}) collective-permute-start(f32[17,8,128]{2,1,0:T(8,128)S(1)} %shard_map.148.refs_0_), channel_id=1, source_target_pairs={{0,20},{4,16},{8,28},{12,24},{16,4},{20,0},{24,12},{28,8},{1,21},{... | collective-permute-start | bytes 208904 | tf_op jit(solution)/shard_map/ppermute | solution.py:369
  5.5 0.5 %collective-permute-start.1 = (f32[17,8,128]{2,1,0:T(8,128)S(1)}, f32[17,8,128]{2,1,0:T(8,128)S(1)}, u32[]{:S(2)}, u32[]{:S(2)}) collective-permute-start(f32[17,8,128]{2,1,0:T(8,128)S(1)} %shard_map.148.refs_0_), channel_id=1, source_target_pairs={{0,16},{4,20},{8,24},{12,28},{16,0},{20,4},{24,8},{28,12},{1,17},{... | collective-permute-start | bytes 208904 | tf_op jit(solution)/shard_map/ppermute | solution.py:369
  6.0 0.1 collective-permute-start.2
  6.1 1.7 %collective-permute-done.refs_1_ = f32[17,8,128]{2,1,0:T(8,128)S(1)} collective-permute-done((f32[17,8,128]{2,1,0:T(8,128)S(1)}, f32[17,8,128]{2,1,0:T(8,128)S(1)}, u32[]{:S(2)}, u32[]{:S(2)}) %collective-permute-start) | collective-permute-done | bytes 69664 | tf_op jit(solution)/shard_map/ppermute | solution.py:369
  7.8 2.0 %collective-permute-done.1.refs_2_ = f32[17,8,128]{2,1,0:T(8,128)S(1)} collective-permute-done((f32[17,8,128]{2,1,0:T(8,128)S(1)}, f32[17,8,128]{2,1,0:T(8,128)S(1)}, u32[]{:S(2)}, u32[]{:S(2)}) %collective-permute-start.1) | collective-permute-done | bytes 69664 | tf_op jit(solution)/shard_map/ppermute | solution.py:369
  9.8 0.5 %collective-permute-done.2.refs_3_ = f32[17,8,128]{2,1,0:T(8,128)S(1)} collective-permute-done((f32[17,8,128]{2,1,0:T(8,128)S(1)}, f32[17,8,128]{2,1,0:T(8,128)S(1)}, u32[]{:S(2)}, u32[]{:S(2)}) %collective-permute-start.2) | collective-permute-done | bytes 69664 | tf_op jit(solution)/shard_map/ppermute | solution.py:369
  10.4 0.1 collective-permute-start.3
  10.4 1.5 %collective-permute-done.3.refs_1_.refs_4_.refs_6_ = f32[4,17,8,128]{3,2,1,0:T(8,128)S(1)} collective-permute-done((f32[4,17,8,128]{3,2,1,0:T(8,128)S(1)}, f32[4,17,8,128]{3,2,1,0:T(8,128)S(1)}, u32[]{:S(2)}, u32[]{:S(2)}) %collective-permute-start.3) | collective-permute-done | bytes 278560 | tf_op jit(solution)/shard_map/ppermute | solution.py:369
  12.0 1.6 %collective-permute-start.4 = (f32[8,1,8,128]{3,2,1,0:T(8,128)S(1)}, f32[8,1,8,128]{3,2,1,0:T(8,128)S(1)}, u32[]{:S(2)}, u32[]{:S(2)}) collective-permute-start(f32[8,1,8,128]{3,2,1,0:T(8,128)S(1)} %shard_map.150), channel_id=1, source_target_pairs={{0,1},{1,2},{2,3},{3,11},{8,0},{9,8},{10,9},{11,10},{16,17},{17,18... | collective-permute-start | bytes 98312 | tf_op jit(solution)/shard_map/ppermute | solution.py:421
  13.6 0.6 %shard_map.146.refs_0_ = f32[15,4,128]{2,1,0:T(4,128)S(1)} custom-call(f32[4,6]{1,0:T(4,128)S(1)} %copy-done.6, f32[4,6]{1,0:T(4,128)S(1)} %copy-done.7, f32[4]{0:T(128)S(1)} %copy-done.8, f32[4]{0:T(128)S(1)} %copy-done.9, f32[4]{0:T(128)S(1)} %copy-done.10), custom_call_target="tpu_custom_call" | custom-call | flops 16777216 | bytes 30720 | tf_op jit(solution)/shard_map/pallas_call | solution.py:357
  14.3 0.9 %collective-permute-done.4.refs_1_.refs_3_ = f32[8,1,8,128]{3,2,1,0:T(8,128)S(1)} collective-permute-done((f32[8,1,8,128]{3,2,1,0:T(8,128)S(1)}, f32[8,1,8,128]{3,2,1,0:T(8,128)S(1)}, u32[]{:S(2)}, u32[]{:S(2)}) %collective-permute-start.4) | collective-permute-done | bytes 32800 | tf_op jit(solution)/shard_map/ppermute | solution.py:421
  15.2 2.3 %collective-permute-done.5.refs_2_.refs_4_ = f32[8,1,8,128]{3,2,1,0:T(8,128)S(1)} collective-permute-done((f32[8,1,8,128]{3,2,1,0:T(8,128)S(1)}, f32[8,1,8,128]{3,2,1,0:T(8,128)S(1)}, u32[]{:S(2)}, u32[]{:S(2)}) %collective-permute-start.5) | collective-permute-done | bytes 32800 | tf_op jit(solution)/shard_map/ppermute | solution.py:422
  17.5 1.0 %shard_map.151 = (f32[5,2,8,128]{3,2,1,0:T(8,128)S(1)}, f32[6,2,8,128]{3,2,1,0:T(8,128)S(1)}, f32[16,128]{1,0:T(8,128)S(1)}) custom-call(f32[15,4,128]{2,1,0:T(4,128)S(1)} %shard_map.146.refs_0_, f32[8,1,8,128]{3,2,1,0:T(8,128)S(1)} %collective-permute-done.4.refs_1_.refs_3_, f32[8,1,8,128]{3,2,1,0:T(8,128)S(1)} %collective-permute-done.5.refs_2_.refs_4_, ...), custom_call_target="tpu_custom_call" | custom-call | flops 8192000 | bytes 751616 | tf_op jit(solution)/shard_map/pallas_call | solution.py:357
  18.4 2.1 %collective-permute-start.6 = (f32[16,128]{1,0:T(8,128)S(1)}, f32[16,128]{1,0:T(8,128)S(1)}, u32[]{:S(2)}, u32[]{:S(2)}) collective-permute-start(f32[16,128]{1,0:T(8,128)S(1)} %get-tuple-element.18.refs_0_), channel_id=1, source_target_pairs={{0,3},{1,2},{2,1},{3,0},{4,7},{5,6},{6,5},{7,4},{8,11},{9,10},{10,... | collective-permute-start | bytes 24584 | tf_op jit(solution)/shard_map/ppermute | solution.py:369
  20.5 1.0 %collective-permute-start.7 = (f32[16,128]{1,0:T(8,128)S(1)}, f32[16,128]{1,0:T(8,128)S(1)}, u32[]{:S(2)}, u32[]{:S(2)}) collective-permute-start(f32[16,128]{1,0:T(8,128)S(1)} %get-tuple-element.18.refs_0_), channel_id=1, source_target_pairs={{0,2},{1,3},{2,0},{3,1},{4,6},{5,7},{6,4},{7,5},{8,10},{9,11},{10,... | collective-permute-start | bytes 24584 | tf_op jit(solution)/shard_map/ppermute | solution.py:369
  21.5 1.3 %collective-permute-start.8 = (f32[16,128]{1,0:T(8,128)S(1)}, f32[16,128]{1,0:T(8,128)S(1)}, u32[]{:S(2)}, u32[]{:S(2)}) collective-permute-start(f32[16,128]{1,0:T(8,128)S(1)} %get-tuple-element.18.refs_0_), channel_id=1, source_target_pairs={{0,1},{1,0},{2,3},{3,2},{4,5},{5,4},{6,7},{7,6},{8,9},{9,8},{10,11... | collective-permute-start | bytes 24584 | tf_op jit(solution)/shard_map/ppermute | solution.py:369
  22.9 0.9 %shard_map.152 = (f32[6,2,8,128]{3,2,1,0:T(8,128)}, f32[6,6,2,8,128]{4,3,2,1,0:T(8,128)}, f32[2,8,128]{2,1,0:T(8,128)}) custom-call(f32[15,4,128]{2,1,0:T(4,128)S(1)} %shard_map.146.refs_0_, f32[6,2,8,128]{3,2,1,0:T(8,128)S(1)} %get-tuple-element.13.refs_1_, f32[6,6,2,8,128]{4,3,2,1,0:T(8,128)S(1)} %copy-done, ...), custom_call_target="tpu_custom_call" | custom-call | flops 1024000 | bytes 1349632 | tf_op jit(solution)/shard_map/pallas_call | solution.py:357
  23.7 0.2 collective-permute-done.6.refs_1_
  23.9 1.1 %collective-permute-done.7.refs_2_ = f32[16,128]{1,0:T(8,128)S(1)} collective-permute-done((f32[16,128]{1,0:T(8,128)S(1)}, f32[16,128]{1,0:T(8,128)S(1)}, u32[]{:S(2)}, u32[]{:S(2)}) %collective-permute-start.7) | collective-permute-done | bytes 8224 | tf_op jit(solution)/shard_map/ppermute | solution.py:369
  25.1 0.1 collective-permute-done.8.refs_3_
  25.2 0.8 %shard_map.153 = (f32[2,8,128]{2,1,0:T(8,128)}, f32[2,8,128]{2,1,0:T(8,128)}) custom-call(f32[5,2,8,128]{3,2,1,0:T(8,128)S(1)} %get-tuple-element.17.basis, f32[16,128]{1,0:T(8,128)S(1)} %get-tuple-element.18.refs_0_, f32[16,128]{1,0:T(8,128)S(1)} %collective-permute-done.6.refs_1_, f32[16,128]{1,0:T(8,128)S(1)} %collective-permute-done.7.refs_2_, ...), custom_call_target="tpu_custom_call" | custom-call | bytes 90112 | tf_op jit(solution)/shard_map/pallas_call | solution.py:357
  (24 shorter events, 0.1 us)
Async XLA Ops:
  0.6 0.7 %copy-start.1 = (f32[3,2,8,128]{3,2,1,0:T(8,128)S(1)}, f32[3,2,8,128]{3,2,1,0:T(8,128)}, u32[]{:S(2)}) copy-start(f32[3,2,8,128]{3,2,1,0:T(8,128)} %new.1) | copy-start | bytes 73732
  0.6 0.7 %copy-start.2 = (f32[3,2,8,128]{3,2,1,0:T(8,128)S(1)}, f32[3,2,8,128]{3,2,1,0:T(8,128)}, u32[]{:S(2)}) copy-start(f32[3,2,8,128]{3,2,1,0:T(8,128)} %old.1) | copy-start | bytes 73732
  0.7 0.7 %copy-start.3 = (f32[2,8,128]{2,1,0:T(8,128)S(1)}, f32[2,8,128]{2,1,0:T(8,128)}, u32[]{:S(2)}) copy-start(f32[2,8,128]{2,1,0:T(8,128)} %energy_max.1) | copy-start | bytes 24580
  0.7 0.7 %copy-start.4 = (s32[2,8,128]{2,1,0:T(8,128)S(1)}, s32[2,8,128]{2,1,0:T(8,128)}, u32[]{:S(2)}) copy-start(s32[2,8,128]{2,1,0:T(8,128)} %region.1) | copy-start | bytes 24580
  0.7 0.7 %copy-start.5 = (s32[2,8,128]{2,1,0:T(8,128)S(1)}, s32[2,8,128]{2,1,0:T(8,128)}, u32[]{:S(2)}) copy-start(s32[2,8,128]{2,1,0:T(8,128)} %dirichlet.1) | copy-start | bytes 24580
  1.5 6.3 %collective-permute-start = (f32[17,8,128]{2,1,0:T(8,128)S(1)}, f32[17,8,128]{2,1,0:T(8,128)S(1)}, u32[]{:S(2)}, u32[]{:S(2)}) collective-permute-start(f32[17,8,128]{2,1,0:T(8,128)S(1)} %shard_map.148.refs_0_), channel_id=1, source_target_pairs={{0,20},{4,16},{8,28},{12,24},{16,4},{20,0},{24,12},{28,8},{1,21},{... | collective-permute-start | bytes 208904 | tf_op jit(solution)/shard_map/ppermute | solution.py:369
  5.5 4.3 %collective-permute-start.1 = (f32[17,8,128]{2,1,0:T(8,128)S(1)}, f32[17,8,128]{2,1,0:T(8,128)S(1)}, u32[]{:S(2)}, u32[]{:S(2)}) collective-permute-start(f32[17,8,128]{2,1,0:T(8,128)S(1)} %shard_map.148.refs_0_), channel_id=1, source_target_pairs={{0,16},{4,20},{8,24},{12,28},{16,0},{20,4},{24,8},{28,12},{1,17},{... | collective-permute-start | bytes 208904 | tf_op jit(solution)/shard_map/ppermute | solution.py:369
  6.0 4.3 %collective-permute-start.2 = (f32[17,8,128]{2,1,0:T(8,128)S(1)}, f32[17,8,128]{2,1,0:T(8,128)S(1)}, u32[]{:S(2)}, u32[]{:S(2)}) collective-permute-start(f32[17,8,128]{2,1,0:T(8,128)S(1)} %shard_map.148.refs_0_), channel_id=1, source_target_pairs={{0,4},{4,0},{8,12},{12,8},{16,20},{20,16},{24,28},{28,24},{1,5},{5... | collective-permute-start | bytes 208904 | tf_op jit(solution)/shard_map/ppermute | solution.py:369
  10.3 3.3 %copy-start.6 = (f32[4,6]{1,0:T(4,128)S(1)}, f32[4,6]{1,0:T(4,128)}, u32[]{:S(2)}) copy-start(f32[4,6]{1,0:T(4,128)} %moduli.1) | copy-start | bytes 292
  10.3 3.3 %copy-start.7 = (f32[4,6]{1,0:T(4,128)S(1)}, f32[4,6]{1,0:T(4,128)}, u32[]{:S(2)}) copy-start(f32[4,6]{1,0:T(4,128)} %times.1) | copy-start | bytes 292
  10.3 3.3 %copy-start.8 = (f32[4]{0:T(128)S(1)}, f32[4]{0:T(128)}, u32[]{:S(2)}) copy-start(f32[4]{0:T(128)} %shear.1) | copy-start | bytes 52
  10.3 3.3 %copy-start.9 = (f32[4]{0:T(128)S(1)}, f32[4]{0:T(128)}, u32[]{:S(2)}) copy-start(f32[4]{0:T(128)} %ratio.1) | copy-start | bytes 52
  10.3 3.3 %copy-start.10 = (f32[4]{0:T(128)S(1)}, f32[4]{0:T(128)}, u32[]{:S(2)}) copy-start(f32[4]{0:T(128)} %scale.1) | copy-start | bytes 52
  10.4 1.6 %collective-permute-start.3 = (f32[4,17,8,128]{3,2,1,0:T(8,128)S(1)}, f32[4,17,8,128]{3,2,1,0:T(8,128)S(1)}, u32[]{:S(2)}, u32[]{:S(2)}) collective-permute-start(f32[4,17,8,128]{3,2,1,0:T(8,128)S(1)} %bitcast.1), channel_id=1, source_target_pairs={{0,8},{8,0},{16,24},{24,16},{1,9},{9,1},{17,25},{25,17},{2,10},{10... | collective-permute-start | bytes 835592 | tf_op jit(solution)/shard_map/ppermute | solution.py:369
  12.0 3.2 %collective-permute-start.4 = (f32[8,1,8,128]{3,2,1,0:T(8,128)S(1)}, f32[8,1,8,128]{3,2,1,0:T(8,128)S(1)}, u32[]{:S(2)}, u32[]{:S(2)}) collective-permute-start(f32[8,1,8,128]{3,2,1,0:T(8,128)S(1)} %shard_map.150), channel_id=1, source_target_pairs={{0,1},{1,2},{2,3},{3,11},{8,0},{9,8},{10,9},{11,10},{16,17},{17,18... | collective-permute-start | bytes 98312 | tf_op jit(solution)/shard_map/ppermute | solution.py:421
  13.6 3.9 %collective-permute-start.5 = (f32[8,1,8,128]{3,2,1,0:T(8,128)S(1)}, f32[8,1,8,128]{3,2,1,0:T(8,128)S(1)}, u32[]{:S(2)}, u32[]{:S(2)}) collective-permute-start(f32[8,1,8,128]{3,2,1,0:T(8,128)S(1)} %shard_map.150), channel_id=1, source_target_pairs={{1,0},{2,1},{3,2},{11,3},{0,8},{8,9},{9,10},{10,11},{17,16},{18,17... | collective-permute-start | bytes 98312 | tf_op jit(solution)/shard_map/ppermute | solution.py:422
  14.2 8.6 %copy-start = (f32[6,6,2,8,128]{4,3,2,1,0:T(8,128)S(1)}, f32[6,6,2,8,128]{4,3,2,1,0:T(8,128)}, u32[]{:S(2)}) copy-start(f32[6,6,2,8,128]{4,3,2,1,0:T(8,128)} %refs_2_.1) | copy-start | bytes 884740
  18.4 5.5 %collective-permute-start.6 = (f32[16,128]{1,0:T(8,128)S(1)}, f32[16,128]{1,0:T(8,128)S(1)}, u32[]{:S(2)}, u32[]{:S(2)}) collective-permute-start(f32[16,128]{1,0:T(8,128)S(1)} %get-tuple-element.18.refs_0_), channel_id=1, source_target_pairs={{0,3},{1,2},{2,1},{3,0},{4,7},{5,6},{6,5},{7,4},{8,11},{9,10},{10,... | collective-permute-start | bytes 24584 | tf_op jit(solution)/shard_map/ppermute | solution.py:369
  20.5 4.5 %collective-permute-start.7 = (f32[16,128]{1,0:T(8,128)S(1)}, f32[16,128]{1,0:T(8,128)S(1)}, u32[]{:S(2)}, u32[]{:S(2)}) collective-permute-start(f32[16,128]{1,0:T(8,128)S(1)} %get-tuple-element.18.refs_0_), channel_id=1, source_target_pairs={{0,2},{1,3},{2,0},{3,1},{4,6},{5,7},{6,4},{7,5},{8,10},{9,11},{10,... | collective-permute-start | bytes 24584 | tf_op jit(solution)/shard_map/ppermute | solution.py:369
  21.5 3.7 %collective-permute-start.8 = (f32[16,128]{1,0:T(8,128)S(1)}, f32[16,128]{1,0:T(8,128)S(1)}, u32[]{:S(2)}, u32[]{:S(2)}) collective-permute-start(f32[16,128]{1,0:T(8,128)S(1)} %get-tuple-element.18.refs_0_), channel_id=1, source_target_pairs={{0,1},{1,0},{2,3},{3,2},{4,5},{5,4},{6,7},{7,6},{8,9},{9,8},{10,11... | collective-permute-start | bytes 24584 | tf_op jit(solution)/shard_map/ppermute | solution.py:369

commit v8 on v7

--- a/solution.py
+++ b/solution.py
@@ -69,6 +69,20 @@
     return result, tile + 1
 
 
+class Layout(typing.NamedTuple):
+    edges: int
+    rows: int
+    old: int
+    size: int
+
+
+def layout(geo):
+    edges = WIDE * geo.lx
+    rows = edges + places(geo)[1]
+    old = rows - (-NARROW * geo.lx // geo.ly)
+    return Layout(edges, rows, old, old + NARROW * geo.lx)
+
+
 def iota(shape, dim):
     return lax.broadcasted_iota(jnp.int32, shape, dim)
 
@@ -77,22 +91,37 @@
     zeros[...] = jnp.zeros(zeros.shape, jnp.float32)
 
 
-def pack_kernel(geo, zeros, new, old, energy_max, region, dirichlet, payload):
+def pack_kernel(geo, zeros, new, old, energy_max, region, dirichlet, *payloads):
     spots, tiles = places(geo)
-    lane = iota((geo.ly, geo.lz), 1)
-    edges = [zeros[...]] * tiles
+    lay = layout(geo)
+    row, lane = iota((geo.ly, geo.lz), 0), iota((geo.ly, geo.lz), 1)
+    top = lax.axis_index("gy") == 0
+    edges, rows = [zeros[...]] * tiles, [zeros[...]] * (lay.old - lay.rows)
+
+    def write(at, value):
+        for payload in payloads:
+            if at < payload.shape[0]:
+                payload[at] = value
+
     for i in range(geo.lx):
         share = (1 - dirichlet[i]).astype(jnp.float32)
         values = [new[a, i] * share for a in range(3)]
         values += [energy_max[i], region[i].astype(jnp.float32)]
         values += [old[a, i] * share for a in range(3)]
         for f, value in enumerate(values):
-            payload[f * geo.lx + i] = value
-            tile, centre = spots[f * geo.lx + i]
+            at = f * geo.lx + i
+            tile, centre = spots[at]
             inside = (lane >= centre - REACHES[f]) & (lane < centre + REACHES[f])
             edges[tile] = jnp.where(inside, pltpu.roll(value, centre, 1), edges[tile])
-    for tile in range(tiles):
-        payload[FIELDS * geo.lx + tile] = edges[tile]
+            if f < WIDE:
+                write(at, value)
+                continue
+            at -= WIDE * geo.lx
+            write(lay.old + at, value)
+            facing = jnp.where(top, value[geo.ly - 1 :], value[:1])
+            rows[at // geo.ly] = jnp.where(row == at % geo.ly, facing, rows[at // geo.ly])
+    for n, value in enumerate(edges + rows):
+        write(lay.edges + n, value)
 
 
 def tables_kernel(moduli, times, shear, ratio, scale, tables):
@@ -139,9 +168,10 @@
     return 1.0 - lax.erf((energy_next - energy) / scale) / ratio
 
 
-def z_edges(geo, halos, array, at, tile):
-    place = array * (halos[0].shape[0] // (2 if geo.split else 1)) + at
-    return halos[0][place, tile], halos[1][place, tile]
+class Place(typing.NamedTuple):
+    array: int
+    start: int
+    edge: int
 
 
 def basis_kernel(geo, where, *refs):
@@ -173,10 +203,10 @@
         tile, centre = spots[f * lx + p % lx]
         parts = []
         for b in range(geo.by):
-            array, at = where[p // lx, b]
-            first, second = z_edges(geo, halos, array, at, tile)
+            array, start, place = where[p // lx, b]
+            first, second = halos[0][place, tile], halos[1][place, tile]
             edge = pltpu.roll(jnp.where((lane[:ly, :lz] < centre) ^ upward, second, first), lz - centre, 1)
-            parts.append(jnp.concatenate([blocks[array][at, f * lx + p % lx], edge], axis=1))
+            parts.append(jnp.concatenate([blocks[array][start + f * lx + p % lx], edge], axis=1))
         return jnp.concatenate(parts, axis=0)
 
     def beside(value):
@@ -242,35 +272,44 @@
     regions, terms = tables.shape[1], visco.shape[0]
     odd = (index_x & 1) == 1
 
-    def own(at, code_y=0):
-        array, place = where[0, code_y % geo.by]
-        return blocks[array][place, at]
+    lay = layout(geo)
+
+    def of(code, at):
+        array, start, _ = where[code]
+        return blocks[array][start + at]
 
     def along_x(step, at):
         target = geo.beside(0, step, index_x)
         if not geo.full:
-            array, place = where[target, 0]
-            return blocks[array][place, at]
+            return of((target, 0), at)
         value = None
         for code in {geo.beside(0, step, index) for index in range(geo.gx)}:
-            array, place = where[code, 0]
-            found = blocks[array][place, at]
+            found = of((code, 0), at)
             value = found if value is None else jnp.where(target == code, found, value)
         return value
+
+    def rows_along_y(at):
+        if not geo.full:
+            return of((0, 1), lay.old + at)[:1], of((0, geo.by - 1), lay.old + at)[ly - 1 :]
+        if geo.gy == 1:
+            return 0.0, 0.0
+        facing = of((0, 1), lay.rows + at // ly)[at % ly : at % ly + 1]
+        return facing, facing
 
     for i in range(lx):
         grad = []
         for a in range(3):
-            at = (WIDE + a) * lx + i
-            value = own(at)
-            next_x = own(at + 1) if i + 1 < lx else along_x(1, at + 1 - lx)
-            prev_x = own(at - 1) if i else along_x(-1, at + lx - 1)
-            first = jnp.where(index_y == geo.gy - 1, 0.0, own(at, 1))
-            last = jnp.where(index_y == 0, 0.0, own(at, -1))
+            at = lay.old + a * lx + i
+            value = of((0, 0), at)
+            next_x = of((0, 0), at + 1) if i + 1 < lx else along_x(1, at + 1 - lx)
+            prev_x = of((0, 0), at - 1) if i else along_x(-1, at + lx - 1)
+            after, before = rows_along_y(a * lx + i)
+            first = jnp.where(index_y == geo.gy - 1, 0.0, after)
+            last = jnp.where(index_y == 0, 0.0, before)
             next_y = pltpu.roll(jnp.where(row == 0, first, value), ly - 1, 0)
             prev_y = pltpu.roll(jnp.where(row == ly - 1, last, value), 1, 0)
-            tile, centre = spots[at]
-            left, right = z_edges(geo, halos, 0, 0, tile)
+            tile, centre = spots[(WIDE + a) * lx + i]
+            left, right = halos[0][0, tile], halos[1][0, tile]
             if geo.split:
                 left, right = jnp.where(odd, right, left), jnp.where(odd, left, right)
             right = jnp.where(index_z == geo.gz - 1, 0.0, pltpu.roll(right, lz - 1 - centre, 1))
@@ -280,11 +319,11 @@
             grad.append([0.5 * (next_x - prev_x), 0.5 * (next_y - prev_y), 0.5 * (next_z - prev_z)])
         dev_old = deviator(grad)
         dev_new = [dev_own[k, i] for k in range(6)]
-        label = own(4 * lx + i)
+        label = of((0, 0), 4 * lx + i)
         masks = [label == r for r in range(regions - 1)]
         shear_cells, ratio_cells, scale_cells = [lookup(tables, entry, masks) for entry in (SHEAR, RATIO, SCALE)]
         energy = shear_cells * contract(dev_new)
-        energy_after = jnp.maximum(own(3 * lx + i), energy)
+        energy_after = jnp.maximum(of((0, 0), 3 * lx + i), energy)
         energy_next[i] = energy_after
         softening = soften(energy, energy_after, scale_cells, ratio_cells)
         jump = [2.0 * shear_cells * (dev_new[k] - dev_old[k]) for k in range(6)]
@@ -318,14 +357,14 @@
             out[j] = out[j] + LENGTH_SQUARED * p[j - 1]
         return out
 
+    def tree(values):
+        while len(values) > 1:
+            paired = [a + b for a, b in zip(values[::2], values[1::2])]
+            values = paired + values[2 * len(paired) :]
+        return values[0]
+
     def product(u, v):
-        value = None
-        for i in range(len(u)):
-            inner = None
-            for j in range(len(v)):
-                inner = gram[i, j] * v[j] if inner is None else inner + gram[i, j] * v[j]
-            value = u[i] * inner if value is None else value + u[i] * inner
-        return value
+        return tree([u[i] * v[j] * gram[i, j] for i in range(len(u)) for j in range(len(v))])
 
     one = jnp.ones((1, 1), jnp.float32)
     field, rest, direction = [], [one], [one]
@@ -377,40 +416,48 @@
 
 def assemble_kernel(*refs):
     parts, blocks = refs[:-1], refs[-1]
-    size = parts[0].shape[0]
-    for n, part in enumerate(parts):
-        blocks[n * size : (n + 1) * size] = part[...]
-
-
-def slabs_kernel(geo, *refs):
+    start = 0
+    for part in parts:
+        blocks[start : start + part.shape[0]] = part[...]
+        start += part.shape[0]
+
+
+def slabs_kernel(geo, places_of, *refs):
     arrays, slabs = refs[:-1], refs[-1]
-    place = 0
-    for array in arrays:
-        for n in range(array.shape[0]):
-            slabs[place] = array[n, FIELDS * geo.lx :]
-            place += 1
-
-
-def gathered(payload, geo):
+    lay = layout(geo)
+    for array, start, edge in places_of:
+        slabs[edge] = arrays[array][start + lay.edges : start + lay.rows]
+
+
+def gathered(payloads, geo):
+    lay, plane = layout(geo), payloads[0].shape[1:]
     if not geo.full:
-        blocks = ring(ring(payload, "gy", geo.hops_y), "gx", geo.hops_x)
-        blocks = blocks.reshape((geo.bx * geo.by,) + payload.shape)
-        where = {(x, y): (0, x * geo.by + y) for x in range(geo.bx) for y in range(geo.by)}
-        slabs = blocks[:, FIELDS * geo.lx :]
-        return [moved(slabs, "gz", lambda i: (i + step) % geo.gz) for step in (1, -1)] + [blocks], where
+        blocks = ring(ring(payloads[0], "gy", geo.hops_y), "gx", geo.hops_x)
+        blocks = blocks.reshape((geo.bx * geo.by, lay.size) + plane)
+        order = [(x, y) for x in range(geo.bx) for y in range(geo.by)]
+        where = {code: Place(0, n * lay.size, n) for n, code in enumerate(order)}
+        slabs = blocks[:, lay.edges : lay.rows]
+        edges = [moved(slabs, "gz", lambda i: (i + step) % geo.gz) for step in (1, -1)]
+        return edges + [blocks.reshape((-1,) + plane)], where
+    whole, with_rows, plain = payloads
+    relays = {geo.beside(0, step, index) & ~1 for step in (1, -1) for index in range(geo.gx)}
     codes = [(0, 0)] + [(x, y) for x in range(0, geo.gx, 2) for y in range(geo.gy) if x or y][::-1]
-    parts = [payload]
+    parts = [whole]
     for x, y in codes[1:]:
+        payload = whole if not y and x in relays else with_rows if not x else plain
         parts.append(moved(payload, ("gx", "gy"), lambda i: (i // geo.gy ^ x) * geo.gy + (i % geo.gy ^ y)))
-    size, plane = payload.shape[0], payload.shape[1:]
-    (blocks,) = call(assemble_kernel, [shaped(len(parts) * size, *plane)], parts)
-    where = {code: (0, place) for place, code in enumerate(codes)}
-    arrays = [blocks.reshape((len(parts),) + payload.shape)]
+    starts = np.cumsum([0] + [part.shape[0] for part in parts]).tolist()
+    (blocks,) = call(assemble_kernel, [shaped(starts[-1], *plane)], parts)
+    where = {code: Place(0, starts[n], n) for n, code in enumerate(codes)}
+    arrays = [blocks]
     if geo.split:
-        where.update({(x + 1, y): (1, place) for place, (x, y) in enumerate(codes)})
-        arrays.append(moved(arrays[0], "gx", lambda i: i ^ 1))
-    tiles = size - FIELDS * geo.lx
-    (slabs,) = call(functools.partial(slabs_kernel, geo), [shaped(len(arrays) * len(parts), tiles, *plane)], arrays)
+        where.update({(x + 1, y): Place(1, starts[n], len(codes) + n) for n, (x, y) in enumerate(codes)})
+        arrays.append(moved(blocks, "gx", lambda i: i ^ 1))
+    (slabs,) = call(
+        functools.partial(slabs_kernel, geo, tuple(where.values())),
+        [shaped(len(where), lay.rows - lay.edges, *plane)],
+        arrays,
+    )
     if not geo.split:
         return [moved(slabs, "gz", lambda i: (i + step) % geo.gz) for step in (1, -1)] + arrays, where
     ring_of_gz = []
@@ -445,12 +492,12 @@
 ):
     geo = geometry(energy_max.shape)
     lx, ly, lz = energy_max.shape
-    _, tiles = places(geo)
     regions, terms = prony_moduli.shape
     (zeros,) = call(first_kernel, [shaped(ly, lz)], [], flops=1 << 34, moved=0)
-    (payload,) = call(
+    lay = layout(geo)
+    payloads = call(
         functools.partial(pack_kernel, geo),
-        [shaped(FIELDS * lx + tiles, ly, lz)],
+        [shaped(size, ly, lz) for size in ((lay.size, lay.old, lay.rows) if geo.full else (lay.size,))],
         [zeros, displacement, displacement_old, energy_max, region, dirichlet],
     )
     (tables,) = call(
@@ -460,7 +507,7 @@
         parameters=[prony_moduli, prony_times, shear_modulus, mullins_ratio, mullins_scale],
         flops=1 << 24,
     )
-    blocks, where = gathered(payload, geo)
+    blocks, where = gathered(payloads, geo)
     planes, rows = geo.bx * lx, geo.by * ly
     basis, dev_own, grams = call(
         functools.partial(basis_kernel, geo, where),

time: 26.2 us -> 26.9 us (1.027)
  waiting for transfers between devices: 10.4 us -> 11 us
    ppermute x7, waiting for transfers between devices: 7.16 us -> 7.84 us  [moved(): lax.ppermute(shard, axis, [(i, target(i)) for i in range(lax.axis_size(ax...]
  transfers between devices with their start and end apart: 9 -> 9, of which waited for: 9 -> 7; matrix products, arithmetic and copies ran while one was open for 0% -> 0% of each run, Pallas kernels for 6% -> 6%
where the time goes in v8:
time: 26.9 us; the launch traced here: 26.7 us
  waiting for transfers between devices  11 us (41%)
  starting transfers between devices  10.7 us (40%)
  Pallas kernels  3.38 us (13%)
  between operations  0.8 us (3%)
  local copies, waits for them, and re-layouts  0.75 us (3%)
    ppermute x7, starting transfers between devices, moved(): lax.ppermute(shard, axis, [(i, target(i)) for i in range(lax.axis_size(ax...  9.1 us
    ppermute x7, waiting for transfers between devices, moved(): lax.ppermute(shard, axis, [(i, target(i)) for i in range(lax.axis_size(ax...  7.84 us
    pallas_call x8, Pallas kernels, call(): pl.pallas_call(kernel, out_shape=outs, in_specs=[smem] * len(parameters)...  3.38 us
    ppermute x1, waiting for transfers between devices, gathered(): second = lax.ppermute(slabs, ('gx', 'gz'), [(b, a) for a, b in ring_of_gz])  2.32 us
    ppermute x1, starting transfers between devices, gathered(): first = lax.ppermute(slabs, ('gx', 'gz'), ring_of_gz)  1.58 us
    ppermute x1, waiting for transfers between devices, gathered(): first = lax.ppermute(slabs, ('gx', 'gz'), ring_of_gz)  0.9 us
    unnamed x22, local copies, waits for them, and re-layouts  0.75 us
  transfers between devices with their start and end apart: 9, of which 7 were waited for; matrix products, arithmetic and copies ran while one was open for 0% of the time, Pallas kernels for 6%

profile of v8, /device:TPU:0, one launch (start us, length us, event | category | flops | bytes accessed | tf_op | source)
XLA Modules:
  0.0 26.7 jit_solution(8298029127047233918)
XLA Ops:
  0.7 0.7 %copy-done.1 = f32[3,2,8,128]{3,2,1,0:T(8,128)S(1)} copy-done((f32[3,2,8,128]{3,2,1,0:T(8,128)S(1)}, f32[3,2,8,128]{3,2,1,0:T(8,128)}, u32[]{:S(2)}) %copy-start.1) | copy-done | bytes 24600
  1.4 0.0 copy-done.2
  1.4 0.1 shard_map.148
  1.5 3.0 %collective-permute-start.1 = (f32[18,8,128]{2,1,0:T(8,128)S(1)}, f32[18,8,128]{2,1,0:T(8,128)S(1)}, u32[]{:S(2)}, u32[]{:S(2)}) collective-permute-start(f32[18,8,128]{2,1,0:T(8,128)S(1)} %get-tuple-element.16.refs_0_), channel_id=1, source_target_pairs={{0,16},{4,20},{8,24},{12,28},{16,0},{20,4},{24,8},{28,12},{1,17},{... | collective-permute-start | bytes 221192 | tf_op jit(solution)/shard_map/ppermute | solution.py:408
  4.5 1.5 %collective-permute-start.2 = (f32[12,8,128]{2,1,0:T(8,128)S(1)}, f32[12,8,128]{2,1,0:T(8,128)S(1)}, u32[]{:S(2)}, u32[]{:S(2)}) collective-permute-start(f32[12,8,128]{2,1,0:T(8,128)S(1)} %get-tuple-element.18), channel_id=1, source_target_pairs={{0,4},{4,0},{8,12},{12,8},{16,20},{20,16},{24,28},{28,24},{1,5},{5... | collective-permute-start | bytes 147464 | tf_op jit(solution)/shard_map/ppermute | solution.py:408
  6.0 0.0 collective-permute-start
  6.1 4.9 %collective-permute-done.refs_1_ = f32[11,8,128]{2,1,0:T(8,128)S(1)} collective-permute-done((f32[11,8,128]{2,1,0:T(8,128)S(1)}, f32[11,8,128]{2,1,0:T(8,128)S(1)}, u32[]{:S(2)}, u32[]{:S(2)}) %collective-permute-start) | collective-permute-done | bytes 45088 | tf_op jit(solution)/shard_map/ppermute | solution.py:408
  11.0 0.0 copy-start.8
  11.0 0.0 copy-start.9
  11.1 0.1 collective-permute-start.3
  11.1 1.5 %collective-permute-done.3.refs_1_.refs_4_.refs_6_ = f32[59,8,128]{2,1,0:T(8,128)S(1)} collective-permute-done((f32[59,8,128]{2,1,0:T(8,128)S(1)}, f32[59,8,128]{2,1,0:T(8,128)S(1)}, u32[]{:S(2)}, u32[]{:S(2)}) %collective-permute-start.3) | collective-permute-done | bytes 241696 | tf_op jit(solution)/shard_map/ppermute | solution.py:408
  12.6 1.6 %collective-permute-start.4 = (f32[8,1,8,128]{3,2,1,0:T(8,128)S(1)}, f32[8,1,8,128]{3,2,1,0:T(8,128)S(1)}, u32[]{:S(2)}, u32[]{:S(2)}) collective-permute-start(f32[8,1,8,128]{3,2,1,0:T(8,128)S(1)} %shard_map.150), channel_id=1, source_target_pairs={{0,1},{1,2},{2,3},{3,11},{8,0},{9,8},{10,9},{11,10},{16,17},{17,18... | collective-permute-start | bytes 98312 | tf_op jit(solution)/shard_map/ppermute | solution.py:468
  14.2 0.6 %shard_map.146.refs_0_ = f32[15,4,128]{2,1,0:T(4,128)S(1)} custom-call(f32[4,6]{1,0:T(4,128)S(1)} %copy-done.6, f32[4,6]{1,0:T(4,128)S(1)} %copy-done.7, f32[4]{0:T(128)S(1)} %copy-done.8, f32[4]{0:T(128)S(1)} %copy-done.9, f32[4]{0:T(128)S(1)} %copy-done.10), custom_call_target="tpu_custom_call" | custom-call | flops 16777216 | bytes 30720 | tf_op jit(solution)/shard_map/pallas_call | solution.py:396
  14.9 0.9 %collective-permute-done.4.refs_1_.refs_3_ = f32[8,1,8,128]{3,2,1,0:T(8,128)S(1)} collective-permute-done((f32[8,1,8,128]{3,2,1,0:T(8,128)S(1)}, f32[8,1,8,128]{3,2,1,0:T(8,128)S(1)}, u32[]{:S(2)}, u32[]{:S(2)}) %collective-permute-start.4) | collective-permute-done | bytes 32800 | tf_op jit(solution)/shard_map/ppermute | solution.py:468
  15.8 2.3 %collective-permute-done.5.refs_2_.refs_4_ = f32[8,1,8,128]{3,2,1,0:T(8,128)S(1)} collective-permute-done((f32[8,1,8,128]{3,2,1,0:T(8,128)S(1)}, f32[8,1,8,128]{3,2,1,0:T(8,128)S(1)}, u32[]{:S(2)}, u32[]{:S(2)}) %collective-permute-start.5) | collective-permute-done | bytes 32800 | tf_op jit(solution)/shard_map/ppermute | solution.py:469
  18.1 1.0 %shard_map.151 = (f32[5,2,8,128]{3,2,1,0:T(8,128)S(1)}, f32[6,2,8,128]{3,2,1,0:T(8,128)S(1)}, f32[16,128]{1,0:T(8,128)S(1)}) custom-call(f32[15,4,128]{2,1,0:T(4,128)S(1)} %shard_map.146.refs_0_, f32[8,1,8,128]{3,2,1,0:T(8,128)S(1)} %collective-permute-done.4.refs_1_.refs_3_, f32[8,1,8,128]{3,2,1,0:T(8,128)S(1)} %collective-permute-done.5.refs_2_.refs_4_, ...), custom_call_target="tpu_custom_call" | custom-call | flops 8192000 | bytes 677888 | tf_op jit(solution)/shard_map/pallas_call | solution.py:396
  19.1 2.1 %collective-permute-start.6 = (f32[16,128]{1,0:T(8,128)S(1)}, f32[16,128]{1,0:T(8,128)S(1)}, u32[]{:S(2)}, u32[]{:S(2)}) collective-permute-start(f32[16,128]{1,0:T(8,128)S(1)} %get-tuple-element.24.refs_0_), channel_id=1, source_target_pairs={{0,3},{1,2},{2,1},{3,0},{4,7},{5,6},{6,5},{7,4},{8,11},{9,10},{10,... | collective-permute-start | bytes 24584 | tf_op jit(solution)/shard_map/ppermute | solution.py:408
  21.2 1.0 %collective-permute-start.7 = (f32[16,128]{1,0:T(8,128)S(1)}, f32[16,128]{1,0:T(8,128)S(1)}, u32[]{:S(2)}, u32[]{:S(2)}) collective-permute-start(f32[16,128]{1,0:T(8,128)S(1)} %get-tuple-element.24.refs_0_), channel_id=1, source_target_pairs={{0,2},{1,3},{2,0},{3,1},{4,6},{5,7},{6,4},{7,5},{8,10},{9,11},{10,... | collective-permute-start | bytes 24584 | tf_op jit(solution)/shard_map/ppermute | solution.py:408
  22.2 1.3 %collective-permute-start.8 = (f32[16,128]{1,0:T(8,128)S(1)}, f32[16,128]{1,0:T(8,128)S(1)}, u32[]{:S(2)}, u32[]{:S(2)}) collective-permute-start(f32[16,128]{1,0:T(8,128)S(1)} %get-tuple-element.24.refs_0_), channel_id=1, source_target_pairs={{0,1},{1,0},{2,3},{3,2},{4,5},{5,4},{6,7},{7,6},{8,9},{9,8},{10,11... | collective-permute-start | bytes 24584 | tf_op jit(solution)/shard_map/ppermute | solution.py:408
  23.5 0.9 %shard_map.152 = (f32[6,2,8,128]{3,2,1,0:T(8,128)}, f32[6,6,2,8,128]{4,3,2,1,0:T(8,128)}, f32[2,8,128]{2,1,0:T(8,128)}) custom-call(f32[15,4,128]{2,1,0:T(4,128)S(1)} %shard_map.146.refs_0_, f32[6,2,8,128]{3,2,1,0:T(8,128)S(1)} %get-tuple-element.19.refs_1_, f32[6,6,2,8,128]{4,3,2,1,0:T(8,128)S(1)} %copy-done, ...), custom_call_target="tpu_custom_call" | custom-call | flops 1024000 | bytes 1275904 | tf_op jit(solution)/shard_map/pallas_call | solution.py:396
  24.4 0.2 collective-permute-done.6.refs_1_
  24.6 1.1 %collective-permute-done.7.refs_2_ = f32[16,128]{1,0:T(8,128)S(1)} collective-permute-done((f32[16,128]{1,0:T(8,128)S(1)}, f32[16,128]{1,0:T(8,128)S(1)}, u32[]{:S(2)}, u32[]{:S(2)}) %collective-permute-start.7) | collective-permute-done | bytes 8224 | tf_op jit(solution)/shard_map/ppermute | solution.py:408
  25.7 0.1 collective-permute-done.8.refs_3_
  25.8 0.8 %shard_map.153 = (f32[2,8,128]{2,1,0:T(8,128)}, f32[2,8,128]{2,1,0:T(8,128)}) custom-call(f32[5,2,8,128]{3,2,1,0:T(8,128)S(1)} %get-tuple-element.23.basis, f32[16,128]{1,0:T(8,128)S(1)} %get-tuple-element.24.refs_0_, f32[16,128]{1,0:T(8,128)S(1)} %collective-permute-done.6.refs_1_, f32[16,128]{1,0:T(8,128)S(1)} %collective-permute-done.7.refs_2_, ...), custom_call_target="tpu_custom_call" | custom-call | bytes 90112 | tf_op jit(solution)/shard_map/pallas_call | solution.py:396
  (24 shorter events, 0.1 us)
Async XLA Ops:
  0.6 0.7 %copy-start.1 = (f32[3,2,8,128]{3,2,1,0:T(8,128)S(1)}, f32[3,2,8,128]{3,2,1,0:T(8,128)}, u32[]{:S(2)}) copy-start(f32[3,2,8,128]{3,2,1,0:T(8,128)} %new.1) | copy-start | bytes 73732
  0.6 0.7 %copy-start.2 = (f32[3,2,8,128]{3,2,1,0:T(8,128)S(1)}, f32[3,2,8,128]{3,2,1,0:T(8,128)}, u32[]{:S(2)}) copy-start(f32[3,2,8,128]{3,2,1,0:T(8,128)} %old.1) | copy-start | bytes 73732
  0.7 0.7 %copy-start.3 = (f32[2,8,128]{2,1,0:T(8,128)S(1)}, f32[2,8,128]{2,1,0:T(8,128)}, u32[]{:S(2)}) copy-start(f32[2,8,128]{2,1,0:T(8,128)} %energy_max.1) | copy-start | bytes 24580
  0.7 0.7 %copy-start.4 = (s32[2,8,128]{2,1,0:T(8,128)S(1)}, s32[2,8,128]{2,1,0:T(8,128)}, u32[]{:S(2)}) copy-start(s32[2,8,128]{2,1,0:T(8,128)} %region.1) | copy-start | bytes 24580
  0.7 0.7 %copy-start.5 = (s32[2,8,128]{2,1,0:T(8,128)S(1)}, s32[2,8,128]{2,1,0:T(8,128)}, u32[]{:S(2)}) copy-start(s32[2,8,128]{2,1,0:T(8,128)} %dirichlet.1) | copy-start | bytes 24580
  1.5 9.5 %collective-permute-start.1 = (f32[18,8,128]{2,1,0:T(8,128)S(1)}, f32[18,8,128]{2,1,0:T(8,128)S(1)}, u32[]{:S(2)}, u32[]{:S(2)}) collective-permute-start(f32[18,8,128]{2,1,0:T(8,128)S(1)} %get-tuple-element.16.refs_0_), channel_id=1, source_target_pairs={{0,16},{4,20},{8,24},{12,28},{16,0},{20,4},{24,8},{28,12},{1,17},{... | collective-permute-start | bytes 221192 | tf_op jit(solution)/shard_map/ppermute | solution.py:408
  4.5 6.4 %collective-permute-start.2 = (f32[12,8,128]{2,1,0:T(8,128)S(1)}, f32[12,8,128]{2,1,0:T(8,128)S(1)}, u32[]{:S(2)}, u32[]{:S(2)}) collective-permute-start(f32[12,8,128]{2,1,0:T(8,128)S(1)} %get-tuple-element.18), channel_id=1, source_target_pairs={{0,4},{4,0},{8,12},{12,8},{16,20},{20,16},{24,28},{28,24},{1,5},{5... | collective-permute-start | bytes 147464 | tf_op jit(solution)/shard_map/ppermute | solution.py:408
  6.0 4.9 %collective-permute-start = (f32[11,8,128]{2,1,0:T(8,128)S(1)}, f32[11,8,128]{2,1,0:T(8,128)S(1)}, u32[]{:S(2)}, u32[]{:S(2)}) collective-permute-start(f32[11,8,128]{2,1,0:T(8,128)S(1)} %get-tuple-element.17), channel_id=1, source_target_pairs={{0,20},{4,16},{8,28},{12,24},{16,4},{20,0},{24,12},{28,8},{1,21},{... | collective-permute-start | bytes 135176 | tf_op jit(solution)/shard_map/ppermute | solution.py:408
  11.0 3.2 %copy-start.6 = (f32[4,6]{1,0:T(4,128)S(1)}, f32[4,6]{1,0:T(4,128)}, u32[]{:S(2)}) copy-start(f32[4,6]{1,0:T(4,128)} %moduli.1) | copy-start | bytes 292
  11.0 3.2 %copy-start.7 = (f32[4,6]{1,0:T(4,128)S(1)}, f32[4,6]{1,0:T(4,128)}, u32[]{:S(2)}) copy-start(f32[4,6]{1,0:T(4,128)} %times.1) | copy-start | bytes 292
  11.0 3.2 %copy-start.8 = (f32[4]{0:T(128)S(1)}, f32[4]{0:T(128)}, u32[]{:S(2)}) copy-start(f32[4]{0:T(128)} %shear.1) | copy-start | bytes 52
  11.0 3.2 %copy-start.9 = (f32[4]{0:T(128)S(1)}, f32[4]{0:T(128)}, u32[]{:S(2)}) copy-start(f32[4]{0:T(128)} %ratio.1) | copy-start | bytes 52
  11.0 3.2 %copy-start.10 = (f32[4]{0:T(128)S(1)}, f32[4]{0:T(128)}, u32[]{:S(2)}) copy-start(f32[4]{0:T(128)} %scale.1) | copy-start | bytes 52
  11.1 1.6 %collective-permute-start.3 = (f32[59,8,128]{2,1,0:T(8,128)S(1)}, f32[59,8,128]{2,1,0:T(8,128)S(1)}, u32[]{:S(2)}, u32[]{:S(2)}) collective-permute-start(f32[59,8,128]{2,1,0:T(8,128)S(1)} %shard_map.149.refs_0_.refs_3_.refs_5_), channel_id=1, source_target_pairs={{0,8},{8,0},{16,24},{24,16},{1,9},{9,1},{17,25},{25,17},{2,10},{10... | collective-permute-start | bytes 725000 | tf_op jit(solution)/shard_map/ppermute | solution.py:408
  12.6 3.2 %collective-permute-start.4 = (f32[8,1,8,128]{3,2,1,0:T(8,128)S(1)}, f32[8,1,8,128]{3,2,1,0:T(8,128)S(1)}, u32[]{:S(2)}, u32[]{:S(2)}) collective-permute-start(f32[8,1,8,128]{3,2,1,0:T(8,128)S(1)} %shard_map.150), channel_id=1, source_target_pairs={{0,1},{1,2},{2,3},{3,11},{8,0},{9,8},{10,9},{11,10},{16,17},{17,18... | collective-permute-start | bytes 98312 | tf_op jit(solution)/shard_map/ppermute | solution.py:468
  14.2 3.9 %collective-permute-start.5 = (f32[8,1,8,128]{3,2,1,0:T(8,128)S(1)}, f32[8,1,8,128]{3,2,1,0:T(8,128)S(1)}, u32[]{:S(2)}, u32[]{:S(2)}) collective-permute-start(f32[8,1,8,128]{3,2,1,0:T(8,128)S(1)} %shard_map.150), channel_id=1, source_target_pairs={{1,0},{2,1},{3,2},{11,3},{0,8},{8,9},{9,10},{10,11},{17,16},{18,17... | collective-permute-start | bytes 98312 | tf_op jit(solution)/shard_map/ppermute | solution.py:469
  14.9 8.6 %copy-start = (f32[6,6,2,8,128]{4,3,2,1,0:T(8,128)S(1)}, f32[6,6,2,8,128]{4,3,2,1,0:T(8,128)}, u32[]{:S(2)}) copy-start(f32[6,6,2,8,128]{4,3,2,1,0:T(8,128)} %refs_2_.1) | copy-start | bytes 884740
  19.1 5.5 %collective-permute-start.6 = (f32[16,128]{1,0:T(8,128)S(1)}, f32[16,128]{1,0:T(8,128)S(1)}, u32[]{:S(2)}, u32[]{:S(2)}) collective-permute-start(f32[16,128]{1,0:T(8,128)S(1)} %get-tuple-element.24.refs_0_), channel_id=1, source_target_pairs={{0,3},{1,2},{2,1},{3,0},{4,7},{5,6},{6,5},{7,4},{8,11},{9,10},{10,... | collective-permute-start | bytes 24584 | tf_op jit(solution)/shard_map/ppermute | solution.py:408
  21.2 4.5 %collective-permute-start.7 = (f32[16,128]{1,0:T(8,128)S(1)}, f32[16,128]{1,0:T(8,128)S(1)}, u32[]{:S(2)}, u32[]{:S(2)}) collective-permute-start(f32[16,128]{1,0:T(8,128)S(1)} %get-tuple-element.24.refs_0_), channel_id=1, source_target_pairs={{0,2},{1,3},{2,0},{3,1},{4,6},{5,7},{6,4},{7,5},{8,10},{9,11},{10,... | collective-permute-start | bytes 24584 | tf_op jit(solution)/shard_map/ppermute | solution.py:408
  22.2 3.7 %collective-permute-start.8 = (f32[16,128]{1,0:T(8,128)S(1)}, f32[16,128]{1,0:T(8,128)S(1)}, u32[]{:S(2)}, u32[]{:S(2)}) collective-permute-start(f32[16,128]{1,0:T(8,128)S(1)} %get-tuple-element.24.refs_0_), channel_id=1, source_target_pairs={{0,1},{1,0},{2,3},{3,2},{4,5},{5,4},{6,7},{7,6},{8,9},{9,8},{10,11... | collective-permute-start | bytes 24584 | tf_op jit(solution)/shard_map/ppermute | solution.py:408

commit v9 on v8

--- a/solution.py
+++ b/solution.py
@@ -470,11 +470,14 @@
     return [first, second] + arrays, where
 
 
-def summed(terms, axis):
-    count = lax.axis_size(axis)
-    if count not in (1, 2, 4):
-        return [lax.psum(terms, axis)]
-    return [terms] + [moved(terms, axis, lambda i: i ^ step) for step in reversed(range(1, count))]
+def summed(terms, geo):
+    if geo.gz not in (1, 2, 4):
+        return [lax.psum(terms, "gz")]
+    if geo.gz < 4 or not geo.split:
+        return [terms] + [moved(terms, "gz", lambda i: i ^ step) for step in range(1, geo.gz)]
+    first = moved(terms, ("gx", "gz"), lambda i: i ^ (3 if i // geo.gz % 2 else 1))
+    second = moved(terms, "gz", lambda i: i ^ 2)
+    return [terms, first, moved(first, "gx", lambda i: i ^ 1), second]
 
 
 def on_device(
@@ -520,7 +523,7 @@
         flops=planes * rows * lz * 500,
     )
     if geo.full:
-        sums = summed(grams, "gz")
+        sums = summed(grams, geo)
     else:
         sums = [lax.psum(grams, ("gx", "gy", "gz"))]
     stress, visco_next, energy_next = call(

time: 26.9 us -> 26.3 us (0.978)
  starting transfers between devices: 10.7 us -> 8.96 us
  waiting for transfers between devices: 11 us -> 12.2 us
    ppermute x7, starting transfers between devices: 9.1 us -> 7.38 us  [moved(): lax.ppermute(shard, axis, [(i, target(i)) for i in range(lax.axis_size(ax...]
    ppermute x7, waiting for transfers between devices: 7.84 us -> 8.99 us  [moved(): lax.ppermute(shard, axis, [(i, target(i)) for i in range(lax.axis_size(ax...]
  transfers between devices with their start and end apart: 9 -> 9, of which waited for: 7 -> 6; matrix products, arithmetic and copies ran while one was open for 0% -> 0% of each run, Pallas kernels for 6% -> 6%
where the time goes in v9:
time: 26.3 us; the launch traced here: 26.1 us
  waiting for transfers between devices  12.2 us (46%)
  starting transfers between devices  8.96 us (34%)
  Pallas kernels  3.38 us (13%)
  between operations  0.8 us (3%)
  local copies, waits for them, and re-layouts  0.75 us (3%)
    ppermute x7, waiting for transfers between devices, moved(): lax.ppermute(shard, axis, [(i, target(i)) for i in range(lax.axis_size(ax...  8.99 us
    ppermute x7, starting transfers between devices, moved(): lax.ppermute(shard, axis, [(i, target(i)) for i in range(lax.axis_size(ax...  7.38 us
    pallas_call x8, Pallas kernels, call(): pl.pallas_call(kernel, out_shape=outs, in_specs=[smem] * len(parameters)...  3.38 us
    ppermute x1, waiting for transfers between devices, gathered(): second = lax.ppermute(slabs, ('gx', 'gz'), [(b, a) for a, b in ring_of_gz])  2.32 us
    ppermute x1, starting transfers between devices, gathered(): first = lax.ppermute(slabs, ('gx', 'gz'), ring_of_gz)  1.58 us
    ppermute x1, waiting for transfers between devices, gathered(): first = lax.ppermute(slabs, ('gx', 'gz'), ring_of_gz)  0.9 us
    unnamed x22, local copies, waits for them, and re-layouts  0.75 us
  transfers between devices with their start and end apart: 9, of which 6 were waited for; matrix products, arithmetic and copies ran while one was open for 0% of the time, Pallas kernels for 6%

profile of v9, /device:TPU:0, one launch (start us, length us, event | category | flops | bytes accessed | tf_op | source)
XLA Modules:
  0.0 26.1 jit_solution(4714273058115248751)
XLA Ops:
  0.7 0.7 %copy-done.1 = f32[3,2,8,128]{3,2,1,0:T(8,128)S(1)} copy-done((f32[3,2,8,128]{3,2,1,0:T(8,128)S(1)}, f32[3,2,8,128]{3,2,1,0:T(8,128)}, u32[]{:S(2)}) %copy-start.1) | copy-done | bytes 24600
  1.4 0.0 copy-done.2
  1.4 0.1 shard_map.148
  1.5 3.0 %collective-permute-start.1 = (f32[18,8,128]{2,1,0:T(8,128)S(1)}, f32[18,8,128]{2,1,0:T(8,128)S(1)}, u32[]{:S(2)}, u32[]{:S(2)}) collective-permute-start(f32[18,8,128]{2,1,0:T(8,128)S(1)} %get-tuple-element.16.refs_0_), channel_id=1, source_target_pairs={{0,16},{4,20},{8,24},{12,28},{16,0},{20,4},{24,8},{28,12},{1,17},{... | collective-permute-start | bytes 221192 | tf_op jit(solution)/shard_map/ppermute | solution.py:408
  4.5 1.5 %collective-permute-start.2 = (f32[12,8,128]{2,1,0:T(8,128)S(1)}, f32[12,8,128]{2,1,0:T(8,128)S(1)}, u32[]{:S(2)}, u32[]{:S(2)}) collective-permute-start(f32[12,8,128]{2,1,0:T(8,128)S(1)} %get-tuple-element.18), channel_id=1, source_target_pairs={{0,4},{4,0},{8,12},{12,8},{16,20},{20,16},{24,28},{28,24},{1,5},{5... | collective-permute-start | bytes 147464 | tf_op jit(solution)/shard_map/ppermute | solution.py:408
  6.0 0.0 collective-permute-start
  6.1 4.9 %collective-permute-done.refs_1_ = f32[11,8,128]{2,1,0:T(8,128)S(1)} collective-permute-done((f32[11,8,128]{2,1,0:T(8,128)S(1)}, f32[11,8,128]{2,1,0:T(8,128)S(1)}, u32[]{:S(2)}, u32[]{:S(2)}) %collective-permute-start) | collective-permute-done | bytes 45088 | tf_op jit(solution)/shard_map/ppermute | solution.py:408
  11.0 0.0 copy-start.6
  11.0 0.0 copy-start.7
  11.0 0.0 copy-start.9
  11.0 0.0 copy-start.10
  11.1 0.1 collective-permute-start.3
  11.1 1.5 %collective-permute-done.3.refs_1_.refs_4_.refs_6_ = f32[59,8,128]{2,1,0:T(8,128)S(1)} collective-permute-done((f32[59,8,128]{2,1,0:T(8,128)S(1)}, f32[59,8,128]{2,1,0:T(8,128)S(1)}, u32[]{:S(2)}, u32[]{:S(2)}) %collective-permute-start.3) | collective-permute-done | bytes 241696 | tf_op jit(solution)/shard_map/ppermute | solution.py:408
  12.6 1.6 %collective-permute-start.4 = (f32[8,1,8,128]{3,2,1,0:T(8,128)S(1)}, f32[8,1,8,128]{3,2,1,0:T(8,128)S(1)}, u32[]{:S(2)}, u32[]{:S(2)}) collective-permute-start(f32[8,1,8,128]{3,2,1,0:T(8,128)S(1)} %shard_map.150), channel_id=1, source_target_pairs={{0,1},{1,2},{2,3},{3,11},{8,0},{9,8},{10,9},{11,10},{16,17},{17,18... | collective-permute-start | bytes 98312 | tf_op jit(solution)/shard_map/ppermute | solution.py:468
  14.2 0.6 %shard_map.146.refs_0_ = f32[15,4,128]{2,1,0:T(4,128)S(1)} custom-call(f32[4,6]{1,0:T(4,128)S(1)} %copy-done.6, f32[4,6]{1,0:T(4,128)S(1)} %copy-done.7, f32[4]{0:T(128)S(1)} %copy-done.8, f32[4]{0:T(128)S(1)} %copy-done.9, f32[4]{0:T(128)S(1)} %copy-done.10), custom_call_target="tpu_custom_call" | custom-call | flops 16777216 | bytes 30720 | tf_op jit(solution)/shard_map/pallas_call | solution.py:396
  14.9 0.9 %collective-permute-done.4.refs_1_.refs_3_ = f32[8,1,8,128]{3,2,1,0:T(8,128)S(1)} collective-permute-done((f32[8,1,8,128]{3,2,1,0:T(8,128)S(1)}, f32[8,1,8,128]{3,2,1,0:T(8,128)S(1)}, u32[]{:S(2)}, u32[]{:S(2)}) %collective-permute-start.4) | collective-permute-done | bytes 32800 | tf_op jit(solution)/shard_map/ppermute | solution.py:468
  15.8 2.3 %collective-permute-done.5.refs_2_.refs_4_ = f32[8,1,8,128]{3,2,1,0:T(8,128)S(1)} collective-permute-done((f32[8,1,8,128]{3,2,1,0:T(8,128)S(1)}, f32[8,1,8,128]{3,2,1,0:T(8,128)S(1)}, u32[]{:S(2)}, u32[]{:S(2)}) %collective-permute-start.5) | collective-permute-done | bytes 32800 | tf_op jit(solution)/shard_map/ppermute | solution.py:469
  18.1 1.0 %shard_map.151 = (f32[5,2,8,128]{3,2,1,0:T(8,128)S(1)}, f32[6,2,8,128]{3,2,1,0:T(8,128)S(1)}, f32[16,128]{1,0:T(8,128)S(1)}) custom-call(f32[15,4,128]{2,1,0:T(4,128)S(1)} %shard_map.146.refs_0_, f32[8,1,8,128]{3,2,1,0:T(8,128)S(1)} %collective-permute-done.4.refs_1_.refs_3_, f32[8,1,8,128]{3,2,1,0:T(8,128)S(1)} %collective-permute-done.5.refs_2_.refs_4_, ...), custom_call_target="tpu_custom_call" | custom-call | flops 8192000 | bytes 677888 | tf_op jit(solution)/shard_map/pallas_call | solution.py:396
  19.1 1.6 %collective-permute-start.6 = (f32[16,128]{1,0:T(8,128)S(1)}, f32[16,128]{1,0:T(8,128)S(1)}, u32[]{:S(2)}, u32[]{:S(2)}) collective-permute-start(f32[16,128]{1,0:T(8,128)S(1)} %get-tuple-element.24.refs_0_), channel_id=1, source_target_pairs={{0,1},{1,0},{2,3},{3,2},{8,11},{9,10},{10,9},{11,8},{16,17},{17,16... | collective-permute-start | bytes 24584 | tf_op jit(solution)/shard_map/ppermute | solution.py:408
  20.7 1.1 %collective-permute-start.8 = (f32[16,128]{1,0:T(8,128)S(1)}, f32[16,128]{1,0:T(8,128)S(1)}, u32[]{:S(2)}, u32[]{:S(2)}) collective-permute-start(f32[16,128]{1,0:T(8,128)S(1)} %get-tuple-element.24.refs_0_), channel_id=1, source_target_pairs={{0,2},{1,3},{2,0},{3,1},{4,6},{5,7},{6,4},{7,5},{8,10},{9,11},{10,... | collective-permute-start | bytes 24584 | tf_op jit(solution)/shard_map/ppermute | solution.py:408
  21.8 1.0 %collective-permute-done.6.refs_1_ = f32[16,128]{1,0:T(8,128)S(1)} collective-permute-done((f32[16,128]{1,0:T(8,128)S(1)}, f32[16,128]{1,0:T(8,128)S(1)}, u32[]{:S(2)}, u32[]{:S(2)}) %collective-permute-start.6) | collective-permute-done | bytes 8224 | tf_op jit(solution)/shard_map/ppermute | solution.py:408
  22.8 0.9 %shard_map.152 = (f32[6,2,8,128]{3,2,1,0:T(8,128)}, f32[6,6,2,8,128]{4,3,2,1,0:T(8,128)}, f32[2,8,128]{2,1,0:T(8,128)}) custom-call(f32[15,4,128]{2,1,0:T(4,128)S(1)} %shard_map.146.refs_0_, f32[6,2,8,128]{3,2,1,0:T(8,128)S(1)} %get-tuple-element.19.refs_1_, f32[6,6,2,8,128]{4,3,2,1,0:T(8,128)S(1)} %copy-done, ...), custom_call_target="tpu_custom_call" | custom-call | flops 1024000 | bytes 1275904 | tf_op jit(solution)/shard_map/pallas_call | solution.py:396
  23.7 1.6 %collective-permute-done.8.refs_3_ = f32[16,128]{1,0:T(8,128)S(1)} collective-permute-done((f32[16,128]{1,0:T(8,128)S(1)}, f32[16,128]{1,0:T(8,128)S(1)}, u32[]{:S(2)}, u32[]{:S(2)}) %collective-permute-start.8) | collective-permute-done | bytes 8224 | tf_op jit(solution)/shard_map/ppermute | solution.py:408
  25.3 0.8 %shard_map.153 = (f32[2,8,128]{2,1,0:T(8,128)}, f32[2,8,128]{2,1,0:T(8,128)}) custom-call(f32[5,2,8,128]{3,2,1,0:T(8,128)S(1)} %get-tuple-element.23.basis, f32[16,128]{1,0:T(8,128)S(1)} %get-tuple-element.24.refs_0_, f32[16,128]{1,0:T(8,128)S(1)} %collective-permute-done.6.refs_1_, f32[16,128]{1,0:T(8,128)S(1)} %collective-permute-done.7.refs_2_, ...), custom_call_target="tpu_custom_call" | custom-call | bytes 90112 | tf_op jit(solution)/shard_map/pallas_call | solution.py:396
  (24 shorter events, 0.1 us)
Async XLA Ops:
  0.6 0.7 %copy-start.1 = (f32[3,2,8,128]{3,2,1,0:T(8,128)S(1)}, f32[3,2,8,128]{3,2,1,0:T(8,128)}, u32[]{:S(2)}) copy-start(f32[3,2,8,128]{3,2,1,0:T(8,128)} %new.1) | copy-start | bytes 73732
  0.6 0.7 %copy-start.2 = (f32[3,2,8,128]{3,2,1,0:T(8,128)S(1)}, f32[3,2,8,128]{3,2,1,0:T(8,128)}, u32[]{:S(2)}) copy-start(f32[3,2,8,128]{3,2,1,0:T(8,128)} %old.1) | copy-start | bytes 73732
  0.7 0.7 %copy-start.3 = (f32[2,8,128]{2,1,0:T(8,128)S(1)}, f32[2,8,128]{2,1,0:T(8,128)}, u32[]{:S(2)}) copy-start(f32[2,8,128]{2,1,0:T(8,128)} %energy_max.1) | copy-start | bytes 24580
  0.7 0.7 %copy-start.4 = (s32[2,8,128]{2,1,0:T(8,128)S(1)}, s32[2,8,128]{2,1,0:T(8,128)}, u32[]{:S(2)}) copy-start(s32[2,8,128]{2,1,0:T(8,128)} %region.1) | copy-start | bytes 24580
  0.7 0.7 %copy-start.5 = (s32[2,8,128]{2,1,0:T(8,128)S(1)}, s32[2,8,128]{2,1,0:T(8,128)}, u32[]{:S(2)}) copy-start(s32[2,8,128]{2,1,0:T(8,128)} %dirichlet.1) | copy-start | bytes 24580
  1.5 9.5 %collective-permute-start.1 = (f32[18,8,128]{2,1,0:T(8,128)S(1)}, f32[18,8,128]{2,1,0:T(8,128)S(1)}, u32[]{:S(2)}, u32[]{:S(2)}) collective-permute-start(f32[18,8,128]{2,1,0:T(8,128)S(1)} %get-tuple-element.16.refs_0_), channel_id=1, source_target_pairs={{0,16},{4,20},{8,24},{12,28},{16,0},{20,4},{24,8},{28,12},{1,17},{... | collective-permute-start | bytes 221192 | tf_op jit(solution)/shard_map/ppermute | solution.py:408
  4.5 6.4 %collective-permute-start.2 = (f32[12,8,128]{2,1,0:T(8,128)S(1)}, f32[12,8,128]{2,1,0:T(8,128)S(1)}, u32[]{:S(2)}, u32[]{:S(2)}) collective-permute-start(f32[12,8,128]{2,1,0:T(8,128)S(1)} %get-tuple-element.18), channel_id=1, source_target_pairs={{0,4},{4,0},{8,12},{12,8},{16,20},{20,16},{24,28},{28,24},{1,5},{5... | collective-permute-start | bytes 147464 | tf_op jit(solution)/shard_map/ppermute | solution.py:408
  6.0 4.9 %collective-permute-start = (f32[11,8,128]{2,1,0:T(8,128)S(1)}, f32[11,8,128]{2,1,0:T(8,128)S(1)}, u32[]{:S(2)}, u32[]{:S(2)}) collective-permute-start(f32[11,8,128]{2,1,0:T(8,128)S(1)} %get-tuple-element.17), channel_id=1, source_target_pairs={{0,20},{4,16},{8,28},{12,24},{16,4},{20,0},{24,12},{28,8},{1,21},{... | collective-permute-start | bytes 135176 | tf_op jit(solution)/shard_map/ppermute | solution.py:408
  11.0 3.2 %copy-start.6 = (f32[4,6]{1,0:T(4,128)S(1)}, f32[4,6]{1,0:T(4,128)}, u32[]{:S(2)}) copy-start(f32[4,6]{1,0:T(4,128)} %moduli.1) | copy-start | bytes 292
  11.0 3.2 %copy-start.7 = (f32[4,6]{1,0:T(4,128)S(1)}, f32[4,6]{1,0:T(4,128)}, u32[]{:S(2)}) copy-start(f32[4,6]{1,0:T(4,128)} %times.1) | copy-start | bytes 292
  11.0 3.2 %copy-start.8 = (f32[4]{0:T(128)S(1)}, f32[4]{0:T(128)}, u32[]{:S(2)}) copy-start(f32[4]{0:T(128)} %shear.1) | copy-start | bytes 52
  11.0 3.2 %copy-start.9 = (f32[4]{0:T(128)S(1)}, f32[4]{0:T(128)}, u32[]{:S(2)}) copy-start(f32[4]{0:T(128)} %ratio.1) | copy-start | bytes 52
  11.0 3.2 %copy-start.10 = (f32[4]{0:T(128)S(1)}, f32[4]{0:T(128)}, u32[]{:S(2)}) copy-start(f32[4]{0:T(128)} %scale.1) | copy-start | bytes 52
  11.1 1.6 %collective-permute-start.3 = (f32[59,8,128]{2,1,0:T(8,128)S(1)}, f32[59,8,128]{2,1,0:T(8,128)S(1)}, u32[]{:S(2)}, u32[]{:S(2)}) collective-permute-start(f32[59,8,128]{2,1,0:T(8,128)S(1)} %shard_map.149.refs_0_.refs_3_.refs_5_), channel_id=1, source_target_pairs={{0,8},{8,0},{16,24},{24,16},{1,9},{9,1},{17,25},{25,17},{2,10},{10... | collective-permute-start | bytes 725000 | tf_op jit(solution)/shard_map/ppermute | solution.py:408
  12.6 3.2 %collective-permute-start.4 = (f32[8,1,8,128]{3,2,1,0:T(8,128)S(1)}, f32[8,1,8,128]{3,2,1,0:T(8,128)S(1)}, u32[]{:S(2)}, u32[]{:S(2)}) collective-permute-start(f32[8,1,8,128]{3,2,1,0:T(8,128)S(1)} %shard_map.150), channel_id=1, source_target_pairs={{0,1},{1,2},{2,3},{3,11},{8,0},{9,8},{10,9},{11,10},{16,17},{17,18... | collective-permute-start | bytes 98312 | tf_op jit(solution)/shard_map/ppermute | solution.py:468
  14.2 3.9 %collective-permute-start.5 = (f32[8,1,8,128]{3,2,1,0:T(8,128)S(1)}, f32[8,1,8,128]{3,2,1,0:T(8,128)S(1)}, u32[]{:S(2)}, u32[]{:S(2)}) collective-permute-start(f32[8,1,8,128]{3,2,1,0:T(8,128)S(1)} %shard_map.150), channel_id=1, source_target_pairs={{1,0},{2,1},{3,2},{11,3},{0,8},{8,9},{9,10},{10,11},{17,16},{18,17... | collective-permute-start | bytes 98312 | tf_op jit(solution)/shard_map/ppermute | solution.py:469
  14.9 7.9 %copy-start = (f32[6,6,2,8,128]{4,3,2,1,0:T(8,128)S(1)}, f32[6,6,2,8,128]{4,3,2,1,0:T(8,128)}, u32[]{:S(2)}) copy-start(f32[6,6,2,8,128]{4,3,2,1,0:T(8,128)} %refs_2_.1) | copy-start | bytes 884740
  19.1 3.7 %collective-permute-start.6 = (f32[16,128]{1,0:T(8,128)S(1)}, f32[16,128]{1,0:T(8,128)S(1)}, u32[]{:S(2)}, u32[]{:S(2)}) collective-permute-start(f32[16,128]{1,0:T(8,128)S(1)} %get-tuple-element.24.refs_0_), channel_id=1, source_target_pairs={{0,1},{1,0},{2,3},{3,2},{8,11},{9,10},{10,9},{11,8},{16,17},{17,16... | collective-permute-start | bytes 24584 | tf_op jit(solution)/shard_map/ppermute | solution.py:408
  20.7 4.5 %collective-permute-start.8 = (f32[16,128]{1,0:T(8,128)S(1)}, f32[16,128]{1,0:T(8,128)S(1)}, u32[]{:S(2)}, u32[]{:S(2)}) collective-permute-start(f32[16,128]{1,0:T(8,128)S(1)} %get-tuple-element.24.refs_0_), channel_id=1, source_target_pairs={{0,2},{1,3},{2,0},{3,1},{4,6},{5,7},{6,4},{7,5},{8,10},{9,11},{10,... | collective-permute-start | bytes 24584 | tf_op jit(solution)/shard_map/ppermute | solution.py:408
  22.8 2.5 %collective-permute-start.7 = (f32[16,128]{1,0:T(8,128)S(1)}, f32[16,128]{1,0:T(8,128)S(1)}, u32[]{:S(2)}, u32[]{:S(2)}) collective-permute-start(f32[16,128]{1,0:T(8,128)S(1)} %collective-permute-done.6.refs_1_), channel_id=1, source_target_pairs={{0,8},{8,0},{16,24},{24,16},{1,9},{9,1},{17,25},{25,17},{2,10},{10... | collective-permute-start | bytes 24584 | tf_op jit(solution)/shard_map/ppermute | solution.py:408

commit v10 on v9

--- a/solution.py
+++ b/solution.py
@@ -127,13 +127,30 @@
 def tables_kernel(moduli, times, shear, ratio, scale, tables):
     regions, terms = moduli.shape
     for r in range(regions):
-        entries = [shear[r], ratio[r], scale[r]]
-        entries += [moduli[r, k] for k in range(terms)] + [times[r, k] for k in range(terms)]
-        for k, entry in enumerate(entries):
-            tables[k, r : r + 1, :] = jnp.full((1, tables.shape[2]), entry, jnp.float32)
-
-
-SHEAR, RATIO, SCALE, MODULI = range(4)
+
+        def spread(entry):
+            return jnp.full((1, tables.shape[2]), entry, jnp.float32)
+
+        tables[SHEAR, r : r + 1, :] = spread(shear[r])
+        tables[INVERSE_RATIO, r : r + 1, :] = spread(ratio[r])
+        tables[INVERSE_SCALE, r : r + 1, :] = spread(scale[r])
+        total = moduli[r, 0]
+        for k in range(1, terms):
+            total = total + moduli[r, k]
+        tables[LONG_TERM, r : r + 1, :] = spread(1.0 - total)
+        for k in range(terms):
+            tables[DECAYS + k, r : r + 1, :] = spread(times[r, k])
+            tables[DECAYS + terms + k, r : r + 1, :] = spread(moduli[r, k])
+    tables[INVERSE_RATIO] = 1.0 / tables[INVERSE_RATIO]
+    tables[INVERSE_SCALE] = 1.0 / tables[INVERSE_SCALE]
+    for k in range(terms):
+        time = tables[DECAYS + k]
+        decay = jnp.exp(-1.0 / time)
+        tables[DECAYS + k] = decay
+        tables[DECAYS + terms + k] = tables[DECAYS + terms + k] * (1.0 - decay) * time
+
+
+SHEAR, INVERSE_RATIO, INVERSE_SCALE, LONG_TERM, DECAYS = range(5)
 
 
 def lookup(tables, entry, masks):
@@ -144,7 +161,7 @@
 
 
 def deviator(grad):
-    trace_third = (grad[0][0] + grad[1][1] + grad[2][2]) / 3.0
+    trace_third = (grad[0][0] + grad[1][1] + grad[2][2]) * (1.0 / 3.0)
     return [
         grad[0][0] - trace_third,
         grad[1][1] - trace_third,
@@ -164,8 +181,8 @@
     )
 
 
-def soften(energy, energy_next, scale, ratio):
-    return 1.0 - lax.erf((energy_next - energy) / scale) / ratio
+def soften(energy, energy_next, inverse_scale, inverse_ratio):
+    return 1.0 - lax.erf((energy_next - energy) * inverse_scale) * inverse_ratio
 
 
 class Place(typing.NamedTuple):
@@ -224,18 +241,18 @@
         for a in range(3):
             next_y, prev_y, next_z, prev_z = beside(held[a, p])
             next_x, prev_x = held[a, next_plane(p)], held[a, prev_plane(p)]
-            grad.append([0.5 * (next_x - prev_x), 0.5 * (next_y - prev_y), 0.5 * (next_z - prev_z)])
+            grad.append([next_x - prev_x, next_y - prev_y, next_z - prev_z])
         dev = deviator(grad)
         if p < lx:
             for k in range(6):
-                dev_own[k, p] = dev[k][:ly, :lz]
+                dev_own[k, p] = 0.5 * dev[k][:ly, :lz]
         label = whole_plane(4, p)
         halves = []
         for half in (slice(0, lz), slice(lz, lanes)):
             masks = [label[:, half] == r for r in range(regions - 1)]
-            halves.append([lookup(tables, entry, masks) for entry in (SHEAR, SCALE, RATIO)])
+            halves.append([lookup(tables, entry, masks) for entry in (SHEAR, INVERSE_SCALE, INVERSE_RATIO)])
         shear_cells, scale_cells, ratio_cells = [jnp.concatenate(pair, axis=1) for pair in zip(*halves)]
-        energy = shear_cells * contract(dev)
+        energy = 0.25 * shear_cells * contract(dev)
         energy_next = jnp.maximum(whole_plane(3, p), energy)
         softening = soften(energy, energy_next, scale_cells, ratio_cells)
         field[0, p] = softening * energy
@@ -321,19 +338,18 @@
         dev_new = [dev_own[k, i] for k in range(6)]
         label = of((0, 0), 4 * lx + i)
         masks = [label == r for r in range(regions - 1)]
-        shear_cells, ratio_cells, scale_cells = [lookup(tables, entry, masks) for entry in (SHEAR, RATIO, SCALE)]
+        shear_cells, ratio_cells, scale_cells, long_term = [
+            lookup(tables, entry, masks) for entry in (SHEAR, INVERSE_RATIO, INVERSE_SCALE, LONG_TERM)
+        ]
         energy = shear_cells * contract(dev_new)
         energy_after = jnp.maximum(of((0, 0), 3 * lx + i), energy)
         energy_next[i] = energy_after
         softening = soften(energy, energy_after, scale_cells, ratio_cells)
         jump = [2.0 * shear_cells * (dev_new[k] - dev_old[k]) for k in range(6)]
-        totals, long_term = [0.0] * 6, 1.0
+        totals = [0.0] * 6
         for term in range(terms):
-            modulus = lookup(tables, MODULI + term, masks)
-            time = lookup(tables, MODULI + terms + term, masks)
-            decay = jnp.exp(-1.0 / time)
-            weight = modulus * (1.0 - decay) * time
-            long_term = long_term - modulus
+            decay = lookup(tables, DECAYS + term, masks)
+            weight = lookup(tables, DECAYS + terms + term, masks)
             for k in range(6):
                 value = decay * visco[term, k, i] + weight * jump[k]
                 visco_next[term, k, i] = value
@@ -475,8 +491,8 @@
         return [lax.psum(terms, "gz")]
     if geo.gz < 4 or not geo.split:
         return [terms] + [moved(terms, "gz", lambda i: i ^ step) for step in range(1, geo.gz)]
-    first = moved(terms, ("gx", "gz"), lambda i: i ^ (3 if i // geo.gz % 2 else 1))
-    second = moved(terms, "gz", lambda i: i ^ 2)
+    first = moved(terms, ("gx", "gz"), lambda i: i ^ (2 if i // geo.gz % 2 else 1))
+    second = moved(terms, "gz", lambda i: i ^ 3)
     return [terms, first, moved(first, "gx", lambda i: i ^ 1), second]
 
 
@@ -505,7 +521,7 @@
     )
     (tables,) = call(
         tables_kernel,
-        [shaped(MODULI + 2 * terms, regions, lz)],
+        [shaped(DECAYS + 2 * terms, regions, lz)],
         [],
         parameters=[prony_moduli, prony_times, shear_modulus, mullins_ratio, mullins_scale],
         flops=1 << 24,

time: 26.3 us -> 27.2 us (1.034)
  starting transfers between devices: 8.96 us -> 10.3 us
  waiting for transfers between devices: 12.2 us -> 11.7 us
    ppermute x7, starting transfers between devices: 7.38 us -> 8.76 us  [moved(): lax.ppermute(shard, axis, [(i, target(i)) for i in range(lax.axis_size(ax...]
    ppermute x7, waiting for transfers between devices: 8.99 us -> 8.5 us  [moved(): lax.ppermute(shard, axis, [(i, target(i)) for i in range(lax.axis_size(ax...]
  transfers between devices with their start and end apart: 9 -> 9, of which waited for: 6 -> 5; matrix products, arithmetic and copies ran while one was open for 0% -> 0% of each run, Pallas kernels for 6% -> 6%
where the time goes in v10:
time: 27.2 us; the launch traced here: 27 us
  waiting for transfers between devices  11.7 us (43%)
  starting transfers between devices  10.3 us (38%)
  Pallas kernels  3.39 us (12%)
  between operations  0.8 us (3%)
  local copies, waits for them, and re-layouts  0.75 us (3%)
    ppermute x7, starting transfers between devices, moved(): lax.ppermute(shard, axis, [(i, target(i)) for i in range(lax.axis_size(ax...  8.76 us
    ppermute x7, waiting for transfers between devices, moved(): lax.ppermute(shard, axis, [(i, target(i)) for i in range(lax.axis_size(ax...  8.5 us
    pallas_call x8, Pallas kernels, call(): pl.pallas_call(kernel, out_shape=outs, in_specs=[smem] * len(parameters)...  3.39 us
    ppermute x1, waiting for transfers between devices, gathered(): second = lax.ppermute(slabs, ('gx', 'gz'), [(b, a) for a, b in ring_of_gz])  2.32 us
    ppermute x1, starting transfers between devices, gathered(): first = lax.ppermute(slabs, ('gx', 'gz'), ring_of_gz)  1.58 us
    ppermute x1, waiting for transfers between devices, gathered(): first = lax.ppermute(slabs, ('gx', 'gz'), ring_of_gz)  0.87 us
    unnamed x22, local copies, waits for them, and re-layouts  0.75 us
  transfers between devices with their start and end apart: 9, of which 5 were waited for; matrix products, arithmetic and copies ran while one was open for 0% of the time, Pallas kernels for 6%

profile of v10, /device:TPU:0, one launch (start us, length us, event | category | flops | bytes accessed | tf_op | source)
XLA Modules:
  0.0 27.0 jit_solution(1335957788598080042)
XLA Ops:
  0.7 0.7 %copy-done.1 = f32[3,2,8,128]{3,2,1,0:T(8,128)S(1)} copy-done((f32[3,2,8,128]{3,2,1,0:T(8,128)S(1)}, f32[3,2,8,128]{3,2,1,0:T(8,128)}, u32[]{:S(2)}) %copy-start.1) | copy-done | bytes 24600
  1.4 0.0 copy-done.2
  1.4 0.1 shard_map.148
  1.5 3.0 %collective-permute-start.1 = (f32[18,8,128]{2,1,0:T(8,128)S(1)}, f32[18,8,128]{2,1,0:T(8,128)S(1)}, u32[]{:S(2)}, u32[]{:S(2)}) collective-permute-start(f32[18,8,128]{2,1,0:T(8,128)S(1)} %get-tuple-element.16.refs_0_), channel_id=1, source_target_pairs={{0,16},{4,20},{8,24},{12,28},{16,0},{20,4},{24,8},{28,12},{1,17},{... | collective-permute-start | bytes 221192 | tf_op jit(solution)/shard_map/ppermute | solution.py:424
  4.5 1.5 %collective-permute-start.2 = (f32[12,8,128]{2,1,0:T(8,128)S(1)}, f32[12,8,128]{2,1,0:T(8,128)S(1)}, u32[]{:S(2)}, u32[]{:S(2)}) collective-permute-start(f32[12,8,128]{2,1,0:T(8,128)S(1)} %get-tuple-element.18), channel_id=1, source_target_pairs={{0,4},{4,0},{8,12},{12,8},{16,20},{20,16},{24,28},{28,24},{1,5},{5... | collective-permute-start | bytes 147464 | tf_op jit(solution)/shard_map/ppermute | solution.py:424
  6.0 0.0 collective-permute-start
  6.1 4.9 %collective-permute-done.refs_1_ = f32[11,8,128]{2,1,0:T(8,128)S(1)} collective-permute-done((f32[11,8,128]{2,1,0:T(8,128)S(1)}, f32[11,8,128]{2,1,0:T(8,128)S(1)}, u32[]{:S(2)}, u32[]{:S(2)}) %collective-permute-start) | collective-permute-done | bytes 45088 | tf_op jit(solution)/shard_map/ppermute | solution.py:424
  11.0 0.0 copy-start.6
  11.0 0.0 copy-start.7
  11.0 0.0 copy-start.9
  11.0 0.0 copy-start.10
  11.1 0.1 collective-permute-start.3
  11.1 1.5 %collective-permute-done.3.refs_1_.refs_4_.refs_6_ = f32[59,8,128]{2,1,0:T(8,128)S(1)} collective-permute-done((f32[59,8,128]{2,1,0:T(8,128)S(1)}, f32[59,8,128]{2,1,0:T(8,128)S(1)}, u32[]{:S(2)}, u32[]{:S(2)}) %collective-permute-start.3) | collective-permute-done | bytes 241696 | tf_op jit(solution)/shard_map/ppermute | solution.py:424
  12.6 1.6 %collective-permute-start.4 = (f32[8,1,8,128]{3,2,1,0:T(8,128)S(1)}, f32[8,1,8,128]{3,2,1,0:T(8,128)S(1)}, u32[]{:S(2)}, u32[]{:S(2)}) collective-permute-start(f32[8,1,8,128]{3,2,1,0:T(8,128)S(1)} %shard_map.150), channel_id=1, source_target_pairs={{0,1},{1,2},{2,3},{3,11},{8,0},{9,8},{10,9},{11,10},{16,17},{17,18... | collective-permute-start | bytes 98312 | tf_op jit(solution)/shard_map/ppermute | solution.py:484
  14.2 0.7 %shard_map.146.refs_0_ = f32[16,4,128]{2,1,0:T(4,128)S(1)} custom-call(f32[4,6]{1,0:T(4,128)S(1)} %copy-done.6, f32[4,6]{1,0:T(4,128)S(1)} %copy-done.7, f32[4]{0:T(128)S(1)} %copy-done.8, f32[4]{0:T(128)S(1)} %copy-done.9, f32[4]{0:T(128)S(1)} %copy-done.10), custom_call_target="tpu_custom_call" | custom-call | flops 16777216 | bytes 32768 | tf_op jit(solution)/shard_map/pallas_call | solution.py:412
  14.9 0.0 copy-start
  14.9 0.9 %collective-permute-done.4.refs_1_.refs_3_ = f32[8,1,8,128]{3,2,1,0:T(8,128)S(1)} collective-permute-done((f32[8,1,8,128]{3,2,1,0:T(8,128)S(1)}, f32[8,1,8,128]{3,2,1,0:T(8,128)S(1)}, u32[]{:S(2)}, u32[]{:S(2)}) %collective-permute-start.4) | collective-permute-done | bytes 32800 | tf_op jit(solution)/shard_map/ppermute | solution.py:484
  15.8 2.3 %collective-permute-done.5.refs_2_.refs_4_ = f32[8,1,8,128]{3,2,1,0:T(8,128)S(1)} collective-permute-done((f32[8,1,8,128]{3,2,1,0:T(8,128)S(1)}, f32[8,1,8,128]{3,2,1,0:T(8,128)S(1)}, u32[]{:S(2)}, u32[]{:S(2)}) %collective-permute-start.5) | collective-permute-done | bytes 32800 | tf_op jit(solution)/shard_map/ppermute | solution.py:485
  18.1 0.9 %shard_map.151 = (f32[5,2,8,128]{3,2,1,0:T(8,128)S(1)}, f32[6,2,8,128]{3,2,1,0:T(8,128)S(1)}, f32[16,128]{1,0:T(8,128)S(1)}) custom-call(f32[16,4,128]{2,1,0:T(4,128)S(1)} %shard_map.146.refs_0_, f32[8,1,8,128]{3,2,1,0:T(8,128)S(1)} %collective-permute-done.4.refs_1_.refs_3_, f32[8,1,8,128]{3,2,1,0:T(8,128)S(1)} %collective-permute-done.5.refs_2_.refs_4_, ...), custom_call_target="tpu_custom_call" | custom-call | flops 8192000 | bytes 679936 | tf_op jit(solution)/shard_map/pallas_call | solution.py:412
  19.1 1.6 %collective-permute-start.6 = (f32[16,128]{1,0:T(8,128)S(1)}, f32[16,128]{1,0:T(8,128)S(1)}, u32[]{:S(2)}, u32[]{:S(2)}) collective-permute-start(f32[16,128]{1,0:T(8,128)S(1)} %get-tuple-element.24.refs_0_), channel_id=1, source_target_pairs={{0,1},{1,0},{2,3},{3,2},{8,10},{9,11},{10,8},{11,9},{16,17},{17,16... | collective-permute-start | bytes 24584 | tf_op jit(solution)/shard_map/ppermute | solution.py:424
  20.7 2.5 %collective-permute-start.8 = (f32[16,128]{1,0:T(8,128)S(1)}, f32[16,128]{1,0:T(8,128)S(1)}, u32[]{:S(2)}, u32[]{:S(2)}) collective-permute-start(f32[16,128]{1,0:T(8,128)S(1)} %get-tuple-element.24.refs_0_), channel_id=1, source_target_pairs={{0,3},{1,2},{2,1},{3,0},{4,7},{5,6},{6,5},{7,4},{8,11},{9,10},{10,... | collective-permute-start | bytes 24584 | tf_op jit(solution)/shard_map/ppermute | solution.py:424
  23.2 0.9 %shard_map.152 = (f32[6,2,8,128]{3,2,1,0:T(8,128)}, f32[6,6,2,8,128]{4,3,2,1,0:T(8,128)}, f32[2,8,128]{2,1,0:T(8,128)}) custom-call(f32[16,4,128]{2,1,0:T(4,128)S(1)} %shard_map.146.refs_0_, f32[6,2,8,128]{3,2,1,0:T(8,128)S(1)} %get-tuple-element.19.refs_1_, f32[6,6,2,8,128]{4,3,2,1,0:T(8,128)S(1)} %copy-done, ...), custom_call_target="tpu_custom_call" | custom-call | flops 1024000 | bytes 1277952 | tf_op jit(solution)/shard_map/pallas_call | solution.py:412
  24.1 2.1 %collective-permute-done.8.refs_3_ = f32[16,128]{1,0:T(8,128)S(1)} collective-permute-done((f32[16,128]{1,0:T(8,128)S(1)}, f32[16,128]{1,0:T(8,128)S(1)}, u32[]{:S(2)}, u32[]{:S(2)}) %collective-permute-start.8) | collective-permute-done | bytes 8224 | tf_op jit(solution)/shard_map/ppermute | solution.py:424
  26.2 0.8 %shard_map.153 = (f32[2,8,128]{2,1,0:T(8,128)}, f32[2,8,128]{2,1,0:T(8,128)}) custom-call(f32[5,2,8,128]{3,2,1,0:T(8,128)S(1)} %get-tuple-element.23.basis, f32[16,128]{1,0:T(8,128)S(1)} %get-tuple-element.24.refs_0_, f32[16,128]{1,0:T(8,128)S(1)} %collective-permute-done.6.refs_1_, f32[16,128]{1,0:T(8,128)S(1)} %collective-permute-done.7.refs_2_, ...), custom_call_target="tpu_custom_call" | custom-call | bytes 90112 | tf_op jit(solution)/shard_map/pallas_call | solution.py:412
  (24 shorter events, 0.1 us)
Async XLA Ops:
  0.6 0.7 %copy-start.1 = (f32[3,2,8,128]{3,2,1,0:T(8,128)S(1)}, f32[3,2,8,128]{3,2,1,0:T(8,128)}, u32[]{:S(2)}) copy-start(f32[3,2,8,128]{3,2,1,0:T(8,128)} %new.1) | copy-start | bytes 73732
  0.6 0.7 %copy-start.2 = (f32[3,2,8,128]{3,2,1,0:T(8,128)S(1)}, f32[3,2,8,128]{3,2,1,0:T(8,128)}, u32[]{:S(2)}) copy-start(f32[3,2,8,128]{3,2,1,0:T(8,128)} %old.1) | copy-start | bytes 73732
  0.7 0.7 %copy-start.3 = (f32[2,8,128]{2,1,0:T(8,128)S(1)}, f32[2,8,128]{2,1,0:T(8,128)}, u32[]{:S(2)}) copy-start(f32[2,8,128]{2,1,0:T(8,128)} %energy_max.1) | copy-start | bytes 24580
  0.7 0.7 %copy-start.4 = (s32[2,8,128]{2,1,0:T(8,128)S(1)}, s32[2,8,128]{2,1,0:T(8,128)}, u32[]{:S(2)}) copy-start(s32[2,8,128]{2,1,0:T(8,128)} %region.1) | copy-start | bytes 24580
  0.7 0.7 %copy-start.5 = (s32[2,8,128]{2,1,0:T(8,128)S(1)}, s32[2,8,128]{2,1,0:T(8,128)}, u32[]{:S(2)}) copy-start(s32[2,8,128]{2,1,0:T(8,128)} %dirichlet.1) | copy-start | bytes 24580
  1.5 9.5 %collective-permute-start.1 = (f32[18,8,128]{2,1,0:T(8,128)S(1)}, f32[18,8,128]{2,1,0:T(8,128)S(1)}, u32[]{:S(2)}, u32[]{:S(2)}) collective-permute-start(f32[18,8,128]{2,1,0:T(8,128)S(1)} %get-tuple-element.16.refs_0_), channel_id=1, source_target_pairs={{0,16},{4,20},{8,24},{12,28},{16,0},{20,4},{24,8},{28,12},{1,17},{... | collective-permute-start | bytes 221192 | tf_op jit(solution)/shard_map/ppermute | solution.py:424
  4.5 6.4 %collective-permute-start.2 = (f32[12,8,128]{2,1,0:T(8,128)S(1)}, f32[12,8,128]{2,1,0:T(8,128)S(1)}, u32[]{:S(2)}, u32[]{:S(2)}) collective-permute-start(f32[12,8,128]{2,1,0:T(8,128)S(1)} %get-tuple-element.18), channel_id=1, source_target_pairs={{0,4},{4,0},{8,12},{12,8},{16,20},{20,16},{24,28},{28,24},{1,5},{5... | collective-permute-start | bytes 147464 | tf_op jit(solution)/shard_map/ppermute | solution.py:424
  6.0 4.9 %collective-permute-start = (f32[11,8,128]{2,1,0:T(8,128)S(1)}, f32[11,8,128]{2,1,0:T(8,128)S(1)}, u32[]{:S(2)}, u32[]{:S(2)}) collective-permute-start(f32[11,8,128]{2,1,0:T(8,128)S(1)} %get-tuple-element.17), channel_id=1, source_target_pairs={{0,20},{4,16},{8,28},{12,24},{16,4},{20,0},{24,12},{28,8},{1,21},{... | collective-permute-start | bytes 135176 | tf_op jit(solution)/shard_map/ppermute | solution.py:424
  11.0 3.2 %copy-start.6 = (f32[4,6]{1,0:T(4,128)S(1)}, f32[4,6]{1,0:T(4,128)}, u32[]{:S(2)}) copy-start(f32[4,6]{1,0:T(4,128)} %moduli.1) | copy-start | bytes 292
  11.0 3.2 %copy-start.7 = (f32[4,6]{1,0:T(4,128)S(1)}, f32[4,6]{1,0:T(4,128)}, u32[]{:S(2)}) copy-start(f32[4,6]{1,0:T(4,128)} %times.1) | copy-start | bytes 292
  11.0 3.2 %copy-start.8 = (f32[4]{0:T(128)S(1)}, f32[4]{0:T(128)}, u32[]{:S(2)}) copy-start(f32[4]{0:T(128)} %shear.1) | copy-start | bytes 52
  11.0 3.2 %copy-start.9 = (f32[4]{0:T(128)S(1)}, f32[4]{0:T(128)}, u32[]{:S(2)}) copy-start(f32[4]{0:T(128)} %ratio.1) | copy-start | bytes 52
  11.0 3.2 %copy-start.10 = (f32[4]{0:T(128)S(1)}, f32[4]{0:T(128)}, u32[]{:S(2)}) copy-start(f32[4]{0:T(128)} %scale.1) | copy-start | bytes 52
  11.1 1.6 %collective-permute-start.3 = (f32[59,8,128]{2,1,0:T(8,128)S(1)}, f32[59,8,128]{2,1,0:T(8,128)S(1)}, u32[]{:S(2)}, u32[]{:S(2)}) collective-permute-start(f32[59,8,128]{2,1,0:T(8,128)S(1)} %shard_map.149.refs_0_.refs_3_.refs_5_), channel_id=1, source_target_pairs={{0,8},{8,0},{16,24},{24,16},{1,9},{9,1},{17,25},{25,17},{2,10},{10... | collective-permute-start | bytes 725000 | tf_op jit(solution)/shard_map/ppermute | solution.py:424
  12.6 3.2 %collective-permute-start.4 = (f32[8,1,8,128]{3,2,1,0:T(8,128)S(1)}, f32[8,1,8,128]{3,2,1,0:T(8,128)S(1)}, u32[]{:S(2)}, u32[]{:S(2)}) collective-permute-start(f32[8,1,8,128]{3,2,1,0:T(8,128)S(1)} %shard_map.150), channel_id=1, source_target_pairs={{0,1},{1,2},{2,3},{3,11},{8,0},{9,8},{10,9},{11,10},{16,17},{17,18... | collective-permute-start | bytes 98312 | tf_op jit(solution)/shard_map/ppermute | solution.py:484
  14.2 3.9 %collective-permute-start.5 = (f32[8,1,8,128]{3,2,1,0:T(8,128)S(1)}, f32[8,1,8,128]{3,2,1,0:T(8,128)S(1)}, u32[]{:S(2)}, u32[]{:S(2)}) collective-permute-start(f32[8,1,8,128]{3,2,1,0:T(8,128)S(1)} %shard_map.150), channel_id=1, source_target_pairs={{1,0},{2,1},{3,2},{11,3},{0,8},{8,9},{9,10},{10,11},{17,16},{18,17... | collective-permute-start | bytes 98312 | tf_op jit(solution)/shard_map/ppermute | solution.py:485
  14.9 8.3 %copy-start = (f32[6,6,2,8,128]{4,3,2,1,0:T(8,128)S(1)}, f32[6,6,2,8,128]{4,3,2,1,0:T(8,128)}, u32[]{:S(2)}) copy-start(f32[6,6,2,8,128]{4,3,2,1,0:T(8,128)} %refs_2_.1) | copy-start | bytes 884740
  19.1 4.1 %collective-permute-start.6 = (f32[16,128]{1,0:T(8,128)S(1)}, f32[16,128]{1,0:T(8,128)S(1)}, u32[]{:S(2)}, u32[]{:S(2)}) collective-permute-start(f32[16,128]{1,0:T(8,128)S(1)} %get-tuple-element.24.refs_0_), channel_id=1, source_target_pairs={{0,1},{1,0},{2,3},{3,2},{8,10},{9,11},{10,8},{11,9},{16,17},{17,16... | collective-permute-start | bytes 24584 | tf_op jit(solution)/shard_map/ppermute | solution.py:424
  20.7 5.4 %collective-permute-start.8 = (f32[16,128]{1,0:T(8,128)S(1)}, f32[16,128]{1,0:T(8,128)S(1)}, u32[]{:S(2)}, u32[]{:S(2)}) collective-permute-start(f32[16,128]{1,0:T(8,128)S(1)} %get-tuple-element.24.refs_0_), channel_id=1, source_target_pairs={{0,3},{1,2},{2,1},{3,0},{4,7},{5,6},{6,5},{7,4},{8,11},{9,10},{10,... | collective-permute-start | bytes 24584 | tf_op jit(solution)/shard_map/ppermute | solution.py:424
  23.2 3.0 %collective-permute-start.7 = (f32[16,128]{1,0:T(8,128)S(1)}, f32[16,128]{1,0:T(8,128)S(1)}, u32[]{:S(2)}, u32[]{:S(2)}) collective-permute-start(f32[16,128]{1,0:T(8,128)S(1)} %collective-permute-done.6.refs_1_), channel_id=1, source_target_pairs={{0,8},{8,0},{16,24},{24,16},{1,9},{9,1},{17,25},{25,17},{2,10},{10... | collective-permute-start | bytes 24584 | tf_op jit(solution)/shard_map/ppermute | solution.py:424

commit v11 on v7

--- a/solution.py
+++ b/solution.py
@@ -427,7 +427,7 @@
     count = lax.axis_size(axis)
     if count not in (1, 2, 4):
         return [lax.psum(terms, axis)]
-    return [terms] + [moved(terms, axis, lambda i: i ^ step) for step in reversed(range(1, count))]
+    return [terms] + [moved(terms, axis, lambda i: (i + step) % count) for step in range(1, count)]
 
 
 def on_device(

time: 26.2 us -> 26.4 us (level)
  starting transfers between devices: 10.7 us -> 11.8 us
  waiting for transfers between devices: 10.4 us -> 9.44 us
    ppermute x7, starting transfers between devices: 9.13 us -> 10.2 us  [moved(): lax.ppermute(shard, axis, [(i, target(i)) for i in range(lax.axis_size(ax...]
    ppermute x7, waiting for transfers between devices: 7.16 us -> 6.23 us  [moved(): lax.ppermute(shard, axis, [(i, target(i)) for i in range(lax.axis_size(ax...]
  transfers between devices with their start and end apart: 9 -> 9, of which waited for: 9 -> 7; matrix products, arithmetic and copies ran while one was open for 0% -> 0% of each run, Pallas kernels for 6% -> 6%
where the time goes in v11:
time: 26.4 us; the launch traced here: 26.2 us
  starting transfers between devices  11.8 us (45%)
  waiting for transfers between devices  9.44 us (36%)
  Pallas kernels  3.39 us (13%)
  between operations  0.8 us (3%)
  local copies, waits for them, and re-layouts  0.75 us (3%)
    ppermute x7, starting transfers between devices, moved(): lax.ppermute(shard, axis, [(i, target(i)) for i in range(lax.axis_size(ax...  10.2 us
    ppermute x7, waiting for transfers between devices, moved(): lax.ppermute(shard, axis, [(i, target(i)) for i in range(lax.axis_size(ax...  6.23 us
    pallas_call x8, Pallas kernels, call(): pl.pallas_call(kernel, out_shape=outs, in_specs=[smem] * len(parameters)...  3.39 us
    ppermute x1, waiting for transfers between devices, gathered(): second = lax.ppermute(slabs, ('gx', 'gz'), [(b, a) for a, b in ring_of_gz])  2.32 us
    ppermute x1, starting transfers between devices, gathered(): first = lax.ppermute(slabs, ('gx', 'gz'), ring_of_gz)  1.58 us
    ppermute x1, waiting for transfers between devices, gathered(): first = lax.ppermute(slabs, ('gx', 'gz'), ring_of_gz)  0.9 us
    unnamed x22, local copies, waits for them, and re-layouts  0.75 us
  transfers between devices with their start and end apart: 9, of which 7 were waited for; matrix products, arithmetic and copies ran while one was open for 0% of the time, Pallas kernels for 6%

profile of v11, /device:TPU:0, one launch (start us, length us, event | category | flops | bytes accessed | tf_op | source)
XLA Modules:
  0.0 26.2 jit_solution(463730024758694336)
XLA Ops:
  0.7 0.7 %copy-done.1 = f32[3,2,8,128]{3,2,1,0:T(8,128)S(1)} copy-done((f32[3,2,8,128]{3,2,1,0:T(8,128)S(1)}, f32[3,2,8,128]{3,2,1,0:T(8,128)}, u32[]{:S(2)}) %copy-start.1) | copy-done | bytes 24600
  1.4 0.0 copy-done.2
  1.4 0.1 shard_map.148.refs_0_
  1.5 4.0 %collective-permute-start = (f32[17,8,128]{2,1,0:T(8,128)S(1)}, f32[17,8,128]{2,1,0:T(8,128)S(1)}, u32[]{:S(2)}, u32[]{:S(2)}) collective-permute-start(f32[17,8,128]{2,1,0:T(8,128)S(1)} %shard_map.148.refs_0_), channel_id=1, source_target_pairs={{0,20},{4,16},{8,28},{12,24},{16,4},{20,0},{24,12},{28,8},{1,21},{... | collective-permute-start | bytes 208904 | tf_op jit(solution)/shard_map/ppermute | solution.py:369
  5.5 0.5 %collective-permute-start.1 = (f32[17,8,128]{2,1,0:T(8,128)S(1)}, f32[17,8,128]{2,1,0:T(8,128)S(1)}, u32[]{:S(2)}, u32[]{:S(2)}) collective-permute-start(f32[17,8,128]{2,1,0:T(8,128)S(1)} %shard_map.148.refs_0_), channel_id=1, source_target_pairs={{0,16},{4,20},{8,24},{12,28},{16,0},{20,4},{24,8},{28,12},{1,17},{... | collective-permute-start | bytes 208904 | tf_op jit(solution)/shard_map/ppermute | solution.py:369
  6.0 0.1 collective-permute-start.2
  6.1 1.7 %collective-permute-done.refs_1_ = f32[17,8,128]{2,1,0:T(8,128)S(1)} collective-permute-done((f32[17,8,128]{2,1,0:T(8,128)S(1)}, f32[17,8,128]{2,1,0:T(8,128)S(1)}, u32[]{:S(2)}, u32[]{:S(2)}) %collective-permute-start) | collective-permute-done | bytes 69664 | tf_op jit(solution)/shard_map/ppermute | solution.py:369
  7.8 2.0 %collective-permute-done.1.refs_2_ = f32[17,8,128]{2,1,0:T(8,128)S(1)} collective-permute-done((f32[17,8,128]{2,1,0:T(8,128)S(1)}, f32[17,8,128]{2,1,0:T(8,128)S(1)}, u32[]{:S(2)}, u32[]{:S(2)}) %collective-permute-start.1) | collective-permute-done | bytes 69664 | tf_op jit(solution)/shard_map/ppermute | solution.py:369
  9.8 0.5 %collective-permute-done.2.refs_3_ = f32[17,8,128]{2,1,0:T(8,128)S(1)} collective-permute-done((f32[17,8,128]{2,1,0:T(8,128)S(1)}, f32[17,8,128]{2,1,0:T(8,128)S(1)}, u32[]{:S(2)}, u32[]{:S(2)}) %collective-permute-start.2) | collective-permute-done | bytes 69664 | tf_op jit(solution)/shard_map/ppermute | solution.py:369
  10.3 0.0 copy-start.6
  10.3 0.0 copy-start.9
  10.4 0.1 collective-permute-start.3
  10.4 1.5 %collective-permute-done.3.refs_1_.refs_4_.refs_6_ = f32[4,17,8,128]{3,2,1,0:T(8,128)S(1)} collective-permute-done((f32[4,17,8,128]{3,2,1,0:T(8,128)S(1)}, f32[4,17,8,128]{3,2,1,0:T(8,128)S(1)}, u32[]{:S(2)}, u32[]{:S(2)}) %collective-permute-start.3) | collective-permute-done | bytes 278560 | tf_op jit(solution)/shard_map/ppermute | solution.py:369
  12.0 1.6 %collective-permute-start.4 = (f32[8,1,8,128]{3,2,1,0:T(8,128)S(1)}, f32[8,1,8,128]{3,2,1,0:T(8,128)S(1)}, u32[]{:S(2)}, u32[]{:S(2)}) collective-permute-start(f32[8,1,8,128]{3,2,1,0:T(8,128)S(1)} %shard_map.150), channel_id=1, source_target_pairs={{0,1},{1,2},{2,3},{3,11},{8,0},{9,8},{10,9},{11,10},{16,17},{17,18... | collective-permute-start | bytes 98312 | tf_op jit(solution)/shard_map/ppermute | solution.py:421
  13.6 0.6 %shard_map.146.refs_0_ = f32[15,4,128]{2,1,0:T(4,128)S(1)} custom-call(f32[4,6]{1,0:T(4,128)S(1)} %copy-done.6, f32[4,6]{1,0:T(4,128)S(1)} %copy-done.7, f32[4]{0:T(128)S(1)} %copy-done.8, f32[4]{0:T(128)S(1)} %copy-done.9, f32[4]{0:T(128)S(1)} %copy-done.10), custom_call_target="tpu_custom_call" | custom-call | flops 16777216 | bytes 30720 | tf_op jit(solution)/shard_map/pallas_call | solution.py:357
  14.3 0.9 %collective-permute-done.4.refs_1_.refs_3_ = f32[8,1,8,128]{3,2,1,0:T(8,128)S(1)} collective-permute-done((f32[8,1,8,128]{3,2,1,0:T(8,128)S(1)}, f32[8,1,8,128]{3,2,1,0:T(8,128)S(1)}, u32[]{:S(2)}, u32[]{:S(2)}) %collective-permute-start.4) | collective-permute-done | bytes 32800 | tf_op jit(solution)/shard_map/ppermute | solution.py:421
  15.2 2.3 %collective-permute-done.5.refs_2_.refs_4_ = f32[8,1,8,128]{3,2,1,0:T(8,128)S(1)} collective-permute-done((f32[8,1,8,128]{3,2,1,0:T(8,128)S(1)}, f32[8,1,8,128]{3,2,1,0:T(8,128)S(1)}, u32[]{:S(2)}, u32[]{:S(2)}) %collective-permute-start.5) | collective-permute-done | bytes 32800 | tf_op jit(solution)/shard_map/ppermute | solution.py:422
  17.5 1.0 %shard_map.151 = (f32[5,2,8,128]{3,2,1,0:T(8,128)S(1)}, f32[6,2,8,128]{3,2,1,0:T(8,128)S(1)}, f32[16,128]{1,0:T(8,128)S(1)}) custom-call(f32[15,4,128]{2,1,0:T(4,128)S(1)} %shard_map.146.refs_0_, f32[8,1,8,128]{3,2,1,0:T(8,128)S(1)} %collective-permute-done.4.refs_1_.refs_3_, f32[8,1,8,128]{3,2,1,0:T(8,128)S(1)} %collective-permute-done.5.refs_2_.refs_4_, ...), custom_call_target="tpu_custom_call" | custom-call | flops 8192000 | bytes 751616 | tf_op jit(solution)/shard_map/pallas_call | solution.py:357
  18.4 1.6 %collective-permute-start.6 = (f32[16,128]{1,0:T(8,128)S(1)}, f32[16,128]{1,0:T(8,128)S(1)}, u32[]{:S(2)}, u32[]{:S(2)}) collective-permute-start(f32[16,128]{1,0:T(8,128)S(1)} %get-tuple-element.18.refs_0_), channel_id=1, source_target_pairs={{0,1},{1,2},{2,3},{3,0},{4,5},{5,6},{6,7},{7,4},{8,9},{9,10},{10,1... | collective-permute-start | bytes 24584 | tf_op jit(solution)/shard_map/ppermute | solution.py:369
  20.1 1.1 %collective-permute-start.7 = (f32[16,128]{1,0:T(8,128)S(1)}, f32[16,128]{1,0:T(8,128)S(1)}, u32[]{:S(2)}, u32[]{:S(2)}) collective-permute-start(f32[16,128]{1,0:T(8,128)S(1)} %get-tuple-element.18.refs_0_), channel_id=1, source_target_pairs={{0,2},{1,3},{2,0},{3,1},{4,6},{5,7},{6,4},{7,5},{8,10},{9,11},{10,... | collective-permute-start | bytes 24584 | tf_op jit(solution)/shard_map/ppermute | solution.py:369
  21.2 2.8 %collective-permute-start.8 = (f32[16,128]{1,0:T(8,128)S(1)}, f32[16,128]{1,0:T(8,128)S(1)}, u32[]{:S(2)}, u32[]{:S(2)}) collective-permute-start(f32[16,128]{1,0:T(8,128)S(1)} %get-tuple-element.18.refs_0_), channel_id=1, source_target_pairs={{0,3},{1,0},{2,1},{3,2},{4,7},{5,4},{6,5},{7,6},{8,11},{9,8},{10,9... | collective-permute-start | bytes 24584 | tf_op jit(solution)/shard_map/ppermute | solution.py:369
  24.0 0.9 %shard_map.152 = (f32[6,2,8,128]{3,2,1,0:T(8,128)}, f32[6,6,2,8,128]{4,3,2,1,0:T(8,128)}, f32[2,8,128]{2,1,0:T(8,128)}) custom-call(f32[15,4,128]{2,1,0:T(4,128)S(1)} %shard_map.146.refs_0_, f32[6,2,8,128]{3,2,1,0:T(8,128)S(1)} %get-tuple-element.13.refs_1_, f32[6,6,2,8,128]{4,3,2,1,0:T(8,128)S(1)} %copy-done, ...), custom_call_target="tpu_custom_call" | custom-call | flops 1024000 | bytes 1349632 | tf_op jit(solution)/shard_map/pallas_call | solution.py:357
  24.9 0.5 %collective-permute-done.8.refs_3_ = f32[16,128]{1,0:T(8,128)S(1)} collective-permute-done((f32[16,128]{1,0:T(8,128)S(1)}, f32[16,128]{1,0:T(8,128)S(1)}, u32[]{:S(2)}, u32[]{:S(2)}) %collective-permute-start.8) | collective-permute-done | bytes 8224 | tf_op jit(solution)/shard_map/ppermute | solution.py:369
  25.4 0.8 %shard_map.153 = (f32[2,8,128]{2,1,0:T(8,128)}, f32[2,8,128]{2,1,0:T(8,128)}) custom-call(f32[5,2,8,128]{3,2,1,0:T(8,128)S(1)} %get-tuple-element.17.basis, f32[16,128]{1,0:T(8,128)S(1)} %get-tuple-element.18.refs_0_, f32[16,128]{1,0:T(8,128)S(1)} %collective-permute-done.6.refs_1_, f32[16,128]{1,0:T(8,128)S(1)} %collective-permute-done.7.refs_2_, ...), custom_call_target="tpu_custom_call" | custom-call | bytes 90112 | tf_op jit(solution)/shard_map/pallas_call | solution.py:357
  (24 shorter events, 0.1 us)
Async XLA Ops:
  0.6 0.7 %copy-start.1 = (f32[3,2,8,128]{3,2,1,0:T(8,128)S(1)}, f32[3,2,8,128]{3,2,1,0:T(8,128)}, u32[]{:S(2)}) copy-start(f32[3,2,8,128]{3,2,1,0:T(8,128)} %new.1) | copy-start | bytes 73732
  0.6 0.7 %copy-start.2 = (f32[3,2,8,128]{3,2,1,0:T(8,128)S(1)}, f32[3,2,8,128]{3,2,1,0:T(8,128)}, u32[]{:S(2)}) copy-start(f32[3,2,8,128]{3,2,1,0:T(8,128)} %old.1) | copy-start | bytes 73732
  0.7 0.7 %copy-start.3 = (f32[2,8,128]{2,1,0:T(8,128)S(1)}, f32[2,8,128]{2,1,0:T(8,128)}, u32[]{:S(2)}) copy-start(f32[2,8,128]{2,1,0:T(8,128)} %energy_max.1) | copy-start | bytes 24580
  0.7 0.7 %copy-start.4 = (s32[2,8,128]{2,1,0:T(8,128)S(1)}, s32[2,8,128]{2,1,0:T(8,128)}, u32[]{:S(2)}) copy-start(s32[2,8,128]{2,1,0:T(8,128)} %region.1) | copy-start | bytes 24580
  0.7 0.7 %copy-start.5 = (s32[2,8,128]{2,1,0:T(8,128)S(1)}, s32[2,8,128]{2,1,0:T(8,128)}, u32[]{:S(2)}) copy-start(s32[2,8,128]{2,1,0:T(8,128)} %dirichlet.1) | copy-start | bytes 24580
  1.5 6.3 %collective-permute-start = (f32[17,8,128]{2,1,0:T(8,128)S(1)}, f32[17,8,128]{2,1,0:T(8,128)S(1)}, u32[]{:S(2)}, u32[]{:S(2)}) collective-permute-start(f32[17,8,128]{2,1,0:T(8,128)S(1)} %shard_map.148.refs_0_), channel_id=1, source_target_pairs={{0,20},{4,16},{8,28},{12,24},{16,4},{20,0},{24,12},{28,8},{1,21},{... | collective-permute-start | bytes 208904 | tf_op jit(solution)/shard_map/ppermute | solution.py:369
  5.5 4.3 %collective-permute-start.1 = (f32[17,8,128]{2,1,0:T(8,128)S(1)}, f32[17,8,128]{2,1,0:T(8,128)S(1)}, u32[]{:S(2)}, u32[]{:S(2)}) collective-permute-start(f32[17,8,128]{2,1,0:T(8,128)S(1)} %shard_map.148.refs_0_), channel_id=1, source_target_pairs={{0,16},{4,20},{8,24},{12,28},{16,0},{20,4},{24,8},{28,12},{1,17},{... | collective-permute-start | bytes 208904 | tf_op jit(solution)/shard_map/ppermute | solution.py:369
  6.0 4.3 %collective-permute-start.2 = (f32[17,8,128]{2,1,0:T(8,128)S(1)}, f32[17,8,128]{2,1,0:T(8,128)S(1)}, u32[]{:S(2)}, u32[]{:S(2)}) collective-permute-start(f32[17,8,128]{2,1,0:T(8,128)S(1)} %shard_map.148.refs_0_), channel_id=1, source_target_pairs={{0,4},{4,0},{8,12},{12,8},{16,20},{20,16},{24,28},{28,24},{1,5},{5... | collective-permute-start | bytes 208904 | tf_op jit(solution)/shard_map/ppermute | solution.py:369
  10.3 3.3 %copy-start.6 = (f32[4,6]{1,0:T(4,128)S(1)}, f32[4,6]{1,0:T(4,128)}, u32[]{:S(2)}) copy-start(f32[4,6]{1,0:T(4,128)} %moduli.1) | copy-start | bytes 292
  10.3 3.3 %copy-start.7 = (f32[4,6]{1,0:T(4,128)S(1)}, f32[4,6]{1,0:T(4,128)}, u32[]{:S(2)}) copy-start(f32[4,6]{1,0:T(4,128)} %times.1) | copy-start | bytes 292
  10.3 3.3 %copy-start.8 = (f32[4]{0:T(128)S(1)}, f32[4]{0:T(128)}, u32[]{:S(2)}) copy-start(f32[4]{0:T(128)} %shear.1) | copy-start | bytes 52
  10.3 3.3 %copy-start.9 = (f32[4]{0:T(128)S(1)}, f32[4]{0:T(128)}, u32[]{:S(2)}) copy-start(f32[4]{0:T(128)} %ratio.1) | copy-start | bytes 52
  10.3 3.3 %copy-start.10 = (f32[4]{0:T(128)S(1)}, f32[4]{0:T(128)}, u32[]{:S(2)}) copy-start(f32[4]{0:T(128)} %scale.1) | copy-start | bytes 52
  10.4 1.6 %collective-permute-start.3 = (f32[4,17,8,128]{3,2,1,0:T(8,128)S(1)}, f32[4,17,8,128]{3,2,1,0:T(8,128)S(1)}, u32[]{:S(2)}, u32[]{:S(2)}) collective-permute-start(f32[4,17,8,128]{3,2,1,0:T(8,128)S(1)} %bitcast.1), channel_id=1, source_target_pairs={{0,8},{8,0},{16,24},{24,16},{1,9},{9,1},{17,25},{25,17},{2,10},{10... | collective-permute-start | bytes 835592 | tf_op jit(solution)/shard_map/ppermute | solution.py:369
  12.0 3.2 %collective-permute-start.4 = (f32[8,1,8,128]{3,2,1,0:T(8,128)S(1)}, f32[8,1,8,128]{3,2,1,0:T(8,128)S(1)}, u32[]{:S(2)}, u32[]{:S(2)}) collective-permute-start(f32[8,1,8,128]{3,2,1,0:T(8,128)S(1)} %shard_map.150), channel_id=1, source_target_pairs={{0,1},{1,2},{2,3},{3,11},{8,0},{9,8},{10,9},{11,10},{16,17},{17,18... | collective-permute-start | bytes 98312 | tf_op jit(solution)/shard_map/ppermute | solution.py:421
  13.6 3.9 %collective-permute-start.5 = (f32[8,1,8,128]{3,2,1,0:T(8,128)S(1)}, f32[8,1,8,128]{3,2,1,0:T(8,128)S(1)}, u32[]{:S(2)}, u32[]{:S(2)}) collective-permute-start(f32[8,1,8,128]{3,2,1,0:T(8,128)S(1)} %shard_map.150), channel_id=1, source_target_pairs={{1,0},{2,1},{3,2},{11,3},{0,8},{8,9},{9,10},{10,11},{17,16},{18,17... | collective-permute-start | bytes 98312 | tf_op jit(solution)/shard_map/ppermute | solution.py:422
  14.2 9.8 %copy-start = (f32[6,6,2,8,128]{4,3,2,1,0:T(8,128)S(1)}, f32[6,6,2,8,128]{4,3,2,1,0:T(8,128)}, u32[]{:S(2)}) copy-start(f32[6,6,2,8,128]{4,3,2,1,0:T(8,128)} %refs_2_.1) | copy-start | bytes 884740
  18.4 6.4 %collective-permute-start.6 = (f32[16,128]{1,0:T(8,128)S(1)}, f32[16,128]{1,0:T(8,128)S(1)}, u32[]{:S(2)}, u32[]{:S(2)}) collective-permute-start(f32[16,128]{1,0:T(8,128)S(1)} %get-tuple-element.18.refs_0_), channel_id=1, source_target_pairs={{0,1},{1,2},{2,3},{3,0},{4,5},{5,6},{6,7},{7,4},{8,9},{9,10},{10,1... | collective-permute-start | bytes 24584 | tf_op jit(solution)/shard_map/ppermute | solution.py:369
  20.1 4.8 %collective-permute-start.7 = (f32[16,128]{1,0:T(8,128)S(1)}, f32[16,128]{1,0:T(8,128)S(1)}, u32[]{:S(2)}, u32[]{:S(2)}) collective-permute-start(f32[16,128]{1,0:T(8,128)S(1)} %get-tuple-element.18.refs_0_), channel_id=1, source_target_pairs={{0,2},{1,3},{2,0},{3,1},{4,6},{5,7},{6,4},{7,5},{8,10},{9,11},{10,... | collective-permute-start | bytes 24584 | tf_op jit(solution)/shard_map/ppermute | solution.py:369
  21.2 4.2 %collective-permute-start.8 = (f32[16,128]{1,0:T(8,128)S(1)}, f32[16,128]{1,0:T(8,128)S(1)}, u32[]{:S(2)}, u32[]{:S(2)}) collective-permute-start(f32[16,128]{1,0:T(8,128)S(1)} %get-tuple-element.18.refs_0_), channel_id=1, source_target_pairs={{0,3},{1,0},{2,1},{3,2},{4,7},{5,4},{6,5},{7,6},{8,11},{9,8},{10,9... | collective-permute-start | bytes 24584 | tf_op jit(solution)/shard_map/ppermute | solution.py:369
